TPU v7x, 32 devices: a whole 2x2x4 slice. The times are simulated.
32 devices in a mesh: row: 16 (over z, y, core), col: 2 (over x).
Axes of the slice: x: 2, y: 2, z: 4, core: 2. Of those that a mesh axis runs over, the one named last changes fastest.
Arguments:
- grad: bfloat16 [3072, 3072], P('row', 'col'), may hold values from -0.75 to 0.75
- left_basis: bfloat16 [3072, 3072], P('row', 'col'), may hold values from -0.109375 to 0.109375
- right_basis: bfloat16 [3072, 3072], P('col', 'row'), may hold values from -0.109375 to 0.109375
- first_moment: float32 [3072, 3072], P('col', 'row'), may hold values from -0.625 to 0.625
- second_moment: float32 [3072, 3072], P('col', 'row'), may hold values from 0.002 to 0.05
- left_factor: float32 [3072, 3072], P('col', 'row'), may hold values from -6 to 6
- right_factor: float32 [3072, 3072], P('col', 'row'), may hold values from -6 to 6
Outputs:
- update: float32 [3072, 3072], P('row', 'col')
- new_first: float32 [3072, 3072], P('col', 'row')
- new_second: float32 [3072, 3072], P('col', 'row')
- new_left: float32 [3072, 3072], P('col', 'row')
- new_right: float32 [3072, 3072], P('col', 'row')
All inputs are finite; a program needn't handle non-finite values.
Results may differ from a plain program's by a relative error of at most 0.005.
Values may be sent and summed in bfloat16 or wider, within the bound.
No kernel may reach another device: no remote copies, remote signals or barrier semaphores. Data moves between devices by JAX's collectives and lax.ppermute only.
A program may use at most 128 MiB of HBM per device.

v0:
```python
import jax
import jax.numpy as jnp
from jax import lax
from jax.sharding import PartitionSpec as P


def contract(left, right, left_dim, right_dim):
    return lax.dot_general(
        left, right, (((left_dim,), (right_dim,)), ((), ())), preferred_element_type=jnp.float32
    )


def split_contract(narrow, wide, narrow_dim, wide_dim):
    upper = wide.astype(jnp.bfloat16)
    lower = (wide - upper.astype(jnp.float32)).astype(jnp.bfloat16)
    return contract(narrow, upper, narrow_dim, wide_dim) + contract(
        narrow, lower, narrow_dim, wide_dim
    )


def on_device(
    grad, left_basis, right_basis, first_moment, second_moment, left_factor, right_factor
):
    basis_rows, grad_rows = (
        lax.all_gather(left_basis, "col", axis=1, tiled=True),
        lax.all_gather(grad, "col", axis=1, tiled=True),
    )
    basis_cols, grad_block = (
        lax.all_to_all(basis_rows, "row", split_axis=1, concat_axis=0, tiled=True),
        lax.all_to_all(grad_rows, "row", split_axis=1, concat_axis=0, tiled=True),
    )
    piece = lax.all_gather(grad, "row", axis=0, tiled=True)
    proj = contract(basis_cols, piece, 0, 0)
    right_sum = contract(piece, grad_block, 0, 0)
    term = contract(piece, grad, 1, 1)
    left_term = term
    proj, right_sum, left_term = (proj, right_sum, left_term)
    left_sum = lax.psum_scatter(
        left_term.astype(jnp.bfloat16), "col", scatter_dimension=0, tiled=True
    ).astype(jnp.float32)
    new_left = 0.95 * left_factor + 0.05 * left_sum
    new_right = 0.95 * right_factor + 0.05 * right_sum
    left_proj = proj.astype(jnp.bfloat16)
    rotate_term = contract(lax.all_gather(right_basis, "row", axis=1, tiled=True), left_proj, 0, 1)
    rotated = lax.psum_scatter(rotate_term, "col", scatter_dimension=0, tiled=True)
    new_first = 0.9 * first_moment + 0.1 * rotated
    new_second = 0.95 * second_moment + 0.05 * rotated * rotated
    bias_one = 1.0 - 0.9**10
    bias_two = 1.0 - 0.95**10
    direction = (new_first / bias_one / (jnp.sqrt(new_second / bias_two) + 1e-08)).astype(
        jnp.bfloat16
    )
    direction_full = lax.all_gather(direction, "col", axis=0, tiled=True)
    half_back = contract(
        direction_full, lax.all_gather(right_basis, "row", axis=1, tiled=True), 0, 1
    )
    update = split_contract(basis_rows, lax.all_gather(half_back, "row", axis=0, tiled=True), 1, 0)
    return (update, new_first, new_second, new_left, new_right)


def solution(mesh):
    in_specs = (
        P("row", "col"),
        P("row", "col"),
        P("col", "row"),
        P("col", "row"),
        P("col", "row"),
        P("col", "row"),
        P("col", "row"),
    )
    out_specs = (
        P("row", "col"),
        P("col", "row"),
        P("col", "row"),
        P("col", "row"),
        P("col", "row"),
    )
    return jax.shard_map(
        on_device, mesh=mesh, in_specs=in_specs, out_specs=out_specs, check_vma=False
    )
```

profile of v0, /device:TPU:0, one launch (start us, length us, event | category | flops | bytes accessed | tf_op | source)
XLA Modules:
  0.0 478.2 jit_solution(12166334297509373757)
XLA Ops:
  9.4 25.6 %all-gather.7.cloned.1.call-done = bf16[192,3072]{1,0:T(8,128)(2,1)} async-done(((bf16[192,1536]{1,0:T(8,128)(2,1)}), bf16[192,3072]{1,0:T(8,128)(2,1)}) %all-gather.7.cloned.1.call-update) | async-done | bytes 1179664 | tf_op jit(solution)/shard_map/all_gather | solution.py:25
  35.1 1.6 copy.14
  36.7 60.5 %all_to_all.38 = bf16[192,16,192]{0,2,1:T(8,128)(2,1)S(1)} all-to-all(bf16[192,16,192]{0,2,1:T(8,128)(2,1)S(1)} %bitcast.26), channel_id=1, replica_groups=mesh['row'=16,'col'=2] {'row'}, dimensions={1} | all-to-all | bytes 2359296 | tf_op jit(solution)/shard_map/all_to_all | solution.py:29
  97.1 0.9 copy.15
  98.0 1.7 all_to_all.31
  99.7 42.8 %all-gather.11.cloned.1.call-done = bf16[1536,3072]{0,1:T(8,128)(2,1)} async-done(((bf16[1536,192]{0,1:T(8,128)(2,1)}), bf16[1536,3072]{0,1:T(8,128)(2,1)}) %all-gather.11.cloned.1.call-update) | async-done | bytes 9437200 | tf_op jit(solution)/shard_map/all_gather | solution.py:44
  142.6 81.9 %all-gather.9.cloned.1.call-done = bf16[3072,1536]{1,0:T(8,128)(2,1)} async-done(((bf16[192,1536]{1,0:T(8,128)(2,1)}), bf16[3072,1536]{1,0:T(8,128)(2,1)}) %all-gather.9.cloned.1.call-update) | async-done | bytes 9437200 | tf_op jit(solution)/shard_map/all_gather | solution.py:32
  224.5 13.0 %convolution_bitcast_fusion = f32[3072,192]{0,1:T(8,128)} fusion(bf16[1536,3072]{0,1:T(8,128)(2,1)} %all-gather.11.cloned.1.call-done, bf16[3072,192]{0,1:T(8,128)(2,1)S(1)} %all_to_all.31, bf16[3072,1536]{1,0:T(8,128)(2,1)} %all-gather.9.cloned.1.call-done), kind=kOutput, calls=%fused_computation.5 | convolution fusion | flops 3624173568 | bytes 22413312 | tf_op jit(solution)/shard_map/dot_general | solution.py:8
  237.6 32.9 %reduce-scatter.3.cloned.1.call-done = f32[1536,192]{0,1:T(8,128)} async-done(((f32[3072,192]{0,1:T(8,128)}), f32[1536,192]{0,1:T(8,128)}) %reduce-scatter.3.cloned.1.call-update) | async-done | bytes 1179664 | tf_op jit(solution)/shard_map/reduce_scatter | solution.py:45
  270.5 3.3 divide_convert_fusion
  274.9 7.9 %convolution_convert_fusion = bf16[3072,192]{0,1:T(8,128)(2,1)} fusion(bf16[3072,1536]{1,0:T(8,128)(2,1)} %all-gather.9.cloned.1.call-done, bf16[192,1536]{1,0:T(8,128)(2,1)S(1)} %copy-done.2), kind=kOutput, calls=%fused_computation.6 | convolution fusion | flops 1812529152 | bytes 11206656 | tf_op jit(solution)/shard_map/dot_general | solution.py:8
  282.9 13.9 %all-gather.13.cloned.1.call-done = bf16[3072,192]{0,1:T(8,128)(2,1)} async-done(((bf16[1536,192]{0,1:T(8,128)(2,1)}), bf16[3072,192]{0,1:T(8,128)(2,1)}) %all-gather.13.cloned.1.call-update) | async-done | bytes 1179664 | tf_op jit(solution)/shard_map/all_gather | solution.py:53
  296.8 7.1 %fusion.13 = f32[192,1536]{1,0:T(8,128)} fusion(bf16[3072,192]{0,1:T(8,128)(2,1)} %all-gather.13.cloned.1.call-done, bf16[1536,3072]{0,1:T(8,128)(2,1)} %all-gather.11.cloned.1.call-done), kind=kOutput, calls=%fused_computation.17 | convolution fusion | flops 1811939328 | bytes 11796480 | tf_op jit(solution)/shard_map/dot_general | solution.py:8
  303.9 17.2 %all-gather.17.cloned.1.call-done = bf16[192,3072]{1,0:T(8,128)(2,1)} async-done(((bf16[192,1536]{1,0:T(8,128)(2,1)}), bf16[192,3072]{1,0:T(8,128)(2,1)}) %all-gather.17.cloned.1.call-update) | async-done | bytes 1179664 | tf_op jit(solution)/shard_map/all_gather | solution.py:26
  321.1 1.6 copy.16
  322.8 46.6 %all_to_all.39 = bf16[192,16,192]{0,2,1:T(8,128)(2,1)S(1)} all-to-all(bf16[192,16,192]{0,2,1:T(8,128)(2,1)S(1)} %bitcast.25), channel_id=1, replica_groups=mesh['row'=16,'col'=2] {'row'}, dimensions={1} | all-to-all | bytes 2359296 | tf_op jit(solution)/shard_map/all_to_all | solution.py:30
  369.3 0.9 copy.17
  370.2 1.7 all_to_all.35
  371.9 7.3 %fusion.10 = f32[1536,192]{0,1:T(8,128)} fusion(bf16[3072,192]{0,1:T(8,128)(2,1)S(1)} %all_to_all.35, bf16[3072,1536]{1,0:T(8,128)(2,1)} %all-gather.9.cloned.1.call-done, f32[1536,192]{0,1:T(8,128)} %param.13), kind=kOutput, calls=%fused_computation.10 | convolution fusion | flops 1812824064 | bytes 12976128 | tf_op jit(solution)/shard_map/dot_general | solution.py:8
  379.2 2.4 multiply_add_fusion
  381.6 69.5 %all-gather.15.cloned.1.call-done = f32[3072,1536]{1,0:T(8,128)} async-done(((f32[192,1536]{1,0:T(8,128)}), f32[3072,1536]{1,0:T(8,128)}) %all-gather.15.cloned.1.call-update) | async-done | bytes 18874384 | tf_op jit(solution)/shard_map/all_gather | solution.py:57
  451.0 14.1 %fusion = f32[1536,192]{0,1:T(8,128)S(1)} fusion(bf16[192,3072]{1,0:T(8,128)(2,1)S(1)} %copy-done.1, f32[3072,1536]{1,0:T(8,128)} %all-gather.15.cloned.1.call-done), kind=kOutput, calls=%fused_computation.1 | convolution fusion | flops 1830813696 | bytes 21233664 | tf_op jit(solution)/shard_map/dot_general | solution.py:8
  465.1 3.0 copy-done
  468.1 3.2 fusion.7
  (28 shorter events, 3.4 us)
Async XLA Ops:
  7.2 27.9 %all-gather.7.cloned.1.call-start = ((), (), s32[]{:S(2)}) async-start(), calls=%async_computation.4 | async-start | bytes 1769472 | tf_op jit(solution)/shard_map/all_gather | solution.py:25
  7.9 134.7 %all-gather.11.cloned.1.call-start = ((), (), s32[]{:S(2)}) async-start(), calls=%async_computation.6 | async-start | bytes 10027008 | tf_op jit(solution)/shard_map/all_gather | solution.py:44
  8.6 215.8 %all-gather.9.cloned.1.call-start = ((), (), s32[]{:S(2)}) async-start(), calls=%async_computation.5 | async-start | bytes 10027008 | tf_op jit(solution)/shard_map/all_gather | solution.py:32
  9.4 261.1 %reduce-scatter.3.cloned.1.call-start = ((), (), s32[]{:S(2)}) async-start(), calls=%async_computation.7 | async-start | bytes 3538944 | tf_op jit(solution)/shard_map/reduce_scatter | solution.py:45
  237.5 33.0 %copy-start.3 = (f32[1536,192]{0,1:T(8,128)S(1)}, f32[1536,192]{0,1:T(8,128)}, u32[]{:S(2)}) copy-start(f32[1536,192]{0,1:T(8,128)} %param.10) | copy-start | bytes 3538948
  237.5 33.0 %copy-start.4 = (f32[1536,192]{0,1:T(8,128)S(1)}, f32[1536,192]{0,1:T(8,128)}, u32[]{:S(2)}) copy-start(f32[1536,192]{0,1:T(8,128)} %param.11) | copy-start | bytes 3538948
  237.5 59.3 %all-gather.13.cloned.1.call-start = ((), (), s32[]{:S(2)}) async-start(), calls=%async_computation.8 | async-start | bytes 1769472 | tf_op jit(solution)/shard_map/all_gather | solution.py:53
  273.9 1.1 copy-start.2
  273.9 47.2 %all-gather.17.cloned.1.call-start = ((), (), s32[]{:S(2)}) async-start(), calls=%async_computation.11 | async-start | bytes 1769472 | tf_op jit(solution)/shard_map/all_gather | solution.py:26
  274.5 104.8 %reduce-scatter.5.cloned.1.call-start = ((), (), s32[]{:S(2)}) async-start(), calls=%async_computation.10 | async-start | bytes 1769472 | tf_op jit(solution)/shard_map/reduce_scatter | solution.py:38
  282.9 168.2 %all-gather.15.cloned.1.call-start = ((), (), s32[]{:S(2)}) async-start(), calls=%async_computation.9 | async-start | bytes 20054016 | tf_op jit(solution)/shard_map/all_gather | solution.py:57
  371.9 7.3 %copy-start.5 = (f32[1536,192]{0,1:T(8,128)S(1)}, f32[1536,192]{0,1:T(8,128)}, u32[]{:S(2)}) copy-start(f32[1536,192]{0,1:T(8,128)} %param.12) | copy-start | bytes 3538948
  379.2 71.8 %copy-start.1 = (bf16[192,3072]{1,0:T(8,128)(2,1)S(1)}, bf16[192,3072]{1,0:T(8,128)(2,1)}, u32[]{:S(2)}) copy-start(bf16[192,3072]{1,0:T(8,128)(2,1)} %all-gather.7.cloned.1.call-done) | copy-start | bytes 3538948
  451.0 17.1 %copy-start = (f32[3072,1536]{1,0:T(8,128)S(1)}, f32[3072,1536]{1,0:T(8,128)}, u32[]{:S(2)}) copy-start(f32[3072,1536]{1,0:T(8,128)} %all-gather.15.cloned.1.call-done) | copy-start | bytes 56623108
Sparse Core Ops, SparseCore 0:
  9.5 25.4 all-gather.6
  37.3 105.1 all-gather.10
  144.8 79.5 all-gather.8
  237.6 32.8 reduce-scatter.2
  274.0 22.7 all-gather.12
  298.3 22.7 all-gather.16
  324.0 21.7 reduce-scatter.4
  348.0 103.0 all-gather.14
where the time goes:
time: 482 us; the launch traced here: 478 us
  waiting for transfers between devices  286 us (59%)
  blocking collectives  107 us (22%)
  matrix products  52.6 us (11%)
  between operations  14.2 us (3%)
  local copies, waits for them, and re-layouts  11.9 us (2%)
  other arithmetic  5.7 us (1%)
    all_gather x1, waiting for transfers between devices, on_device(): piece = lax.all_gather(grad, 'row', axis=0, tiled=True)  81.9 us
    all_gather x1, waiting for transfers between devices, on_device(): lax.all_gather(half_back, 'row', axis=0, tiled=True)  69.5 us
    all_to_all x1, blocking collectives, on_device(): lax.all_to_all(basis_rows, 'row', split_axis=1, concat_axis=0, tiled=True)  60.5 us
    dot_general x6, matrix products, contract(): lax.dot_general(left, right, (((left_dim,), (right_dim,)), ((), ())), pre...  52.6 us
    all_to_all x1, blocking collectives, on_device(): lax.all_to_all(grad_rows, 'row', split_axis=1, concat_axis=0, tiled=True)  46.6 us
    all_gather x1, waiting for transfers between devices, on_device(): lax.all_gather(right_basis, 'row', axis=1, tiled=True)  42.8 us
    reduce_scatter x1, waiting for transfers between devices, on_device(): lax.psum_scatter(rotate_term, 'col', scatter_dimension=0, tiled=True)  32.9 us
    all_gather x1, waiting for transfers between devices, on_device(): lax.all_gather(left_basis, 'col', axis=1, tiled=True)  25.6 us
  transfers between devices with their start and end apart: 8, of which 7 were waited for; matrix products, arithmetic and copies ran while one was open for 6% of the time, Pallas kernels for 0%

commit v1 on v0

v1 whole, which is shorter than its diff:
```python
import jax
import jax.numpy as jnp
from jax import lax
from jax.sharding import PartitionSpec as P

BF16 = jnp.bfloat16
F32 = jnp.float32


def dot(left, right, left_dim, right_dim):
    return lax.dot_general(
        left, right, (((left_dim,), (right_dim,)), ((), ())), preferred_element_type=F32
    )


def after(value, *earlier):
    return lax.optimization_barrier((value, *earlier))[0]


def solution(mesh):
    rows, X = mesh.shape["row"], mesh.shape["col"]
    A = rows // 4

    def sender(to):
        pairs = []
        for row in range(rows):
            for x in range(X):
                z, y, c, w = to(row // 4, row // 2 % 2, row % 2, x)
                pairs.append((row * X + x, ((z * 2 + y) * 2 + c) * X + w))
        return lambda value: lax.ppermute(value, ("row", "col"), pairs)

    flip_y = sender(lambda z, y, c, x: (z, 1 - y, c, x))
    flip_c = sender(lambda z, y, c, x: (z, y, 1 - c, x))
    up = sender(lambda z, y, c, x: ((z + 1) % A, y, c, x))
    along_x = [sender(lambda z, y, c, x, s=s: (z, y, c, (x + s) % X)) for s in range(X)]

    def plane_gather(mine):
        other_y = flip_y(mine)
        return [mine, flip_c(mine), other_y, flip_c(other_y)]

    def plane_scatter(blocks):
        got = flip_c(jnp.concatenate([blocks[1], blocks[3]]).astype(BF16)).astype(F32)
        height = blocks[0].shape[0]
        mine, other = blocks[0] + got[:height], blocks[2] + got[height:]
        return mine + flip_y(other.astype(BF16)).astype(F32)

    def on_device(grad, left_basis, right_basis, first, second, left_factor, right_factor):
        b, width = grad.shape
        row, x = lax.axis_index("row"), lax.axis_index("col")
        z, y, c = row // 4, row // 2 % 2, row % 2
        per = A // X
        wide = 4 * b

        def at(blocks, index):
            return lax.dynamic_index_in_dim(blocks, index, 0, keepdims=False)

        left_plane = jnp.concatenate(plane_gather(left_basis))
        grad_plane = jnp.concatenate(plane_gather(grad))
        want = (jnp.arange(per * b) // b) * wide + row % 4 * b + jnp.arange(per * b) % b
        pick = (jnp.arange(width)[:, None] == want[None, :]).astype(BF16)
        mine = dot(pick, left_plane, 0, 1).astype(BF16)
        parts = jnp.stack([mine] + [along_x[s](mine) for s in range(1, X)])
        left_cols = jnp.concatenate([at(parts, (x - w) % X) for w in range(X)]).reshape(A, b, wide)
        left_at = [at(left_cols, (z - r) % A) for r in range(A)]

        right = jnp.zeros((A, 2, 2, b, width), BF16)
        block = right_basis.T
        for r in range(A):
            for k, piece in enumerate(plane_gather(block)):
                place = ((z - r) % A, y ^ (k // 2), c ^ (k % 2), 0, 0)
                right = lax.dynamic_update_slice(right, piece[None, None, None], place)
            if r < A - 1:
                block = up(block)
        right = right.reshape(rows * b, width)

        total = dot(left_at[1], grad_plane, 1, 0)
        for r in range(2, A + 1):
            total = up(total.astype(BF16)).astype(F32) + dot(left_at[r % A], grad_plane, 1, 0)
        left_proj = total.astype(BF16)

        rotate = dot(left_proj, right, 1, 1)
        rotated = lax.dynamic_slice_in_dim(rotate, x * width, width, 1)
        for s in range(1, X):
            piece = lax.dynamic_slice_in_dim(rotate, (x + s) % X * width, width, 1)
            rotated += along_x[s](piece.astype(BF16)).astype(F32)
        new_first = 0.9 * first.T + 0.1 * rotated
        new_second = 0.95 * second.T + 0.05 * rotated * rotated
        bias_one = 1.0 - 0.9**10
        bias_two = 1.0 - 0.95**10
        direction = (new_first / bias_one / (jnp.sqrt(new_second / bias_two) + 1e-08)).astype(BF16)
        parts = jnp.stack([direction] + [along_x[s](direction) for s in range(1, X)])
        direction = jnp.concatenate([at(parts, (x - w) % X) for w in range(X)], axis=1)
        half = dot(direction, right, 1, 0).astype(BF16)

        block = after(grad, left_proj)
        grads = [block]
        for r in range(1, A):
            block = up(block)
            grads.append(block)

        update = dot(left_at[0], half, 0, 0)
        for r in range(1, A):
            half = up(half)
            update += dot(left_at[r], half, 0, 0)
        update = plane_scatter(jnp.split(update, 4))

        have = jnp.concatenate(grads)
        span = width // per
        mine = lax.dynamic_slice_in_dim(have, z % per * span, span, 1)
        cols = mine
        for s in range(1, X):
            pairs = []
            for q in range(rows):
                source = q // 4 // per
                pairs.append((q * X + source, q * X + (source + s) % X))
            got = lax.ppermute(mine, ("row", "col"), pairs)
            cols = jnp.where((z // per + s) % X == x, got, cols)
        term = dot(cols, have, 0, 0).reshape(4, span // 4, width)
        right_sum = plane_scatter([at(term, (row % 4) ^ k) for k in range(4)])
        new_right = 0.95 * right_factor.T + 0.05 * right_sum

        stacked = jnp.stack(grads)
        ordered = jnp.concatenate([at(stacked, (z - w) % A) for w in range(A)])
        term = dot(grad_plane, ordered, 1, 1)
        left_sum = lax.dynamic_slice_in_dim(term, x * per * b, per * b, 1)
        for s in range(1, X):
            piece = lax.dynamic_slice_in_dim(term, (x + s) % X * per * b, per * b, 1)
            left_sum += along_x[s](piece.astype(BF16)).astype(F32)
        own, core, over, cross = jnp.split(left_sum.astype(BF16), 4)
        got = flip_c(jnp.concatenate([core, cross]))
        over_pair = flip_y(jnp.concatenate([over, got[b:]], axis=1))
        joined = jnp.concatenate([own, got[:b], over_pair], axis=1)
        k, p, i = jnp.arange(4)[:, None, None], jnp.arange(per)[:, None], jnp.arange(b)
        goes = (p * wide + (k ^ (row % 4)) * b + i).reshape(-1)
        order = (goes[:, None] == jnp.arange(width)[None, :]).astype(BF16)
        new_left = 0.95 * left_factor.T + 0.05 * dot(joined, order, 1, 0)
        return update, new_first.T, new_second.T, new_left.T, new_right.T

    slab, turned = P("row", "col"), P("col", "row")
    return jax.shard_map(
        on_device,
        mesh=mesh,
        in_specs=(slab, slab) + (turned,) * 5,
        out_specs=(slab,) + (turned,) * 4,
        check_vma=False,
    )
```

time: 482 us -> 269 us (0.56)
  blocking collectives: 107 us -> 0 us
  waiting for transfers between devices: 286 us -> 192 us
  matrix products: 52.6 us -> 22.6 us
  starting transfers between devices: 0.32 us -> 27 us
  between operations: 14.2 us -> 1.31 us
  other arithmetic: 5.7 us -> 15.3 us
    all_gather x6 -> x0, waiting for transfers between devices: 251 us -> none  [the longest x1 81.9 us: on_device(): piece = lax.all_gather(grad, 'row', axis=0, tiled=True)]
    ppermute x0 -> x41, waiting for transfers between devices: none -> 192 us  [the longest x40 188 us: sender(): return lambda value: lax.ppermute(value, ('row', 'col'), pairs)]
    all_to_all x2 -> x0, blocking collectives: 107 us -> none  [the longest x1 60.5 us: on_device(): lax.all_to_all(basis_rows, 'row', split_axis=1, concat_axis=0, tiled=True)]
    reduce_scatter x2 -> x0, waiting for transfers between devices: 32.9 us -> none  [the longest x1 32.9 us: on_device(): lax.psum_scatter(rotate_term, 'col', scatter_dimension=0, tiled=True)]
    dot_general x6 -> x14, matrix products: 52.6 us -> 22.6 us  [dot(): lax.dot_general(left, right, (((left_dim,), (right_dim,)), ((), ())), pre...]
    ppermute x0 -> x41, starting transfers between devices: none -> 27 us  [the longest x40 23.9 us: sender(): return lambda value: lax.ppermute(value, ('row', 'col'), pairs)]
    transpose x0 -> x2, other arithmetic: none -> 5.96 us  [on_device(): return (update, new_first.T, new_second.T, new_left.T, new_right.T)]
    all_to_all x4 -> x0, local copies, waits for them, and re-layouts: 5.17 us -> none  [the longest x2 2.59 us: on_device(): lax.all_to_all(grad_rows, 'row', split_axis=1, concat_axis=0, tiled=True)]
  transfers between devices with their start and end apart: 8 -> 41, of which waited for: 7 -> 20; matrix products, arithmetic and copies ran while one was open for 6% -> 15% of each run, Pallas kernels for 0% -> 0%
where the time goes in v1:
time: 269 us
  waiting for transfers between devices  192 us (71%)
  starting transfers between devices  27 us (10%)
  matrix products  22.6 us (8%)
  other arithmetic  15.3 us (6%)
  local copies, waits for them, and re-layouts  10.5 us (4%)
    ppermute x40, waiting for transfers between devices, sender(): return lambda value: lax.ppermute(value, ('row', 'col'), pairs)  188 us
    ppermute x40, starting transfers between devices, sender(): return lambda value: lax.ppermute(value, ('row', 'col'), pairs)  23.9 us
    dot_general x14, matrix products, dot(): lax.dot_general(left, right, (((left_dim,), (right_dim,)), ((), ())), pre...  22.6 us
    transpose x2, other arithmetic, on_device(): return (update, new_first.T, new_second.T, new_left.T, new_right.T)  5.96 us
  transfers between devices with their start and end apart: 41, of which 20 were waited for; matrix products, arithmetic and copies ran while one was open for 15% of the time, Pallas kernels for 0%

profile of v1, /device:TPU:0, one launch (start us, length us, event | category | flops | bytes accessed | tf_op | source)
XLA Modules:
  0.0 268.7 jit_solution(16283047831737172269)
XLA Ops:
  1.1 2.6 collective-permute-start.11
  10.9 7.2 %collective-permute-done.11 = bf16[192,1536]{1,0:T(8,128)(2,1)S(1)} collective-permute-done((bf16[192,1536]{1,0:T(8,128)(2,1)}, bf16[192,1536]{1,0:T(8,128)(2,1)S(1)}, u32[]{:S(2)}, u32[]{:S(2)}) %collective-permute-start.11) | collective-permute-done | bytes 589856 | tf_op jit(solution)/shard_map/ppermute | solution.py:30
  18.1 12.7 %collective-permute-done.1 = bf16[192,1536]{1,0:T(8,128)(2,1)} collective-permute-done((bf16[192,1536]{1,0:T(8,128)(2,1)}, bf16[192,1536]{1,0:T(8,128)(2,1)}, u32[]{:S(2)}, u32[]{:S(2)}) %collective-permute-start.1) | collective-permute-done | bytes 589856 | tf_op jit(solution)/shard_map/ppermute | solution.py:30
  32.7 10.4 %collective-permute-done.5 = bf16[192,1536]{1,0:T(8,128)(2,1)S(1)} collective-permute-done((bf16[192,1536]{1,0:T(8,128)(2,1)S(1)}, bf16[192,1536]{1,0:T(8,128)(2,1)S(1)}, u32[]{:S(2)}, u32[]{:S(2)}) %collective-permute-start.5) | collective-permute-done | bytes 589856 | tf_op jit(solution)/shard_map/ppermute | solution.py:30
  50.4 9.7 %collective-permute-done.17 = bf16[192,1536]{1,0:T(8,128)(2,1)S(1)} collective-permute-done((bf16[192,1536]{1,0:T(8,128)(2,1)S(1)}, bf16[192,1536]{1,0:T(8,128)(2,1)S(1)}, u32[]{:S(2)}, u32[]{:S(2)}) %collective-permute-start.17) | collective-permute-done | bytes 589856 | tf_op jit(solution)/shard_map/ppermute | solution.py:30
  67.5 12.7 %collective-permute-done.21 = bf16[192,1536]{1,0:T(8,128)(2,1)S(1)} collective-permute-done((bf16[192,1536]{1,0:T(8,128)(2,1)S(1)}, bf16[192,1536]{1,0:T(8,128)(2,1)S(1)}, u32[]{:S(2)}, u32[]{:S(2)}) %collective-permute-start.21) | collective-permute-done | bytes 589856 | tf_op jit(solution)/shard_map/ppermute | solution.py:30
  81.2 11.0 %collective-permute-done.7 = bf16[192,1536]{1,0:T(8,128)(2,1)S(1)} collective-permute-done((bf16[192,1536]{1,0:T(8,128)(2,1)S(1)}, bf16[192,1536]{1,0:T(8,128)(2,1)S(1)}, u32[]{:S(2)}, u32[]{:S(2)}) %collective-permute-start.7) | collective-permute-done | bytes 589856 | tf_op jit(solution)/shard_map/ppermute | solution.py:30
  92.9 3.0 %collective-permute-done.23 = bf16[192,1536]{1,0:T(8,128)(2,1)S(1)} collective-permute-done((bf16[192,1536]{1,0:T(8,128)(2,1)S(1)}, bf16[192,1536]{1,0:T(8,128)(2,1)S(1)}, u32[]{:S(2)}, u32[]{:S(2)}) %collective-permute-start.23) | collective-permute-done | bytes 589856 | tf_op jit(solution)/shard_map/ppermute | solution.py:30
  96.1 13.3 %collective-permute-done.8 = bf16[192,1536]{1,0:T(8,128)(2,1)S(1)} collective-permute-done((bf16[192,1536]{1,0:T(8,128)(2,1)S(1)}, bf16[192,1536]{1,0:T(8,128)(2,1)S(1)}, u32[]{:S(2)}, u32[]{:S(2)}) %collective-permute-start.8) | collective-permute-done | bytes 589856 | tf_op jit(solution)/shard_map/ppermute | solution.py:30
  110.2 15.4 %collective-permute-done.9 = bf16[192,1536]{1,0:T(8,128)(2,1)S(1)} collective-permute-done((bf16[192,1536]{1,0:T(8,128)(2,1)S(1)}, bf16[192,1536]{1,0:T(8,128)(2,1)S(1)}, u32[]{:S(2)}, u32[]{:S(2)}) %collective-permute-start.9) | collective-permute-done | bytes 589856 | tf_op jit(solution)/shard_map/ppermute | solution.py:30
  126.3 3.2 %fusion.105 = f32[192,3072]{1,0:T(8,128)S(1)} fusion(bf16[192,1536]{1,0:T(8,128)(2,1)S(1)} %fusion.6, bf16[3072,1536]{1,0:T(8,128)(2,1)S(1)} %bitcast.124), kind=kOutput, calls=%fused_computation.174 | convolution fusion | flops 1811939328 | bytes 12386304 | tf_op jit(solution)/shard_map/dot_general | solution.py:11
  132.6 11.7 %collective-permute-done.25 = bf16[192,1536]{1,0:T(8,128)(2,1)} collective-permute-done((bf16[192,1536]{1,0:T(8,128)(2,1)}, bf16[192,1536]{1,0:T(8,128)(2,1)}, u32[]{:S(2)}, u32[]{:S(2)}) %collective-permute-start.25) | collective-permute-done | bytes 589856 | tf_op jit(solution)/shard_map/ppermute | solution.py:30
  144.3 4.5 %fusion.100 = (f32[1536,192]{0,1:T(8,128)}, bf16[192,1536]{1,0:T(8,128)(2,1)S(1)}, f32[1536,192]{0,1:T(8,128)}) fusion(bf16[192,1536]{1,0:T(8,128)(2,1)} %collective-permute-done.25, f32[192,3072]{1,0:T(8,128)} %copy-done.2, s32[]{:T(128)S(6)} %select_n.279, f32[1536,192]{0,1:T(8,128)} %param.11, f32[1536,192]{0,1:T(8,128)} %param.10), kind=kLoop, calls=%fused_computation.169 | loop fusion | flops 4128768 | bytes 7077892 | tf_op jit(solution)/shard_map/transpose | solution.py:137
  150.6 10.1 %collective-permute-done.26 = bf16[192,1536]{1,0:T(8,128)(2,1)S(1)} collective-permute-done((bf16[192,1536]{1,0:T(8,128)(2,1)S(1)}, bf16[192,1536]{1,0:T(8,128)(2,1)S(1)}, u32[]{:S(2)}, u32[]{:S(2)}) %collective-permute-start.26) | collective-permute-done | bytes 589856 | tf_op jit(solution)/shard_map/ppermute | solution.py:30
  165.4 23.9 %collective-permute-done.34 = bf16[192,1536]{1,0:T(8,128)(2,1)S(1)} collective-permute-done((bf16[192,1536]{1,0:T(8,128)(2,1)S(1)}, bf16[192,1536]{1,0:T(8,128)(2,1)S(1)}, u32[]{:S(2)}, u32[]{:S(2)}) %collective-permute-start.34) | collective-permute-done | bytes 589856 | tf_op jit(solution)/shard_map/ppermute | solution.py:30
  192.9 3.2 %collective-permute-start.38 = (bf16[768,768]{1,0:T(8,128)(2,1)S(1)}, bf16[768,768]{1,0:T(8,128)(2,1)S(1)}, u32[]{:S(2)}, u32[]{:S(2)}) collective-permute-start(bf16[768,768]{1,0:T(8,128)(2,1)S(1)} %constant_dynamic-slice_fusion), channel_id=1, source_target_pairs={{0,1},{2,3},{4,5},{6,7},{8,9},{10,11},{12,13},{14,15},{17,16},{19,... | collective-permute-start | bytes 3538952 | tf_op jit(solution)/shard_map/ppermute | solution.py:116
  196.9 9.7 %collective-permute-done.28 = bf16[192,1536]{1,0:T(8,128)(2,1)S(1)} collective-permute-done((bf16[192,1536]{1,0:T(8,128)(2,1)S(1)}, bf16[192,1536]{1,0:T(8,128)(2,1)S(1)}, u32[]{:S(2)}, u32[]{:S(2)}) %collective-permute-start.28) | collective-permute-done | bytes 589856 | tf_op jit(solution)/shard_map/ppermute | solution.py:30
  209.0 9.2 %collective-permute-done.29 = bf16[192,1536]{1,0:T(8,128)(2,1)S(1)} collective-permute-done((bf16[192,1536]{1,0:T(8,128)(2,1)S(1)}, bf16[192,1536]{1,0:T(8,128)(2,1)S(1)}, u32[]{:S(2)}, u32[]{:S(2)}) %collective-permute-start.29) | collective-permute-done | bytes 589856 | tf_op jit(solution)/shard_map/ppermute | solution.py:30
  218.2 3.1 %fusion.104 = (bf16[768,1536]{1,0:T(8,128)(2,1)S(1)}, f32[768,1536]{1,0:T(8,128)}) fusion(bf16[192,1536]{1,0:T(8,128)(2,1)S(1)} %collective-permute-done.29, bf16[4,192,768]{2,1,0:T(8,128)(2,1)S(1)} %bitcast.133, s32[]{:T(128)S(6)} %select_n.271, f32[768,1536]{1,0:T(8,128)S(1)} %fusion.60, f32[768,1536]{1,0:T(8,128)S(1)} %fusion.66, ...), kind=kOutput, calls=%fused_computation.173 | convolution fusion | flops 457703424 | bytes 22118404 | tf_op jit(solution)/shard_map/dot_general | solution.py:11
  221.6 4.1 %collective-permute-done.38 = bf16[768,768]{1,0:T(8,128)(2,1)S(1)} collective-permute-done((bf16[768,768]{1,0:T(8,128)(2,1)S(1)}, bf16[768,768]{1,0:T(8,128)(2,1)S(1)}, u32[]{:S(2)}, u32[]{:S(2)}) %collective-permute-start.38) | collective-permute-done | bytes 1179680 | tf_op jit(solution)/shard_map/ppermute | solution.py:116
  237.8 4.6 %collective-permute-done.37 = bf16[192,768]{1,0:T(8,128)(2,1)S(1)} collective-permute-done((bf16[192,768]{1,0:T(8,128)(2,1)S(1)}, bf16[192,768]{1,0:T(8,128)(2,1)S(1)}, u32[]{:S(2)}, u32[]{:S(2)}) %collective-permute-start.37) | collective-permute-done | bytes 294944 | tf_op jit(solution)/shard_map/ppermute | solution.py:30
  242.4 3.0 %fusion.3 = f32[1536,192]{0,1:T(8,128)} fusion(s32[1536]{0:T(1024)S(1)} %add.369, f32[1536,192]{0,1:T(8,128)S(1)} %copy-done.10, bf16[192,768]{1,0:T(8,128)(2,1)S(1)} %collective-permute-done.37, bf16[192,384]{1,0:T(8,128)(2,1)S(1)} %get-tuple-element.26, bf16[192,384]{1,0:T(8,128)(2,1)S(1)} %copy-done.9), kind=kOutput, calls=%fused_computation.8 | convolution fusion | flops 910983168 | bytes 2955264 | tf_op jit(solution)/shard_map/dot_general | solution.py:11
  245.4 9.6 %collective-permute-done.31 = bf16[192,1536]{1,0:T(8,128)(2,1)S(1)} collective-permute-done((bf16[192,1536]{1,0:T(8,128)(2,1)S(1)}, bf16[192,1536]{1,0:T(8,128)(2,1)S(1)}, u32[]{:S(2)}, u32[]{:S(2)}) %collective-permute-start.31) | collective-permute-done | bytes 589856 | tf_op jit(solution)/shard_map/ppermute | solution.py:30
  257.5 9.7 %collective-permute-done.40 = bf16[192,1536]{1,0:T(8,128)(2,1)S(1)} collective-permute-done((bf16[192,1536]{1,0:T(8,128)(2,1)S(1)}, bf16[192,1536]{1,0:T(8,128)(2,1)S(1)}, u32[]{:S(2)}, u32[]{:S(2)}) %collective-permute-start.40) | collective-permute-done | bytes 589856 | tf_op jit(solution)/shard_map/ppermute | solution.py:30
  (151 shorter events, 59.6 us)
Async XLA Ops:
  1.1 17.0 %collective-permute-start.11 = (bf16[192,1536]{1,0:T(8,128)(2,1)}, bf16[192,1536]{1,0:T(8,128)(2,1)S(1)}, u32[]{:S(2)}, u32[]{:S(2)}) collective-permute-start(bf16[192,1536]{1,0:T(8,128)(2,1)} %bitcast.143), channel_id=1, source_target_pairs={{0,4},{1,5},{2,6},{3,7},{4,0},{5,1},{6,2},{7,3},{8,12},{9,13},{10,... | collective-permute-start | bytes 1769480 | tf_op jit(solution)/shard_map/ppermute | solution.py:30
  3.7 27.2 %collective-permute-start.13 = (bf16[192,1536]{1,0:T(8,128)(2,1)}, bf16[192,1536]{1,0:T(8,128)(2,1)S(1)}, u32[]{:S(2)}, u32[]{:S(2)}) collective-permute-start(bf16[192,1536]{1,0:T(8,128)(2,1)} %bitcast.144), channel_id=1, source_target_pairs={{0,8},{1,9},{2,10},{3,11},{4,12},{5,13},{6,14},{7,15},{8,16},{9,17... | collective-permute-start | bytes 1769480 | tf_op jit(solution)/shard_map/ppermute | solution.py:30
  5.3 26.2 %collective-permute-start.4 = (bf16[192,1536]{1,0:T(8,128)(2,1)}, bf16[192,1536]{1,0:T(8,128)(2,1)}, u32[]{:S(2)}, u32[]{:S(2)}) collective-permute-start(bf16[192,1536]{1,0:T(8,128)(2,1)} %param.7), channel_id=1, source_target_pairs={{0,2},{1,3},{2,0},{3,1},{4,6},{5,7},{6,4},{7,5},{8,10},{9,11},{10,... | collective-permute-start | bytes 1769480 | tf_op jit(solution)/shard_map/ppermute | solution.py:30
  5.3 25.6 %collective-permute-start.1 = (bf16[192,1536]{1,0:T(8,128)(2,1)}, bf16[192,1536]{1,0:T(8,128)(2,1)}, u32[]{:S(2)}, u32[]{:S(2)}) collective-permute-start(bf16[192,1536]{1,0:T(8,128)(2,1)} %param.8), channel_id=1, source_target_pairs={{0,4},{1,5},{2,6},{3,7},{4,0},{5,1},{6,2},{7,3},{8,12},{9,13},{10,... | collective-permute-start | bytes 1769480 | tf_op jit(solution)/shard_map/ppermute | solution.py:30
  8.3 34.9 %collective-permute-start.5 = (bf16[192,1536]{1,0:T(8,128)(2,1)S(1)}, bf16[192,1536]{1,0:T(8,128)(2,1)S(1)}, u32[]{:S(2)}, u32[]{:S(2)}) collective-permute-start(bf16[192,1536]{1,0:T(8,128)(2,1)S(1)} %copy-done.3), channel_id=1, source_target_pairs={{0,4},{1,5},{2,6},{3,7},{4,0},{5,1},{6,2},{7,3},{8,12},{9,13},{10,... | collective-permute-start | bytes 1769480 | tf_op jit(solution)/shard_map/ppermute | solution.py:30
  18.1 26.9 %collective-permute-start = (bf16[192,1536]{1,0:T(8,128)(2,1)S(1)}, bf16[192,1536]{1,0:T(8,128)(2,1)S(1)}, u32[]{:S(2)}, u32[]{:S(2)}) collective-permute-start(bf16[192,1536]{1,0:T(8,128)(2,1)S(1)} %copy-done.11), channel_id=1, source_target_pairs={{0,2},{1,3},{2,0},{3,1},{4,6},{5,7},{6,4},{7,5},{8,10},{9,11},{10,... | collective-permute-start | bytes 1769480 | tf_op jit(solution)/shard_map/ppermute | solution.py:30
  30.9 17.9 %collective-permute-start.12 = (bf16[192,1536]{1,0:T(8,128)(2,1)S(1)}, bf16[192,1536]{1,0:T(8,128)(2,1)S(1)}, u32[]{:S(2)}, u32[]{:S(2)}) collective-permute-start(bf16[192,1536]{1,0:T(8,128)(2,1)S(1)} %collective-permute-done.11), channel_id=1, source_target_pairs={{0,2},{1,3},{2,0},{3,1},{4,6},{5,7},{6,4},{7,5},{8,10},{9,11},{10,... | collective-permute-start | bytes 1769480 | tf_op jit(solution)/shard_map/ppermute | solution.py:30
  31.5 28.7 %collective-permute-start.14 = (bf16[192,1536]{1,0:T(8,128)(2,1)S(1)}, bf16[192,1536]{1,0:T(8,128)(2,1)S(1)}, u32[]{:S(2)}, u32[]{:S(2)}) collective-permute-start(bf16[192,1536]{1,0:T(8,128)(2,1)S(1)} %collective-permute-done.13), channel_id=1, source_target_pairs={{0,2},{1,3},{2,0},{3,1},{4,6},{5,7},{6,4},{7,5},{8,10},{9,11},{10,... | collective-permute-start | bytes 1769480 | tf_op jit(solution)/shard_map/ppermute | solution.py:30
  43.2 17.0 %collective-permute-start.17 = (bf16[192,1536]{1,0:T(8,128)(2,1)S(1)}, bf16[192,1536]{1,0:T(8,128)(2,1)S(1)}, u32[]{:S(2)}, u32[]{:S(2)}) collective-permute-start(bf16[192,1536]{1,0:T(8,128)(2,1)S(1)} %collective-permute-done.13), channel_id=1, source_target_pairs={{0,8},{1,9},{2,10},{3,11},{4,12},{5,13},{6,14},{7,15},{8,16},{9,17... | collective-permute-start | bytes 1769480 | tf_op jit(solution)/shard_map/ppermute | solution.py:30
  45.0 16.8 %collective-permute-start.15 = (bf16[192,1536]{1,0:T(8,128)(2,1)S(1)}, bf16[192,1536]{1,0:T(8,128)(2,1)S(1)}, u32[]{:S(2)}, u32[]{:S(2)}) collective-permute-start(bf16[192,1536]{1,0:T(8,128)(2,1)S(1)} %collective-permute-done.13), channel_id=1, source_target_pairs={{0,4},{1,5},{2,6},{3,7},{4,0},{5,1},{6,2},{7,3},{8,12},{9,13},{10,... | collective-permute-start | bytes 1769480 | tf_op jit(solution)/shard_map/ppermute | solution.py:30
  60.1 20.9 %collective-permute-start.18 = (bf16[192,1536]{1,0:T(8,128)(2,1)S(1)}, bf16[192,1536]{1,0:T(8,128)(2,1)S(1)}, u32[]{:S(2)}, u32[]{:S(2)}) collective-permute-start(bf16[192,1536]{1,0:T(8,128)(2,1)S(1)} %collective-permute-done.17), channel_id=1, source_target_pairs={{0,2},{1,3},{2,0},{3,1},{4,6},{5,7},{6,4},{7,5},{8,10},{9,11},{10,... | collective-permute-start | bytes 1769480 | tf_op jit(solution)/shard_map/ppermute | solution.py:30
  60.3 20.5 %collective-permute-start.19 = (bf16[192,1536]{1,0:T(8,128)(2,1)S(1)}, bf16[192,1536]{1,0:T(8,128)(2,1)S(1)}, u32[]{:S(2)}, u32[]{:S(2)}) collective-permute-start(bf16[192,1536]{1,0:T(8,128)(2,1)S(1)} %collective-permute-done.17), channel_id=1, source_target_pairs={{0,4},{1,5},{2,6},{3,7},{4,0},{5,1},{6,2},{7,3},{8,12},{9,13},{10,... | collective-permute-start | bytes 1769480 | tf_op jit(solution)/shard_map/ppermute | solution.py:30
  61.8 18.4 %collective-permute-start.16 = (bf16[192,1536]{1,0:T(8,128)(2,1)S(1)}, bf16[192,1536]{1,0:T(8,128)(2,1)S(1)}, u32[]{:S(2)}, u32[]{:S(2)}) collective-permute-start(bf16[192,1536]{1,0:T(8,128)(2,1)S(1)} %collective-permute-done.15), channel_id=1, source_target_pairs={{0,2},{1,3},{2,0},{3,1},{4,6},{5,7},{6,4},{7,5},{8,10},{9,11},{10,... | collective-permute-start | bytes 1769480 | tf_op jit(solution)/shard_map/ppermute | solution.py:30
  62.2 18.0 %collective-permute-start.21 = (bf16[192,1536]{1,0:T(8,128)(2,1)S(1)}, bf16[192,1536]{1,0:T(8,128)(2,1)S(1)}, u32[]{:S(2)}, u32[]{:S(2)}) collective-permute-start(bf16[192,1536]{1,0:T(8,128)(2,1)S(1)} %collective-permute-done.17), channel_id=1, source_target_pairs={{0,8},{1,9},{2,10},{3,11},{4,12},{5,13},{6,14},{7,15},{8,16},{9,17... | collective-permute-start | bytes 1769480 | tf_op jit(solution)/shard_map/ppermute | solution.py:30
  65.8 26.4 %collective-permute-start.7 = (bf16[192,1536]{1,0:T(8,128)(2,1)S(1)}, bf16[192,1536]{1,0:T(8,128)(2,1)S(1)}, u32[]{:S(2)}, u32[]{:S(2)}) collective-permute-start(bf16[192,1536]{1,0:T(8,128)(2,1)S(1)} %convolution_convert_fusion.1), channel_id=1, source_target_pairs={{0,8},{1,9},{2,10},{3,11},{4,12},{5,13},{6,14},{7,15},{8,16},{9,17... | collective-permute-start | bytes 1769480 | tf_op jit(solution)/shard_map/ppermute | solution.py:30
  80.2 15.9 %collective-permute-start.22 = (bf16[192,1536]{1,0:T(8,128)(2,1)S(1)}, bf16[192,1536]{1,0:T(8,128)(2,1)S(1)}, u32[]{:S(2)}, u32[]{:S(2)}) collective-permute-start(bf16[192,1536]{1,0:T(8,128)(2,1)S(1)} %collective-permute-done.21), channel_id=1, source_target_pairs={{0,2},{1,3},{2,0},{3,1},{4,6},{5,7},{6,4},{7,5},{8,10},{9,11},{10,... | collective-permute-start | bytes 1769480 | tf_op jit(solution)/shard_map/ppermute | solution.py:30
  92.8 16.6 %collective-permute-start.8 = (bf16[192,1536]{1,0:T(8,128)(2,1)S(1)}, bf16[192,1536]{1,0:T(8,128)(2,1)S(1)}, u32[]{:S(2)}, u32[]{:S(2)}) collective-permute-start(bf16[192,1536]{1,0:T(8,128)(2,1)S(1)} %fusion.4), channel_id=1, source_target_pairs={{0,8},{1,9},{2,10},{3,11},{4,12},{5,13},{6,14},{7,15},{8,16},{9,17... | collective-permute-start | bytes 1769480 | tf_op jit(solution)/shard_map/ppermute | solution.py:30
  132.6 17.7 %collective-permute-start.32 = (bf16[192,1536]{1,0:T(8,128)(2,1)}, bf16[192,1536]{1,0:T(8,128)(2,1)S(1)}, u32[]{:S(2)}, u32[]{:S(2)}) collective-permute-start(bf16[192,1536]{1,0:T(8,128)(2,1)} %param.7), channel_id=1, source_target_pairs={{0,8},{1,9},{2,10},{3,11},{4,12},{5,13},{6,14},{7,15},{8,16},{9,17... | collective-permute-start | bytes 1769480 | tf_op jit(solution)/shard_map/ppermute | solution.py:30
  163.2 29.6 %collective-permute-start.27 = (bf16[192,1536]{1,0:T(8,128)(2,1)S(1)}, bf16[192,1536]{1,0:T(8,128)(2,1)S(1)}, u32[]{:S(2)}, u32[]{:S(2)}) collective-permute-start(bf16[192,1536]{1,0:T(8,128)(2,1)S(1)} %convolution_convert_fusion), channel_id=1, source_target_pairs={{0,8},{1,9},{2,10},{3,11},{4,12},{5,13},{6,14},{7,15},{8,16},{9,17... | collective-permute-start | bytes 1769480 | tf_op jit(solution)/shard_map/ppermute | solution.py:30
  164.6 24.7 %collective-permute-start.34 = (bf16[192,1536]{1,0:T(8,128)(2,1)S(1)}, bf16[192,1536]{1,0:T(8,128)(2,1)S(1)}, u32[]{:S(2)}, u32[]{:S(2)}) collective-permute-start(bf16[192,1536]{1,0:T(8,128)(2,1)S(1)} %collective-permute-done.33), channel_id=1, source_target_pairs={{0,8},{1,9},{2,10},{3,11},{4,12},{5,13},{6,14},{7,15},{8,16},{9,17... | collective-permute-start | bytes 1769480 | tf_op jit(solution)/shard_map/ppermute | solution.py:30
  192.9 32.8 %collective-permute-start.38 = (bf16[768,768]{1,0:T(8,128)(2,1)S(1)}, bf16[768,768]{1,0:T(8,128)(2,1)S(1)}, u32[]{:S(2)}, u32[]{:S(2)}) collective-permute-start(bf16[768,768]{1,0:T(8,128)(2,1)S(1)} %constant_dynamic-slice_fusion), channel_id=1, source_target_pairs={{0,1},{2,3},{4,5},{6,7},{8,9},{10,11},{12,13},{14,15},{17,16},{19,... | collective-permute-start | bytes 3538952 | tf_op jit(solution)/shard_map/ppermute | solution.py:116
  208.2 22.3 %collective-permute-start.36 = (bf16[384,384]{1,0:T(8,128)(2,1)}, bf16[384,384]{1,0:T(8,128)(2,1)}, u32[]{:S(2)}, u32[]{:S(2)}) collective-permute-start(bf16[384,384]{1,0:T(8,128)(2,1)} %pad_maximum_fusion.4), channel_id=1, source_target_pairs={{0,2},{1,3},{2,0},{3,1},{4,6},{5,7},{6,4},{7,5},{8,10},{9,11},{10,... | collective-permute-start | bytes 884744 | tf_op jit(solution)/shard_map/ppermute | solution.py:30
  235.0 20.0 %collective-permute-start.31 = (bf16[192,1536]{1,0:T(8,128)(2,1)S(1)}, bf16[192,1536]{1,0:T(8,128)(2,1)S(1)}, u32[]{:S(2)}, u32[]{:S(2)}) collective-permute-start(bf16[192,1536]{1,0:T(8,128)(2,1)S(1)} %fusion.34), channel_id=1, source_target_pairs={{0,4},{1,5},{2,6},{3,7},{4,0},{5,1},{6,2},{7,3},{8,12},{9,13},{10,... | collective-permute-start | bytes 1769480 | tf_op jit(solution)/shard_map/ppermute | solution.py:30
  237.0 30.3 %collective-permute-start.40 = (bf16[192,1536]{1,0:T(8,128)(2,1)S(1)}, bf16[192,1536]{1,0:T(8,128)(2,1)S(1)}, u32[]{:S(2)}, u32[]{:S(2)}) collective-permute-start(bf16[192,1536]{1,0:T(8,128)(2,1)S(1)} %fusion.29), channel_id=1, source_target_pairs={{0,4},{1,5},{2,6},{3,7},{4,0},{5,1},{6,2},{7,3},{8,12},{9,13},{10,... | collective-permute-start | bytes 1769480 | tf_op jit(solution)/shard_map/ppermute | solution.py:30
  (29 other events, 329.3 us)

commit v2 on v1

v2 whole, which is shorter than its diff:
```python
import jax
import jax.numpy as jnp
from jax import lax
from jax.sharding import PartitionSpec as P

BF16 = jnp.bfloat16
F32 = jnp.float32


def dot(left, right, left_dim, right_dim):
    return lax.dot_general(
        left, right, (((left_dim,), (right_dim,)), ((), ())), preferred_element_type=F32
    )


def tie(*values):
    return lax.optimization_barrier(values)


def solution(mesh):
    rows, X = mesh.shape["row"], mesh.shape["col"]
    A = rows // 4

    def sender(to):
        pairs = []
        for row in range(rows):
            for x in range(X):
                z, y, c, w = to(row // 4, row // 2 % 2, row % 2, x)
                pairs.append((row * X + x, ((z * 2 + y) * 2 + c) * X + w))
        return lambda value: lax.ppermute(value, ("row", "col"), pairs)

    flip_y = sender(lambda z, y, c, x: (z, 1 - y, c, x))
    flip_c = sender(lambda z, y, c, x: (z, y, 1 - c, x))
    up = sender(lambda z, y, c, x: ((z + 1) % A, y, c, x))
    along_x = [sender(lambda z, y, c, x, s=s: (z, y, c, (x + s) % X)) for s in range(X)]

    def plane_scatter(blocks):
        got = flip_c(jnp.concatenate([blocks[1], blocks[3]]).astype(BF16)).astype(F32)
        height = blocks[0].shape[0]
        mine, other = blocks[0] + got[:height], blocks[2] + got[height:]
        return mine + flip_y(other.astype(BF16)).astype(F32)

    def on_device(grad, left_basis, right_basis, first, second, left_factor, right_factor):
        b, width = grad.shape
        row, x = lax.axis_index("row"), lax.axis_index("col")
        z, y, c = row // 4, row // 2 % 2, row % 2
        per = A // X
        wide = 4 * b
        cuts = [(0, width // 2), (width // 2, width)]

        def at(blocks, index):
            return lax.dynamic_index_in_dim(blocks, index, 0, keepdims=False)

        def pick(rows_, side):
            k = jnp.arange(per * b)
            want = k // b * wide + (side * 2 + c) * b + k % b
            ones = (jnp.arange(width)[:, None] == want[None, :]).astype(BF16)
            return dot(ones, rows_, 0, 1).astype(BF16)

        rights = [right_basis.T]
        for r in range(1, A):
            rights.append(up(rights[-1]))
        left_rows = jnp.concatenate([left_basis, flip_c(left_basis)])
        left_y, grad = tie(pick(left_rows, 1 - y), grad)
        left_y, grad_y, grad_c = flip_y(left_y), flip_y(grad), flip_c(grad)
        left_mine = pick(left_rows, y)
        parts = [jnp.concatenate([left_mine, left_y], axis=1)]
        for s in range(1, X):
            parts.append(jnp.concatenate([along_x[s](left_mine), along_x[s](left_y)], axis=1))
        parts = jnp.stack(parts)
        left_cols = jnp.concatenate([at(parts, (x - w) % X) for w in range(X)]).reshape(A, b, wide)
        left_at = [at(left_cols, (z - r) % A) for r in range(A)]
        grad_yc = flip_c(grad_y)
        grad_plane = jnp.concatenate([grad, grad_c, grad_y, grad_yc])

        sums = [dot(left_at[1], grad_plane[:, lo:hi], 1, 0) for lo, hi in cuts]
        for r in range(2, A + 1):
            sums = [total.astype(BF16) for total in sums]
            if r < A:
                sums[0], rights[r] = tie(sums[0], rights[r])
            sums = [up(total) for total in sums]
            sums = [
                total.astype(F32) + dot(left_at[r % A], grad_plane[:, lo:hi], 1, 0)
                for total, (lo, hi) in zip(sums, cuts)
            ]
        left_proj = jnp.concatenate([total.astype(BF16) for total in sums], axis=1)

        right = jnp.zeros((A, 2, 2, b, width), BF16)
        for r, block in enumerate(rights):
            block, grad_y = tie(block, grad_y)
            other = flip_y(block)
            from_z = (z - r) % A
            q = (from_z // per - x) % X * per + from_z % per
            for k, piece in enumerate([block, flip_c(block), other, flip_c(other)]):
                place = (q, y ^ (k // 2), c ^ (k % 2), 0, 0)
                right = lax.dynamic_update_slice(right, piece[None, None, None], place)
        right = right.reshape(rows * b, width)

        grads, left_proj = tie(grad, left_proj)
        grads = [grads]
        for r in range(1, A):
            grads.append(up(grads[-1]))

        parts = [slice(p * wide, (p + 1) * wide) for p in range(per)]
        rotate = dot(left_proj, right, 1, 1)
        got = [[] for _ in parts]
        for s in range(1, X):
            for p in range(per):
                lo = s * width + p * wide
                got[p].append(along_x[s](rotate[:, lo : lo + wide].astype(BF16)))
        new_first, new_second, direction = [], [], []
        for p, part in enumerate(parts):
            rotated = rotate[:, part]
            for piece in got[p]:
                rotated += piece.astype(F32)
            new_first.append(0.9 * first.T[:, part] + 0.1 * rotated)
            new_second.append(0.95 * second.T[:, part] + 0.05 * rotated * rotated)
            bias_one = 1.0 - 0.9**10
            bias_two = 1.0 - 0.95**10
            root = jnp.sqrt(new_second[p] / bias_two) + 1e-08
            direction.append((new_first[p] / bias_one / root).astype(BF16))
        for s in range(X - 1, 0, -1):
            direction += [along_x[s](piece) for piece in direction[:per]]
        half = dot(jnp.concatenate(direction, axis=1), right, 1, 0).astype(BF16)
        halves = [half[:, lo:hi] for lo, hi in cuts]

        have = jnp.concatenate(grads)
        span = width // per
        cols = []
        for r, block in enumerate(grads):
            mine = lax.dynamic_slice_in_dim(block, z % per * span, span, 1)
            if r:
                mine, halves[1] = tie(mine, halves[1])
            take = mine
            for s in range(1, X):
                pairs = []
                for q in range(rows):
                    source = q // 4 // per
                    pairs.append((q * X + source, q * X + (source + s) % X))
                sent = lax.ppermute(mine, ("row", "col"), pairs)
                take = jnp.where((z // per + s) % X == x, sent, take)
            cols.append(take)
        cols = jnp.concatenate(cols)

        term = dot(cols, have, 0, 0).reshape(4, span // 4, width)
        right_sum = plane_scatter([at(term, (row % 4) ^ k) for k in range(4)])

        grad_rows = jnp.concatenate([grad, grad_c, grad_y, grad_yc])
        stacked = jnp.stack(grads)
        ordered = jnp.concatenate([at(stacked, (z - w) % A) for w in range(A)])
        term = dot(grad_rows, ordered, 1, 1)
        left_sum = lax.dynamic_slice_in_dim(term, x * per * b, per * b, 1)
        for s in range(1, X):
            piece = lax.dynamic_slice_in_dim(term, (x + s) % X * per * b, per * b, 1)
            left_sum += along_x[s](piece.astype(BF16)).astype(F32)
        own, core, over, cross = jnp.split(left_sum.astype(BF16), 4)
        got = flip_c(jnp.concatenate([core, cross]))
        over_pair = flip_y(jnp.concatenate([over, got[b:]], axis=1))
        joined = jnp.concatenate([own, got[:b], over_pair], axis=1)
        update = [dot(left_at[0], half, 0, 0) for half in halves]
        for r in range(1, A):
            halves = [up(half) for half in halves]
            if r == A - 1:
                halves[0], right_sum, joined = tie(halves[0], right_sum, joined)
            update = [total + dot(left_at[r], half, 0, 0) for total, half in zip(update, halves)]
        update = jnp.concatenate([plane_scatter(jnp.split(u, 4)) for u in update], axis=1)

        k, p, i = jnp.arange(4)[:, None, None], jnp.arange(per)[:, None], jnp.arange(b)
        goes = (p * wide + (k ^ (row % 4)) * b + i).reshape(-1)
        order = (goes[:, None] == jnp.arange(width)[None, :]).astype(BF16)
        new_right = 0.95 * right_factor.T + 0.05 * right_sum
        new_left = 0.95 * left_factor.T + 0.05 * dot(joined, order, 1, 0)
        new_first, new_second = (jnp.concatenate(v, axis=1) for v in (new_first, new_second))
        return update, new_first.T, new_second.T, new_left.T, new_right.T

    slab, turned = P("row", "col"), P("col", "row")
    return jax.shard_map(
        on_device,
        mesh=mesh,
        in_specs=(slab, slab) + (turned,) * 5,
        out_specs=(slab,) + (turned,) * 4,
        check_vma=False,
    )
```

time: 269 us -> 231 us (0.86)
  waiting for transfers between devices: 192 us -> 142 us
  starting transfers between devices: 27 us -> 40 us
  other arithmetic: 15.3 us -> 7.97 us
  local copies, waits for them, and re-layouts: 10.5 us -> 14.3 us
    ppermute x40 -> x50, waiting for transfers between devices: 188 us -> 134 us  [sender(): return lambda value: lax.ppermute(value, ('row', 'col'), pairs)]
    ppermute x1 -> x4, starting transfers between devices: 3.16 us -> 11.8 us  [on_device(): sent = lax.ppermute(mine, ('row', 'col'), pairs)]
    ppermute x40 -> x50, starting transfers between devices: 23.9 us -> 28.2 us  [sender(): return lambda value: lax.ppermute(value, ('row', 'col'), pairs)]
    ppermute x1 -> x4, waiting for transfers between devices: 4.12 us -> 8.2 us  [on_device(): sent = lax.ppermute(mine, ('row', 'col'), pairs)]
    dynamic_update_slice x16, local copies, waits for them, and re-layouts: 1.82 us -> 5.02 us  [on_device(): right = lax.dynamic_update_slice(right, piece[None, None, None], place)]
    transpose x2, other arithmetic: 5.96 us -> 2.9 us  [on_device(): return (update, new_first.T, new_second.T, new_left.T, new_right.T)]
    unnamed x30 -> x22, local copies, waits for them, and re-layouts: 4.29 us -> 6.98 us
    dot_general x14 -> x23, matrix products: 22.6 us -> 23.3 us  [dot(): lax.dot_general(left, right, (((left_dim,), (right_dim,)), ((), ())), pre...]
  transfers between devices with their start and end apart: 41 -> 54, of which waited for: 20 -> 30; matrix products, arithmetic and copies ran while one was open for 15% -> 19% of each run, Pallas kernels for 0% -> 0%
where the time goes in v2:
time: 231 us; the launch traced here: 230 us
  waiting for transfers between devices  142 us (61%)
  starting transfers between devices  40 us (17%)
  matrix products  23.3 us (10%)
  local copies, waits for them, and re-layouts  14.3 us (6%)
  other arithmetic  7.97 us (3%)
    ppermute x50, waiting for transfers between devices, sender(): return lambda value: lax.ppermute(value, ('row', 'col'), pairs)  134 us
    ppermute x50, starting transfers between devices, sender(): return lambda value: lax.ppermute(value, ('row', 'col'), pairs)  28.2 us
    dot_general x23, matrix products, dot(): lax.dot_general(left, right, (((left_dim,), (right_dim,)), ((), ())), pre...  23.3 us
    ppermute x4, starting transfers between devices, on_device(): sent = lax.ppermute(mine, ('row', 'col'), pairs)  11.8 us
    ppermute x4, waiting for transfers between devices, on_device(): sent = lax.ppermute(mine, ('row', 'col'), pairs)  8.2 us
    unnamed x22, local copies, waits for them, and re-layouts  6.98 us
    dynamic_update_slice x16, local copies, waits for them, and re-layouts, on_device(): right = lax.dynamic_update_slice(right, piece[None, None, None], place)  5.02 us
  transfers between devices with their start and end apart: 54, of which 30 were waited for; matrix products, arithmetic and copies ran while one was open for 19% of the time, Pallas kernels for 0%

profile of v2, /device:TPU:0, one launch (start us, length us, event | category | flops | bytes accessed | tf_op | source)
XLA Modules:
  0.0 230.1 jit_solution(17110499106044265772)
XLA Ops:
  11.7 8.2 %collective-permute-done.7 = bf16[192,1536]{1,0:T(8,128)(2,1)S(1)} collective-permute-done((bf16[192,1536]{1,0:T(8,128)(2,1)}, bf16[192,1536]{1,0:T(8,128)(2,1)S(1)}, u32[]{:S(2)}, u32[]{:S(2)}) %collective-permute-start.7) | collective-permute-done | bytes 589856 | tf_op jit(solution)/shard_map/ppermute | solution.py:30
  22.4 6.2 %collective-permute-done.5 = bf16[192,1536]{1,0:T(8,128)(2,1)S(1)} collective-permute-done((bf16[192,1536]{1,0:T(8,128)(2,1)S(1)}, bf16[192,1536]{1,0:T(8,128)(2,1)S(1)}, u32[]{:S(2)}, u32[]{:S(2)}) %collective-permute-start.5) | collective-permute-done | bytes 589856 | tf_op jit(solution)/shard_map/ppermute | solution.py:30
  46.0 15.5 %collective-permute-done.9 = bf16[192,768]{1,0:T(8,128)(2,1)S(1)} collective-permute-done((bf16[192,768]{1,0:T(8,128)(2,1)S(1)}, bf16[192,768]{1,0:T(8,128)(2,1)S(1)}, u32[]{:S(2)}, u32[]{:S(2)}) %collective-permute-start.9) | collective-permute-done | bytes 294944 | tf_op jit(solution)/shard_map/ppermute | solution.py:30
  62.0 3.8 %collective-permute-done.13 = bf16[192,768]{1,0:T(8,128)(2,1)S(1)} collective-permute-done((bf16[192,768]{1,0:T(8,128)(2,1)S(1)}, bf16[192,768]{1,0:T(8,128)(2,1)S(1)}, u32[]{:S(2)}, u32[]{:S(2)}) %collective-permute-start.13) | collective-permute-done | bytes 294944 | tf_op jit(solution)/shard_map/ppermute | solution.py:30
  67.4 6.2 %collective-permute-done.11 = bf16[192,768]{1,0:T(8,128)(2,1)S(1)} collective-permute-done((bf16[192,768]{1,0:T(8,128)(2,1)S(1)}, bf16[192,768]{1,0:T(8,128)(2,1)S(1)}, u32[]{:S(2)}, u32[]{:S(2)}) %collective-permute-start.11) | collective-permute-done | bytes 294944 | tf_op jit(solution)/shard_map/ppermute | solution.py:30
  75.5 4.1 %collective-permute-done.14 = bf16[192,768]{1,0:T(8,128)(2,1)S(1)} collective-permute-done((bf16[192,768]{1,0:T(8,128)(2,1)S(1)}, bf16[192,768]{1,0:T(8,128)(2,1)S(1)}, u32[]{:S(2)}, u32[]{:S(2)}) %collective-permute-start.14) | collective-permute-done | bytes 294944 | tf_op jit(solution)/shard_map/ppermute | solution.py:30
  84.6 5.8 %collective-permute-done.23 = bf16[192,1536]{1,0:T(8,128)(2,1)S(1)} collective-permute-done((bf16[192,1536]{1,0:T(8,128)(2,1)}, bf16[192,1536]{1,0:T(8,128)(2,1)S(1)}, u32[]{:S(2)}, u32[]{:S(2)}) %collective-permute-start.23) | collective-permute-done | bytes 589856 | tf_op jit(solution)/shard_map/ppermute | solution.py:30
  90.6 4.5 %collective-permute-done.12 = bf16[192,768]{1,0:T(8,128)(2,1)S(1)} collective-permute-done((bf16[192,768]{1,0:T(8,128)(2,1)S(1)}, bf16[192,768]{1,0:T(8,128)(2,1)S(1)}, u32[]{:S(2)}, u32[]{:S(2)}) %collective-permute-start.12) | collective-permute-done | bytes 294944 | tf_op jit(solution)/shard_map/ppermute | solution.py:30
  95.5 4.7 %collective-permute-done.15 = bf16[192,768]{1,0:T(8,128)(2,1)S(1)} collective-permute-done((bf16[192,768]{1,0:T(8,128)(2,1)S(1)}, bf16[192,768]{1,0:T(8,128)(2,1)S(1)}, u32[]{:S(2)}, u32[]{:S(2)}) %collective-permute-start.15) | collective-permute-done | bytes 294944 | tf_op jit(solution)/shard_map/ppermute | solution.py:30
  100.7 3.6 %collective-permute-start.35 = (bf16[192,768]{1,0:T(8,128)(2,1)S(1)}, bf16[192,768]{1,0:T(8,128)(2,1)S(1)}, u32[]{:S(2)}, u32[]{:S(2)}) collective-permute-start(bf16[192,768]{1,0:T(8,128)(2,1)S(1)} %constant_dynamic-slice_fusion.3), channel_id=1, source_target_pairs={{0,1},{2,3},{4,5},{6,7},{8,9},{10,11},{12,13},{14,15},{17,16},{19,... | collective-permute-start | bytes 884744 | tf_op jit(solution)/shard_map/ppermute | solution.py:140
  106.4 3.2 %fusion.152 = (bf16[192,3072]{1,0:T(8,128)(2,1)S(1)}, f32[192,3072]{1,0:T(8,128)S(1)}) fusion(bf16[192,1536]{1,0:T(8,128)(2,1)S(1)} %pad_maximum_fusion.4, bf16[3072,1536]{1,0:T(8,128)(2,1)S(1)} %bitcast.127), kind=kOutput, calls=%fused_computation.245 | convolution fusion | flops 1812529152 | bytes 13565952 | tf_op jit(solution)/shard_map/dot_general | solution.py:11
  111.9 4.6 %collective-permute-done.36 = bf16[192,1536]{1,0:T(8,128)(2,1)S(1)} collective-permute-done((bf16[192,1536]{1,0:T(8,128)(2,1)S(1)}, bf16[192,1536]{1,0:T(8,128)(2,1)S(1)}, u32[]{:S(2)}, u32[]{:S(2)}) %collective-permute-start.36) | collective-permute-done | bytes 589856 | tf_op jit(solution)/shard_map/ppermute | solution.py:30
  119.6 5.5 %collective-permute-done.29 = bf16[192,768]{1,0:T(8,128)(2,1)S(1)} collective-permute-done((bf16[192,768]{1,0:T(8,128)(2,1)S(1)}, bf16[192,768]{1,0:T(8,128)(2,1)S(1)}, u32[]{:S(2)}, u32[]{:S(2)}) %collective-permute-start.29) | collective-permute-done | bytes 294944 | tf_op jit(solution)/shard_map/ppermute | solution.py:30
  131.5 4.5 %collective-permute-done.30 = bf16[192,768]{1,0:T(8,128)(2,1)S(1)} collective-permute-done((bf16[192,768]{1,0:T(8,128)(2,1)S(1)}, bf16[192,768]{1,0:T(8,128)(2,1)S(1)}, u32[]{:S(2)}, u32[]{:S(2)}) %collective-permute-start.30) | collective-permute-done | bytes 294944 | tf_op jit(solution)/shard_map/ppermute | solution.py:30
  136.0 4.6 %collective-permute-done.31 = bf16[192,768]{1,0:T(8,128)(2,1)S(1)} collective-permute-done((bf16[192,768]{1,0:T(8,128)(2,1)S(1)}, bf16[192,768]{1,0:T(8,128)(2,1)S(1)}, u32[]{:S(2)}, u32[]{:S(2)}) %collective-permute-start.31) | collective-permute-done | bytes 294944 | tf_op jit(solution)/shard_map/ppermute | solution.py:30
  147.1 5.5 %collective-permute-done.37 = bf16[192,768]{1,0:T(8,128)(2,1)S(1)} collective-permute-done((bf16[192,768]{1,0:T(8,128)(2,1)S(1)}, bf16[192,768]{1,0:T(8,128)(2,1)S(1)}, u32[]{:S(2)}, u32[]{:S(2)}) %collective-permute-start.37) | collective-permute-done | bytes 294944 | tf_op jit(solution)/shard_map/ppermute | solution.py:140
  152.7 3.1 %collective-permute-done.32 = bf16[192,768]{1,0:T(8,128)(2,1)S(1)} collective-permute-done((bf16[192,768]{1,0:T(8,128)(2,1)S(1)}, bf16[192,768]{1,0:T(8,128)(2,1)S(1)}, u32[]{:S(2)}, u32[]{:S(2)}) %collective-permute-start.32) | collective-permute-done | bytes 294944 | tf_op jit(solution)/shard_map/ppermute | solution.py:30
  157.7 4.4 %collective-permute-start.41 = (bf16[192,768]{1,0:T(8,128)(2,1)S(1)}, bf16[192,768]{1,0:T(8,128)(2,1)S(1)}, u32[]{:S(2)}, u32[]{:S(2)}) collective-permute-start(bf16[192,768]{1,0:T(8,128)(2,1)S(1)} %constant_dynamic-slice_fusion), channel_id=1, source_target_pairs={{0,1},{2,3},{4,5},{6,7},{8,9},{10,11},{12,13},{14,15},{17,16},{19,... | collective-permute-start | bytes 884744 | tf_op jit(solution)/shard_map/ppermute | solution.py:140
  171.8 5.5 %collective-permute-done.49 = bf16[192,768]{1,0:T(8,128)(2,1)S(1)} collective-permute-done((bf16[192,768]{1,0:T(8,128)(2,1)S(1)}, bf16[192,768]{1,0:T(8,128)(2,1)S(1)}, u32[]{:S(2)}, u32[]{:S(2)}) %collective-permute-start.49) | collective-permute-done | bytes 294944 | tf_op jit(solution)/shard_map/ppermute | solution.py:30
  179.9 6.9 %collective-permute-done.50 = bf16[192,768]{1,0:T(8,128)(2,1)S(1)} collective-permute-done((bf16[192,768]{1,0:T(8,128)(2,1)S(1)}, bf16[192,768]{1,0:T(8,128)(2,1)S(1)}, u32[]{:S(2)}, u32[]{:S(2)}) %collective-permute-start.50) | collective-permute-done | bytes 294944 | tf_op jit(solution)/shard_map/ppermute | solution.py:30
  188.1 7.2 %collective-permute-done.51 = bf16[192,768]{1,0:T(8,128)(2,1)S(1)} collective-permute-done((bf16[192,768]{1,0:T(8,128)(2,1)S(1)}, bf16[192,768]{1,0:T(8,128)(2,1)S(1)}, u32[]{:S(2)}, u32[]{:S(2)}) %collective-permute-start.51) | collective-permute-done | bytes 294944 | tf_op jit(solution)/shard_map/ppermute | solution.py:30
  199.5 13.3 %collective-permute-done.43 = bf16[192,1536]{1,0:T(8,128)(2,1)S(1)} collective-permute-done((bf16[192,1536]{1,0:T(8,128)(2,1)S(1)}, bf16[192,1536]{1,0:T(8,128)(2,1)S(1)}, u32[]{:S(2)}, u32[]{:S(2)}) %collective-permute-start.43) | collective-permute-done | bytes 589856 | tf_op jit(solution)/shard_map/ppermute | solution.py:30
  213.8 4.9 %collective-permute-done.53 = bf16[192,768]{1,0:T(8,128)(2,1)S(1)} collective-permute-done((bf16[192,768]{1,0:T(8,128)(2,1)S(1)}, bf16[192,768]{1,0:T(8,128)(2,1)S(1)}, u32[]{:S(2)}, u32[]{:S(2)}) %collective-permute-start.53) | collective-permute-done | bytes 294944 | tf_op jit(solution)/shard_map/ppermute | solution.py:30
  224.3 4.5 %collective-permute-done.48 = bf16[192,768]{1,0:T(8,128)(2,1)S(1)} collective-permute-done((bf16[192,768]{1,0:T(8,128)(2,1)S(1)}, bf16[192,768]{1,0:T(8,128)(2,1)S(1)}, u32[]{:S(2)}, u32[]{:S(2)}) %collective-permute-start.48) | collective-permute-done | bytes 294944 | tf_op jit(solution)/shard_map/ppermute | solution.py:30
  (200 shorter events, 87.8 us)
Async XLA Ops:
  1.1 18.8 %collective-permute-start.7 = (bf16[192,1536]{1,0:T(8,128)(2,1)}, bf16[192,1536]{1,0:T(8,128)(2,1)S(1)}, u32[]{:S(2)}, u32[]{:S(2)}) collective-permute-start(bf16[192,1536]{1,0:T(8,128)(2,1)} %bitcast.156), channel_id=1, source_target_pairs={{0,8},{1,9},{2,10},{3,11},{4,12},{5,13},{6,14},{7,15},{8,16},{9,17... | collective-permute-start | bytes 1769480 | tf_op jit(solution)/shard_map/ppermute | solution.py:30
  8.7 19.9 %collective-permute-start.5 = (bf16[192,1536]{1,0:T(8,128)(2,1)S(1)}, bf16[192,1536]{1,0:T(8,128)(2,1)S(1)}, u32[]{:S(2)}, u32[]{:S(2)}) collective-permute-start(bf16[192,1536]{1,0:T(8,128)(2,1)S(1)} %copy-done), channel_id=1, source_target_pairs={{0,4},{1,5},{2,6},{3,7},{4,0},{5,1},{6,2},{7,3},{8,12},{9,13},{10,... | collective-permute-start | bytes 1769480 | tf_op jit(solution)/shard_map/ppermute | solution.py:30
  9.3 22.2 %collective-permute-start.4 = (bf16[192,1536]{1,0:T(8,128)(2,1)S(1)}, bf16[192,1536]{1,0:T(8,128)(2,1)}, u32[]{:S(2)}, u32[]{:S(2)}) collective-permute-start(bf16[192,1536]{1,0:T(8,128)(2,1)S(1)} %copy-done), channel_id=1, source_target_pairs={{0,2},{1,3},{2,0},{3,1},{4,6},{5,7},{6,4},{7,5},{8,10},{9,11},{10,... | collective-permute-start | bytes 1769480 | tf_op jit(solution)/shard_map/ppermute | solution.py:30
  10.2 18.5 %collective-permute-start.2 = (bf16[384,384]{0,1:T(8,128)(2,1)S(1)}, bf16[384,384]{0,1:T(8,128)(2,1)S(1)}, u32[]{:S(2)}, u32[]{:S(2)}) collective-permute-start(bf16[384,384]{0,1:T(8,128)(2,1)S(1)} %fusion.36), channel_id=1, source_target_pairs={{0,1},{1,0},{2,3},{3,2},{4,5},{5,4},{6,7},{7,6},{8,9},{9,8},{10,11... | collective-permute-start | bytes 884744 | tf_op jit(solution)/shard_map/ppermute | solution.py:30
  20.0 17.0 %collective-permute-start.8 = (bf16[192,1536]{1,0:T(8,128)(2,1)S(1)}, bf16[192,1536]{1,0:T(8,128)(2,1)}, u32[]{:S(2)}, u32[]{:S(2)}) collective-permute-start(bf16[192,1536]{1,0:T(8,128)(2,1)S(1)} %collective-permute-done.7), channel_id=1, source_target_pairs={{0,8},{1,9},{2,10},{3,11},{4,12},{5,13},{6,14},{7,15},{8,16},{9,17... | collective-permute-start | bytes 1769480 | tf_op jit(solution)/shard_map/ppermute | solution.py:30
  28.6 15.9 %collective-permute-start.17 = (bf16[192,1536]{1,0:T(8,128)(2,1)S(1)}, bf16[192,1536]{1,0:T(8,128)(2,1)}, u32[]{:S(2)}, u32[]{:S(2)}) collective-permute-start(bf16[192,1536]{1,0:T(8,128)(2,1)S(1)} %bitcast.158), channel_id=1, source_target_pairs={{0,4},{1,5},{2,6},{3,7},{4,0},{5,1},{6,2},{7,3},{8,12},{9,13},{10,... | collective-permute-start | bytes 1769480 | tf_op jit(solution)/shard_map/ppermute | solution.py:30
  30.2 50.4 %collective-permute-start.19 = (bf16[192,1536]{1,0:T(8,128)(2,1)S(1)}, bf16[192,1536]{1,0:T(8,128)(2,1)}, u32[]{:S(2)}, u32[]{:S(2)}) collective-permute-start(bf16[192,1536]{1,0:T(8,128)(2,1)S(1)} %collective-permute-done.7), channel_id=1, source_target_pairs={{0,2},{1,3},{2,0},{3,1},{4,6},{5,7},{6,4},{7,5},{8,10},{9,11},{10,... | collective-permute-start | bytes 1769480 | tf_op jit(solution)/shard_map/ppermute | solution.py:30
  37.0 25.0 %collective-permute-start.10 = (bf16[192,1536]{1,0:T(8,128)(2,1)}, bf16[192,1536]{1,0:T(8,128)(2,1)S(1)}, u32[]{:S(2)}, u32[]{:S(2)}) collective-permute-start(bf16[192,1536]{1,0:T(8,128)(2,1)} %collective-permute-done.8), channel_id=1, source_target_pairs={{0,8},{1,9},{2,10},{3,11},{4,12},{5,13},{6,14},{7,15},{8,16},{9,17... | collective-permute-start | bytes 1769480 | tf_op jit(solution)/shard_map/ppermute | solution.py:30
  40.0 21.6 %collective-permute-start.9 = (bf16[192,768]{1,0:T(8,128)(2,1)S(1)}, bf16[192,768]{1,0:T(8,128)(2,1)S(1)}, u32[]{:S(2)}, u32[]{:S(2)}) collective-permute-start(bf16[192,768]{1,0:T(8,128)(2,1)S(1)} %convolution_convert_fusion.2), channel_id=1, source_target_pairs={{0,8},{1,9},{2,10},{3,11},{4,12},{5,13},{6,14},{7,15},{8,16},{9,17... | collective-permute-start | bytes 884744 | tf_op jit(solution)/shard_map/ppermute | solution.py:30
  41.6 24.2 %collective-permute-start.13 = (bf16[192,768]{1,0:T(8,128)(2,1)S(1)}, bf16[192,768]{1,0:T(8,128)(2,1)S(1)}, u32[]{:S(2)}, u32[]{:S(2)}) collective-permute-start(bf16[192,768]{1,0:T(8,128)(2,1)S(1)} %convolution_convert_fusion.1), channel_id=1, source_target_pairs={{0,8},{1,9},{2,10},{3,11},{4,12},{5,13},{6,14},{7,15},{8,16},{9,17... | collective-permute-start | bytes 884744 | tf_op jit(solution)/shard_map/ppermute | solution.py:30
  44.5 29.6 %collective-permute-start.20 = (bf16[192,1536]{1,0:T(8,128)(2,1)S(1)}, bf16[192,1536]{1,0:T(8,128)(2,1)S(1)}, u32[]{:S(2)}, u32[]{:S(2)}) collective-permute-start(bf16[192,1536]{1,0:T(8,128)(2,1)S(1)} %collective-permute-done.7), channel_id=1, source_target_pairs={{0,4},{1,5},{2,6},{3,7},{4,0},{5,1},{6,2},{7,3},{8,12},{9,13},{10,... | collective-permute-start | bytes 1769480 | tf_op jit(solution)/shard_map/ppermute | solution.py:30
  61.5 18.4 %collective-permute-start.18 = (bf16[192,1536]{1,0:T(8,128)(2,1)}, bf16[192,1536]{1,0:T(8,128)(2,1)S(1)}, u32[]{:S(2)}, u32[]{:S(2)}) collective-permute-start(bf16[192,1536]{1,0:T(8,128)(2,1)} %collective-permute-done.17), channel_id=1, source_target_pairs={{0,2},{1,3},{2,0},{3,1},{4,6},{5,7},{6,4},{7,5},{8,10},{9,11},{10,... | collective-permute-start | bytes 1769480 | tf_op jit(solution)/shard_map/ppermute | solution.py:30
  74.1 16.4 %collective-permute-start.23 = (bf16[192,1536]{1,0:T(8,128)(2,1)}, bf16[192,1536]{1,0:T(8,128)(2,1)S(1)}, u32[]{:S(2)}, u32[]{:S(2)}) collective-permute-start(bf16[192,1536]{1,0:T(8,128)(2,1)} %collective-permute-done.8), channel_id=1, source_target_pairs={{0,4},{1,5},{2,6},{3,7},{4,0},{5,1},{6,2},{7,3},{8,12},{9,13},{10,... | collective-permute-start | bytes 1769480 | tf_op jit(solution)/shard_map/ppermute | solution.py:30
  80.0 24.5 %collective-permute-start.25 = (bf16[192,1536]{1,0:T(8,128)(2,1)S(1)}, bf16[192,1536]{1,0:T(8,128)(2,1)S(1)}, u32[]{:S(2)}, u32[]{:S(2)}) collective-permute-start(bf16[192,1536]{1,0:T(8,128)(2,1)S(1)} %collective-permute-done.10), channel_id=1, source_target_pairs={{0,2},{1,3},{2,0},{3,1},{4,6},{5,7},{6,4},{7,5},{8,10},{9,11},{10,... | collective-permute-start | bytes 1769480 | tf_op jit(solution)/shard_map/ppermute | solution.py:30
  80.7 23.6 %collective-permute-start.26 = (bf16[192,1536]{1,0:T(8,128)(2,1)S(1)}, bf16[192,1536]{1,0:T(8,128)(2,1)S(1)}, u32[]{:S(2)}, u32[]{:S(2)}) collective-permute-start(bf16[192,1536]{1,0:T(8,128)(2,1)S(1)} %collective-permute-done.10), channel_id=1, source_target_pairs={{0,4},{1,5},{2,6},{3,7},{4,0},{5,1},{6,2},{7,3},{8,12},{9,13},{10,... | collective-permute-start | bytes 1769480 | tf_op jit(solution)/shard_map/ppermute | solution.py:30
  84.6 15.6 %collective-permute-start.15 = (bf16[192,768]{1,0:T(8,128)(2,1)S(1)}, bf16[192,768]{1,0:T(8,128)(2,1)S(1)}, u32[]{:S(2)}, u32[]{:S(2)}) collective-permute-start(bf16[192,768]{1,0:T(8,128)(2,1)S(1)} %fusion.33), channel_id=1, source_target_pairs={{0,8},{1,9},{2,10},{3,11},{4,12},{5,13},{6,14},{7,15},{8,16},{9,17... | collective-permute-start | bytes 884744 | tf_op jit(solution)/shard_map/ppermute | solution.py:30
  100.6 15.9 %collective-permute-start.36 = (bf16[192,1536]{1,0:T(8,128)(2,1)S(1)}, bf16[192,1536]{1,0:T(8,128)(2,1)S(1)}, u32[]{:S(2)}, u32[]{:S(2)}) collective-permute-start(bf16[192,1536]{1,0:T(8,128)(2,1)S(1)} %copy-done), channel_id=1, source_target_pairs={{0,8},{1,9},{2,10},{3,11},{4,12},{5,13},{6,14},{7,15},{8,16},{9,17... | collective-permute-start | bytes 1769480 | tf_op jit(solution)/shard_map/ppermute | solution.py:30
  109.8 15.4 %collective-permute-start.29 = (bf16[192,768]{1,0:T(8,128)(2,1)S(1)}, bf16[192,768]{1,0:T(8,128)(2,1)S(1)}, u32[]{:S(2)}, u32[]{:S(2)}) collective-permute-start(bf16[192,768]{1,0:T(8,128)(2,1)S(1)} %get-tuple-element.75), channel_id=1, source_target_pairs={{0,1},{1,0},{2,3},{3,2},{4,5},{5,4},{6,7},{7,6},{8,9},{9,8},{10,11... | collective-permute-start | bytes 884744 | tf_op jit(solution)/shard_map/ppermute | solution.py:30
  116.5 15.0 %collective-permute-start.38 = (bf16[192,1536]{1,0:T(8,128)(2,1)S(1)}, bf16[192,1536]{1,0:T(8,128)(2,1)S(1)}, u32[]{:S(2)}, u32[]{:S(2)}) collective-permute-start(bf16[192,1536]{1,0:T(8,128)(2,1)S(1)} %collective-permute-done.36), channel_id=1, source_target_pairs={{0,8},{1,9},{2,10},{3,11},{4,12},{5,13},{6,14},{7,15},{8,16},{9,17... | collective-permute-start | bytes 1769480 | tf_op jit(solution)/shard_map/ppermute | solution.py:30
  131.5 25.7 %collective-permute-start.40 = (bf16[192,1536]{1,0:T(8,128)(2,1)S(1)}, bf16[192,1536]{1,0:T(8,128)(2,1)S(1)}, u32[]{:S(2)}, u32[]{:S(2)}) collective-permute-start(bf16[192,1536]{1,0:T(8,128)(2,1)S(1)} %collective-permute-done.38), channel_id=1, source_target_pairs={{0,8},{1,9},{2,10},{3,11},{4,12},{5,13},{6,14},{7,15},{8,16},{9,17... | collective-permute-start | bytes 1769480 | tf_op jit(solution)/shard_map/ppermute | solution.py:30
  166.0 47.0 %collective-permute-start.34 = (bf16[192,768]{1,0:T(8,128)(2,1)S(1)}, bf16[192,768]{1,0:T(8,128)(2,1)S(1)}, u32[]{:S(2)}, u32[]{:S(2)}) collective-permute-start(bf16[192,768]{1,0:T(8,128)(2,1)S(1)} %collective-permute-done.33), channel_id=1, source_target_pairs={{0,8},{1,9},{2,10},{3,11},{4,12},{5,13},{6,14},{7,15},{8,16},{9,17... | collective-permute-start | bytes 884744 | tf_op jit(solution)/shard_map/ppermute | solution.py:30
  171.7 24.4 %collective-permute-start.42 = (bf16[384,1536]{1,0:T(8,128)(2,1)S(1)}, bf16[384,1536]{1,0:T(8,128)(2,1)S(1)}, u32[]{:S(2)}, u32[]{:S(2)}) collective-permute-start(bf16[384,1536]{1,0:T(8,128)(2,1)S(1)} %pad_maximum_fusion.2), channel_id=1, source_target_pairs={{0,2},{1,3},{2,0},{3,1},{4,6},{5,7},{6,4},{7,5},{8,10},{9,11},{10,... | collective-permute-start | bytes 3538952 | tf_op jit(solution)/shard_map/ppermute | solution.py:30
  196.5 16.2 %collective-permute-start.43 = (bf16[192,1536]{1,0:T(8,128)(2,1)S(1)}, bf16[192,1536]{1,0:T(8,128)(2,1)S(1)}, u32[]{:S(2)}, u32[]{:S(2)}) collective-permute-start(bf16[192,1536]{1,0:T(8,128)(2,1)S(1)} %fusion.37), channel_id=1, source_target_pairs={{0,4},{1,5},{2,6},{3,7},{4,0},{5,1},{6,2},{7,3},{8,12},{9,13},{10,... | collective-permute-start | bytes 1769480 | tf_op jit(solution)/shard_map/ppermute | solution.py:30
  198.2 20.4 %collective-permute-start.53 = (bf16[192,768]{1,0:T(8,128)(2,1)S(1)}, bf16[192,768]{1,0:T(8,128)(2,1)S(1)}, u32[]{:S(2)}, u32[]{:S(2)}) collective-permute-start(bf16[192,768]{1,0:T(8,128)(2,1)S(1)} %fusion.70), channel_id=1, source_target_pairs={{0,4},{1,5},{2,6},{3,7},{4,0},{5,1},{6,2},{7,3},{8,12},{9,13},{10,... | collective-permute-start | bytes 884744 | tf_op jit(solution)/shard_map/ppermute | solution.py:30
  (39 other events, 361.2 us)

commit v3 on v2

--- a/solution.py
+++ b/solution.py
@@ -122,6 +122,7 @@
         for s in range(X - 1, 0, -1):
             direction += [along_x[s](piece) for piece in direction[:per]]
         half = dot(jnp.concatenate(direction, axis=1), right, 1, 0).astype(BF16)
+        late, half = tie(grads[A - 2], half)
         halves = [half[:, lo:hi] for lo, hi in cuts]
 
         have = jnp.concatenate(grads)
@@ -129,15 +130,9 @@
         cols = []
         for r, block in enumerate(grads):
             mine = lax.dynamic_slice_in_dim(block, z % per * span, span, 1)
-            if r:
-                mine, halves[1] = tie(mine, halves[1])
             take = mine
             for s in range(1, X):
-                pairs = []
-                for q in range(rows):
-                    source = q // 4 // per
-                    pairs.append((q * X + source, q * X + (source + s) % X))
-                sent = lax.ppermute(mine, ("row", "col"), pairs)
+                sent = along_x[s](mine)
                 take = jnp.where((z // per + s) % X == x, sent, take)
             cols.append(take)
         cols = jnp.concatenate(cols)
@@ -160,8 +155,6 @@
         update = [dot(left_at[0], half, 0, 0) for half in halves]
         for r in range(1, A):
             halves = [up(half) for half in halves]
-            if r == A - 1:
-                halves[0], right_sum, joined = tie(halves[0], right_sum, joined)
             update = [total + dot(left_at[r], half, 0, 0) for total, half in zip(update, halves)]
         update = jnp.concatenate([plane_scatter(jnp.split(u, 4)) for u in update], axis=1)
 

time: 231 us -> 226 us (0.978)
  starting transfers between devices: 40 us -> 35.5 us
    ppermute x4 -> x0, starting transfers between devices: 11.8 us -> none  [on_device(): sent = lax.ppermute(mine, ('row', 'col'), pairs)]
    ppermute x50 -> x54, waiting for transfers between devices: 134 us -> 143 us  [sender(): return lambda value: lax.ppermute(value, ('row', 'col'), pairs)]
    ppermute x4 -> x0, waiting for transfers between devices: 8.2 us -> none  [on_device(): sent = lax.ppermute(mine, ('row', 'col'), pairs)]
    ppermute x50 -> x54, starting transfers between devices: 28.2 us -> 35.5 us  [sender(): return lambda value: lax.ppermute(value, ('row', 'col'), pairs)]
  transfers between devices with their start and end apart: 54 -> 54, of which waited for: 30 -> 31; matrix products, arithmetic and copies ran while one was open for 19% -> 19% of each run, Pallas kernels for 0% -> 0%
where the time goes in v3:
time: 226 us; the launch traced here: 225 us
  waiting for transfers between devices  143 us (63%)
  starting transfers between devices  35.5 us (16%)
  matrix products  23.5 us (10%)
  local copies, waits for them, and re-layouts  13.7 us (6%)
  other arithmetic  7.99 us (4%)
    ppermute x54, waiting for transfers between devices, sender(): return lambda value: lax.ppermute(value, ('row', 'col'), pairs)  143 us
    ppermute x54, starting transfers between devices, sender(): return lambda value: lax.ppermute(value, ('row', 'col'), pairs)  35.5 us
    dot_general x23, matrix products, dot(): lax.dot_general(left, right, (((left_dim,), (right_dim,)), ((), ())), pre...  23.5 us
    unnamed x22, local copies, waits for them, and re-layouts  7.46 us
  transfers between devices with their start and end apart: 54, of which 31 were waited for; matrix products, arithmetic and copies ran while one was open for 19% of the time, Pallas kernels for 0%

profile of v3, /device:TPU:0, one launch (start us, length us, event | category | flops | bytes accessed | tf_op | source)
XLA Modules:
  0.0 225.1 jit_solution(17291927273520898613)
XLA Ops:
  1.1 2.6 %collective-permute-start.7 = (bf16[192,1536]{1,0:T(8,128)(2,1)}, bf16[192,1536]{1,0:T(8,128)(2,1)S(1)}, u32[]{:S(2)}, u32[]{:S(2)}) collective-permute-start(bf16[192,1536]{1,0:T(8,128)(2,1)} %bitcast.152), channel_id=1, source_target_pairs={{0,8},{1,9},{2,10},{3,11},{4,12},{5,13},{6,14},{7,15},{8,16},{9,17... | collective-permute-start | bytes 1769480 | tf_op jit(solution)/shard_map/ppermute | solution.py:30
  11.8 8.2 %collective-permute-done.7 = bf16[192,1536]{1,0:T(8,128)(2,1)S(1)} collective-permute-done((bf16[192,1536]{1,0:T(8,128)(2,1)}, bf16[192,1536]{1,0:T(8,128)(2,1)S(1)}, u32[]{:S(2)}, u32[]{:S(2)}) %collective-permute-start.7) | collective-permute-done | bytes 589856 | tf_op jit(solution)/shard_map/ppermute | solution.py:30
  22.4 6.2 %collective-permute-done.5 = bf16[192,1536]{1,0:T(8,128)(2,1)S(1)} collective-permute-done((bf16[192,1536]{1,0:T(8,128)(2,1)S(1)}, bf16[192,1536]{1,0:T(8,128)(2,1)S(1)}, u32[]{:S(2)}, u32[]{:S(2)}) %collective-permute-start.5) | collective-permute-done | bytes 589856 | tf_op jit(solution)/shard_map/ppermute | solution.py:30
  46.0 15.5 %collective-permute-done.9 = bf16[192,768]{1,0:T(8,128)(2,1)S(1)} collective-permute-done((bf16[192,768]{1,0:T(8,128)(2,1)S(1)}, bf16[192,768]{1,0:T(8,128)(2,1)S(1)}, u32[]{:S(2)}, u32[]{:S(2)}) %collective-permute-start.9) | collective-permute-done | bytes 294944 | tf_op jit(solution)/shard_map/ppermute | solution.py:30
  62.0 3.8 %collective-permute-done.13 = bf16[192,768]{1,0:T(8,128)(2,1)S(1)} collective-permute-done((bf16[192,768]{1,0:T(8,128)(2,1)S(1)}, bf16[192,768]{1,0:T(8,128)(2,1)S(1)}, u32[]{:S(2)}, u32[]{:S(2)}) %collective-permute-start.13) | collective-permute-done | bytes 294944 | tf_op jit(solution)/shard_map/ppermute | solution.py:30
  67.4 6.2 %collective-permute-done.11 = bf16[192,768]{1,0:T(8,128)(2,1)S(1)} collective-permute-done((bf16[192,768]{1,0:T(8,128)(2,1)S(1)}, bf16[192,768]{1,0:T(8,128)(2,1)S(1)}, u32[]{:S(2)}, u32[]{:S(2)}) %collective-permute-start.11) | collective-permute-done | bytes 294944 | tf_op jit(solution)/shard_map/ppermute | solution.py:30
  75.5 4.1 %collective-permute-done.14 = bf16[192,768]{1,0:T(8,128)(2,1)S(1)} collective-permute-done((bf16[192,768]{1,0:T(8,128)(2,1)S(1)}, bf16[192,768]{1,0:T(8,128)(2,1)S(1)}, u32[]{:S(2)}, u32[]{:S(2)}) %collective-permute-start.14) | collective-permute-done | bytes 294944 | tf_op jit(solution)/shard_map/ppermute | solution.py:30
  83.6 6.9 %collective-permute-done.25 = bf16[192,1536]{1,0:T(8,128)(2,1)S(1)} collective-permute-done((bf16[192,1536]{1,0:T(8,128)(2,1)}, bf16[192,1536]{1,0:T(8,128)(2,1)S(1)}, u32[]{:S(2)}, u32[]{:S(2)}) %collective-permute-start.25) | collective-permute-done | bytes 589856 | tf_op jit(solution)/shard_map/ppermute | solution.py:30
  90.6 3.4 %collective-permute-done.12 = bf16[192,768]{1,0:T(8,128)(2,1)S(1)} collective-permute-done((bf16[192,768]{1,0:T(8,128)(2,1)S(1)}, bf16[192,768]{1,0:T(8,128)(2,1)S(1)}, u32[]{:S(2)}, u32[]{:S(2)}) %collective-permute-start.12) | collective-permute-done | bytes 294944 | tf_op jit(solution)/shard_map/ppermute | solution.py:30
  94.4 4.7 %collective-permute-done.15 = bf16[192,768]{1,0:T(8,128)(2,1)S(1)} collective-permute-done((bf16[192,768]{1,0:T(8,128)(2,1)S(1)}, bf16[192,768]{1,0:T(8,128)(2,1)S(1)}, u32[]{:S(2)}, u32[]{:S(2)}) %collective-permute-start.15) | collective-permute-done | bytes 294944 | tf_op jit(solution)/shard_map/ppermute | solution.py:30
  104.8 3.2 %fusion.161 = (bf16[192,3072]{1,0:T(8,128)(2,1)S(1)}, f32[192,3072]{1,0:T(8,128)S(1)}) fusion(bf16[192,1536]{1,0:T(8,128)(2,1)S(1)} %pad_maximum_fusion.4, bf16[3072,1536]{1,0:T(8,128)(2,1)S(1)} %bitcast.123), kind=kOutput, calls=%fused_computation.252 | convolution fusion | flops 1812529152 | bytes 13565952 | tf_op jit(solution)/shard_map/dot_general | solution.py:11
  110.2 5.4 %collective-permute-done.16 = bf16[192,1536]{1,0:T(8,128)(2,1)S(1)} collective-permute-done((bf16[192,1536]{1,0:T(8,128)(2,1)S(1)}, bf16[192,1536]{1,0:T(8,128)(2,1)S(1)}, u32[]{:S(2)}, u32[]{:S(2)}) %collective-permute-start.16) | collective-permute-done | bytes 589856 | tf_op jit(solution)/shard_map/ppermute | solution.py:30
  118.0 6.3 %collective-permute-done.31 = bf16[192,768]{1,0:T(8,128)(2,1)S(1)} collective-permute-done((bf16[192,768]{1,0:T(8,128)(2,1)S(1)}, bf16[192,768]{1,0:T(8,128)(2,1)S(1)}, u32[]{:S(2)}, u32[]{:S(2)}) %collective-permute-start.31) | collective-permute-done | bytes 294944 | tf_op jit(solution)/shard_map/ppermute | solution.py:30
  132.5 4.4 %collective-permute-done.32 = bf16[192,768]{1,0:T(8,128)(2,1)S(1)} collective-permute-done((bf16[192,768]{1,0:T(8,128)(2,1)S(1)}, bf16[192,768]{1,0:T(8,128)(2,1)S(1)}, u32[]{:S(2)}, u32[]{:S(2)}) %collective-permute-start.32) | collective-permute-done | bytes 294944 | tf_op jit(solution)/shard_map/ppermute | solution.py:30
  136.9 6.3 %collective-permute-done.33 = bf16[192,768]{1,0:T(8,128)(2,1)S(1)} collective-permute-done((bf16[192,768]{1,0:T(8,128)(2,1)S(1)}, bf16[192,768]{1,0:T(8,128)(2,1)S(1)}, u32[]{:S(2)}, u32[]{:S(2)}) %collective-permute-start.33) | collective-permute-done | bytes 294944 | tf_op jit(solution)/shard_map/ppermute | solution.py:30
  148.8 8.8 %collective-permute-done.34 = bf16[192,768]{1,0:T(8,128)(2,1)S(1)} collective-permute-done((bf16[192,768]{1,0:T(8,128)(2,1)S(1)}, bf16[192,768]{1,0:T(8,128)(2,1)S(1)}, u32[]{:S(2)}, u32[]{:S(2)}) %collective-permute-start.34) | collective-permute-done | bytes 294944 | tf_op jit(solution)/shard_map/ppermute | solution.py:30
  157.6 6.3 %collective-permute-done.39 = bf16[192,768]{1,0:T(8,128)(2,1)S(1)} collective-permute-done((bf16[192,768]{1,0:T(8,128)(2,1)S(1)}, bf16[192,768]{1,0:T(8,128)(2,1)S(1)}, u32[]{:S(2)}, u32[]{:S(2)}) %collective-permute-start.39) | collective-permute-done | bytes 294944 | tf_op jit(solution)/shard_map/ppermute | solution.py:30
  167.8 3.1 %fusion.4 = f32[768,768]{1,0:T(8,128)S(1)} fusion(bf16[192,1536]{1,0:T(8,128)(2,1)S(1)} %collective-permute-done.6, bf16[192,1536]{1,0:T(8,128)(2,1)S(1)} %copy-done.6, bf16[192,1536]{1,0:T(8,128)(2,1)} %collective-permute-done.4, bf16[192,1536]{1,0:T(8,128)(2,1)S(1)} %copy-done, bf16[192,1536]{1,0:T(8,128)(2,1)S(1)} %get-tuple-element.51, ...), kind=kOutput, calls=%fused_computation.6 | convolution fusion | flops 1830813696 | bytes 7077888 | tf_op jit(solution)/shard_map/dot_general | solution.py:11
  172.3 4.2 %collective-permute-done.40 = bf16[192,768]{1,0:T(8,128)(2,1)S(1)} collective-permute-done((bf16[192,768]{1,0:T(8,128)(2,1)S(1)}, bf16[192,768]{1,0:T(8,128)(2,1)S(1)}, u32[]{:S(2)}, u32[]{:S(2)}) %collective-permute-start.40) | collective-permute-done | bytes 294944 | tf_op jit(solution)/shard_map/ppermute | solution.py:30
  179.6 3.9 %collective-permute-done.36 = bf16[192,768]{1,0:T(8,128)(2,1)S(1)} collective-permute-done((bf16[192,768]{1,0:T(8,128)(2,1)S(1)}, bf16[192,768]{1,0:T(8,128)(2,1)S(1)}, u32[]{:S(2)}, u32[]{:S(2)}) %collective-permute-start.36) | collective-permute-done | bytes 294944 | tf_op jit(solution)/shard_map/ppermute | solution.py:30
  193.3 6.0 %collective-permute-done.47 = bf16[192,768]{1,0:T(8,128)(2,1)S(1)} collective-permute-done((bf16[192,768]{1,0:T(8,128)(2,1)S(1)}, bf16[192,768]{1,0:T(8,128)(2,1)S(1)}, u32[]{:S(2)}, u32[]{:S(2)}) %collective-permute-start.47) | collective-permute-done | bytes 294944 | tf_op jit(solution)/shard_map/ppermute | solution.py:30
  199.3 3.0 %fusion.3 = f32[1536,192]{0,1:T(8,128)} fusion(s32[1536]{0:T(1024)S(1)} %add.501, f32[1536,192]{0,1:T(8,128)S(1)} %copy-done.8, bf16[192,768]{1,0:T(8,128)(2,1)S(1)} %collective-permute-done.47, bf16[192,384]{1,0:T(8,128)(2,1)S(1)} %get-tuple-element.68, bf16[192,384]{1,0:T(8,128)(2,1)S(1)} %get-tuple-element.62), kind=kOutput, calls=%fused_computation.4 | convolution fusion | flops 910983168 | bytes 2955264 | tf_op jit(solution)/shard_map/dot_general | solution.py:11
  205.7 6.2 %collective-permute-done.43 = bf16[192,768]{1,0:T(8,128)(2,1)S(1)} collective-permute-done((bf16[192,768]{1,0:T(8,128)(2,1)S(1)}, bf16[192,768]{1,0:T(8,128)(2,1)S(1)}, u32[]{:S(2)}, u32[]{:S(2)}) %collective-permute-start.43) | collective-permute-done | bytes 294944 | tf_op jit(solution)/shard_map/ppermute | solution.py:30
  213.2 10.6 %collective-permute-done.53 = bf16[192,1536]{1,0:T(8,128)(2,1)S(1)} collective-permute-done((bf16[192,1536]{1,0:T(8,128)(2,1)S(1)}, bf16[192,1536]{1,0:T(8,128)(2,1)S(1)}, u32[]{:S(2)}, u32[]{:S(2)}) %collective-permute-start.53) | collective-permute-done | bytes 589856 | tf_op jit(solution)/shard_map/ppermute | solution.py:30
  (198 shorter events, 83.9 us)
Async XLA Ops:
  1.1 18.8 %collective-permute-start.7 = (bf16[192,1536]{1,0:T(8,128)(2,1)}, bf16[192,1536]{1,0:T(8,128)(2,1)S(1)}, u32[]{:S(2)}, u32[]{:S(2)}) collective-permute-start(bf16[192,1536]{1,0:T(8,128)(2,1)} %bitcast.152), channel_id=1, source_target_pairs={{0,8},{1,9},{2,10},{3,11},{4,12},{5,13},{6,14},{7,15},{8,16},{9,17... | collective-permute-start | bytes 1769480 | tf_op jit(solution)/shard_map/ppermute | solution.py:30
  8.7 22.8 %collective-permute-start.4 = (bf16[192,1536]{1,0:T(8,128)(2,1)S(1)}, bf16[192,1536]{1,0:T(8,128)(2,1)}, u32[]{:S(2)}, u32[]{:S(2)}) collective-permute-start(bf16[192,1536]{1,0:T(8,128)(2,1)S(1)} %copy-done), channel_id=1, source_target_pairs={{0,2},{1,3},{2,0},{3,1},{4,6},{5,7},{6,4},{7,5},{8,10},{9,11},{10,... | collective-permute-start | bytes 1769480 | tf_op jit(solution)/shard_map/ppermute | solution.py:30
  8.8 19.8 %collective-permute-start.5 = (bf16[192,1536]{1,0:T(8,128)(2,1)S(1)}, bf16[192,1536]{1,0:T(8,128)(2,1)S(1)}, u32[]{:S(2)}, u32[]{:S(2)}) collective-permute-start(bf16[192,1536]{1,0:T(8,128)(2,1)S(1)} %copy-done), channel_id=1, source_target_pairs={{0,4},{1,5},{2,6},{3,7},{4,0},{5,1},{6,2},{7,3},{8,12},{9,13},{10,... | collective-permute-start | bytes 1769480 | tf_op jit(solution)/shard_map/ppermute | solution.py:30
  10.2 18.4 %collective-permute-start.2 = (bf16[384,384]{0,1:T(8,128)(2,1)S(1)}, bf16[384,384]{0,1:T(8,128)(2,1)S(1)}, u32[]{:S(2)}, u32[]{:S(2)}) collective-permute-start(bf16[384,384]{0,1:T(8,128)(2,1)S(1)} %fusion.36), channel_id=1, source_target_pairs={{0,1},{1,0},{2,3},{3,2},{4,5},{5,4},{6,7},{7,6},{8,9},{9,8},{10,11... | collective-permute-start | bytes 884744 | tf_op jit(solution)/shard_map/ppermute | solution.py:30
  20.0 17.0 %collective-permute-start.8 = (bf16[192,1536]{1,0:T(8,128)(2,1)S(1)}, bf16[192,1536]{1,0:T(8,128)(2,1)}, u32[]{:S(2)}, u32[]{:S(2)}) collective-permute-start(bf16[192,1536]{1,0:T(8,128)(2,1)S(1)} %collective-permute-done.7), channel_id=1, source_target_pairs={{0,8},{1,9},{2,10},{3,11},{4,12},{5,13},{6,14},{7,15},{8,16},{9,17... | collective-permute-start | bytes 1769480 | tf_op jit(solution)/shard_map/ppermute | solution.py:30
  28.6 15.9 %collective-permute-start.19 = (bf16[192,1536]{1,0:T(8,128)(2,1)S(1)}, bf16[192,1536]{1,0:T(8,128)(2,1)}, u32[]{:S(2)}, u32[]{:S(2)}) collective-permute-start(bf16[192,1536]{1,0:T(8,128)(2,1)S(1)} %bitcast.154), channel_id=1, source_target_pairs={{0,4},{1,5},{2,6},{3,7},{4,0},{5,1},{6,2},{7,3},{8,12},{9,13},{10,... | collective-permute-start | bytes 1769480 | tf_op jit(solution)/shard_map/ppermute | solution.py:30
  31.3 49.3 %collective-permute-start.21 = (bf16[192,1536]{1,0:T(8,128)(2,1)S(1)}, bf16[192,1536]{1,0:T(8,128)(2,1)S(1)}, u32[]{:S(2)}, u32[]{:S(2)}) collective-permute-start(bf16[192,1536]{1,0:T(8,128)(2,1)S(1)} %collective-permute-done.7), channel_id=1, source_target_pairs={{0,2},{1,3},{2,0},{3,1},{4,6},{5,7},{6,4},{7,5},{8,10},{9,11},{10,... | collective-permute-start | bytes 1769480 | tf_op jit(solution)/shard_map/ppermute | solution.py:30
  37.0 25.0 %collective-permute-start.10 = (bf16[192,1536]{1,0:T(8,128)(2,1)}, bf16[192,1536]{1,0:T(8,128)(2,1)S(1)}, u32[]{:S(2)}, u32[]{:S(2)}) collective-permute-start(bf16[192,1536]{1,0:T(8,128)(2,1)} %collective-permute-done.8), channel_id=1, source_target_pairs={{0,8},{1,9},{2,10},{3,11},{4,12},{5,13},{6,14},{7,15},{8,16},{9,17... | collective-permute-start | bytes 1769480 | tf_op jit(solution)/shard_map/ppermute | solution.py:30
  40.0 21.6 %collective-permute-start.9 = (bf16[192,768]{1,0:T(8,128)(2,1)S(1)}, bf16[192,768]{1,0:T(8,128)(2,1)S(1)}, u32[]{:S(2)}, u32[]{:S(2)}) collective-permute-start(bf16[192,768]{1,0:T(8,128)(2,1)S(1)} %convolution_convert_fusion.2), channel_id=1, source_target_pairs={{0,8},{1,9},{2,10},{3,11},{4,12},{5,13},{6,14},{7,15},{8,16},{9,17... | collective-permute-start | bytes 884744 | tf_op jit(solution)/shard_map/ppermute | solution.py:30
  41.6 24.2 %collective-permute-start.13 = (bf16[192,768]{1,0:T(8,128)(2,1)S(1)}, bf16[192,768]{1,0:T(8,128)(2,1)S(1)}, u32[]{:S(2)}, u32[]{:S(2)}) collective-permute-start(bf16[192,768]{1,0:T(8,128)(2,1)S(1)} %convolution_convert_fusion.1), channel_id=1, source_target_pairs={{0,8},{1,9},{2,10},{3,11},{4,12},{5,13},{6,14},{7,15},{8,16},{9,17... | collective-permute-start | bytes 884744 | tf_op jit(solution)/shard_map/ppermute | solution.py:30
  44.5 29.6 %collective-permute-start.22 = (bf16[192,1536]{1,0:T(8,128)(2,1)S(1)}, bf16[192,1536]{1,0:T(8,128)(2,1)S(1)}, u32[]{:S(2)}, u32[]{:S(2)}) collective-permute-start(bf16[192,1536]{1,0:T(8,128)(2,1)S(1)} %collective-permute-done.7), channel_id=1, source_target_pairs={{0,4},{1,5},{2,6},{3,7},{4,0},{5,1},{6,2},{7,3},{8,12},{9,13},{10,... | collective-permute-start | bytes 1769480 | tf_op jit(solution)/shard_map/ppermute | solution.py:30
  61.5 18.4 %collective-permute-start.20 = (bf16[192,1536]{1,0:T(8,128)(2,1)}, bf16[192,1536]{1,0:T(8,128)(2,1)S(1)}, u32[]{:S(2)}, u32[]{:S(2)}) collective-permute-start(bf16[192,1536]{1,0:T(8,128)(2,1)} %collective-permute-done.19), channel_id=1, source_target_pairs={{0,2},{1,3},{2,0},{3,1},{4,6},{5,7},{6,4},{7,5},{8,10},{9,11},{10,... | collective-permute-start | bytes 1769480 | tf_op jit(solution)/shard_map/ppermute | solution.py:30
  74.0 16.4 %collective-permute-start.25 = (bf16[192,1536]{1,0:T(8,128)(2,1)}, bf16[192,1536]{1,0:T(8,128)(2,1)S(1)}, u32[]{:S(2)}, u32[]{:S(2)}) collective-permute-start(bf16[192,1536]{1,0:T(8,128)(2,1)} %collective-permute-done.8), channel_id=1, source_target_pairs={{0,4},{1,5},{2,6},{3,7},{4,0},{5,1},{6,2},{7,3},{8,12},{9,13},{10,... | collective-permute-start | bytes 1769480 | tf_op jit(solution)/shard_map/ppermute | solution.py:30
  80.0 22.8 %collective-permute-start.27 = (bf16[192,1536]{1,0:T(8,128)(2,1)S(1)}, bf16[192,1536]{1,0:T(8,128)(2,1)S(1)}, u32[]{:S(2)}, u32[]{:S(2)}) collective-permute-start(bf16[192,1536]{1,0:T(8,128)(2,1)S(1)} %collective-permute-done.10), channel_id=1, source_target_pairs={{0,2},{1,3},{2,0},{3,1},{4,6},{5,7},{6,4},{7,5},{8,10},{9,11},{10,... | collective-permute-start | bytes 1769480 | tf_op jit(solution)/shard_map/ppermute | solution.py:30
  80.7 22.0 %collective-permute-start.28 = (bf16[192,1536]{1,0:T(8,128)(2,1)S(1)}, bf16[192,1536]{1,0:T(8,128)(2,1)S(1)}, u32[]{:S(2)}, u32[]{:S(2)}) collective-permute-start(bf16[192,1536]{1,0:T(8,128)(2,1)S(1)} %collective-permute-done.10), channel_id=1, source_target_pairs={{0,4},{1,5},{2,6},{3,7},{4,0},{5,1},{6,2},{7,3},{8,12},{9,13},{10,... | collective-permute-start | bytes 1769480 | tf_op jit(solution)/shard_map/ppermute | solution.py:30
  99.5 16.1 %collective-permute-start.16 = (bf16[192,1536]{1,0:T(8,128)(2,1)S(1)}, bf16[192,1536]{1,0:T(8,128)(2,1)S(1)}, u32[]{:S(2)}, u32[]{:S(2)}) collective-permute-start(bf16[192,1536]{1,0:T(8,128)(2,1)S(1)} %copy-done), channel_id=1, source_target_pairs={{0,8},{1,9},{2,10},{3,11},{4,12},{5,13},{6,14},{7,15},{8,16},{9,17... | collective-permute-start | bytes 1769480 | tf_op jit(solution)/shard_map/ppermute | solution.py:30
  126.6 16.6 %collective-permute-start.33 = (bf16[192,768]{1,0:T(8,128)(2,1)S(1)}, bf16[192,768]{1,0:T(8,128)(2,1)S(1)}, u32[]{:S(2)}, u32[]{:S(2)}) collective-permute-start(bf16[192,768]{1,0:T(8,128)(2,1)S(1)} %get-tuple-element.47), channel_id=1, source_target_pairs={{0,1},{1,0},{2,3},{3,2},{4,5},{5,4},{6,7},{7,6},{8,9},{9,8},{10,11... | collective-permute-start | bytes 884744 | tf_op jit(solution)/shard_map/ppermute | solution.py:30
  131.9 16.8 %collective-permute-start.50 = (bf16[192,768]{1,0:T(8,128)(2,1)S(1)}, bf16[192,768]{1,0:T(8,128)(2,1)S(1)}, u32[]{:S(2)}, u32[]{:S(2)}) collective-permute-start(bf16[192,768]{1,0:T(8,128)(2,1)S(1)} %constant_dynamic-slice_fusion.1), channel_id=1, source_target_pairs={{0,1},{1,0},{2,3},{3,2},{4,5},{5,4},{6,7},{7,6},{8,9},{9,8},{10,11... | collective-permute-start | bytes 884744 | tf_op jit(solution)/shard_map/ppermute | solution.py:30
  132.5 32.5 %collective-permute-start.44 = (bf16[192,1536]{1,0:T(8,128)(2,1)S(1)}, bf16[192,1536]{1,0:T(8,128)(2,1)S(1)}, u32[]{:S(2)}, u32[]{:S(2)}) collective-permute-start(bf16[192,1536]{1,0:T(8,128)(2,1)S(1)} %collective-permute-done.17), channel_id=1, source_target_pairs={{0,8},{1,9},{2,10},{3,11},{4,12},{5,13},{6,14},{7,15},{8,16},{9,17... | collective-permute-start | bytes 1769480 | tf_op jit(solution)/shard_map/ppermute | solution.py:30
  145.9 18.1 %collective-permute-start.39 = (bf16[192,768]{1,0:T(8,128)(2,1)S(1)}, bf16[192,768]{1,0:T(8,128)(2,1)S(1)}, u32[]{:S(2)}, u32[]{:S(2)}) collective-permute-start(bf16[192,768]{1,0:T(8,128)(2,1)S(1)} %get-tuple-element.67), channel_id=1, source_target_pairs={{0,8},{1,9},{2,10},{3,11},{4,12},{5,13},{6,14},{7,15},{8,16},{9,17... | collective-permute-start | bytes 884744 | tf_op jit(solution)/shard_map/ppermute | solution.py:30
  171.0 16.4 %collective-permute-start.45 = (bf16[768,384]{1,0:T(8,128)(2,1)S(1)}, bf16[768,384]{1,0:T(8,128)(2,1)S(1)}, u32[]{:S(2)}, u32[]{:S(2)}) collective-permute-start(bf16[768,384]{1,0:T(8,128)(2,1)S(1)} %dynamic-slice_convert_fusion.2), channel_id=1, source_target_pairs={{0,1},{1,0},{2,3},{3,2},{4,5},{5,4},{6,7},{7,6},{8,9},{9,8},{10,11... | collective-permute-start | bytes 1769480 | tf_op jit(solution)/shard_map/ppermute | solution.py:30
  179.5 22.8 %collective-permute-start.52 = (bf16[384,1536]{1,0:T(8,128)(2,1)S(1)}, bf16[384,1536]{1,0:T(8,128)(2,1)S(1)}, u32[]{:S(2)}, u32[]{:S(2)}) collective-permute-start(bf16[384,1536]{1,0:T(8,128)(2,1)S(1)} %pad_maximum_fusion.3), channel_id=1, source_target_pairs={{0,2},{1,3},{2,0},{3,1},{4,6},{5,7},{6,4},{7,5},{8,10},{9,11},{10,... | collective-permute-start | bytes 3538952 | tf_op jit(solution)/shard_map/ppermute | solution.py:30
  191.8 20.1 %collective-permute-start.43 = (bf16[192,768]{1,0:T(8,128)(2,1)S(1)}, bf16[192,768]{1,0:T(8,128)(2,1)S(1)}, u32[]{:S(2)}, u32[]{:S(2)}) collective-permute-start(bf16[192,768]{1,0:T(8,128)(2,1)S(1)} %fusion.72), channel_id=1, source_target_pairs={{0,4},{1,5},{2,6},{3,7},{4,0},{5,1},{6,2},{7,3},{8,12},{9,13},{10,... | collective-permute-start | bytes 884744 | tf_op jit(solution)/shard_map/ppermute | solution.py:30
  202.8 21.0 %collective-permute-start.53 = (bf16[192,1536]{1,0:T(8,128)(2,1)S(1)}, bf16[192,1536]{1,0:T(8,128)(2,1)S(1)}, u32[]{:S(2)}, u32[]{:S(2)}) collective-permute-start(bf16[192,1536]{1,0:T(8,128)(2,1)S(1)} %fusion.37), channel_id=1, source_target_pairs={{0,4},{1,5},{2,6},{3,7},{4,0},{5,1},{6,2},{7,3},{8,12},{9,13},{10,... | collective-permute-start | bytes 1769480 | tf_op jit(solution)/shard_map/ppermute | solution.py:30
  (39 other events, 398.9 us)

commit v4 on v3

--- a/solution.py
+++ b/solution.py
@@ -34,11 +34,14 @@
     up = sender(lambda z, y, c, x: ((z + 1) % A, y, c, x))
     along_x = [sender(lambda z, y, c, x, s=s: (z, y, c, (x + s) % X)) for s in range(X)]
 
-    def plane_scatter(blocks):
+    def core_sum(blocks):
         got = flip_c(jnp.concatenate([blocks[1], blocks[3]]).astype(BF16)).astype(F32)
         height = blocks[0].shape[0]
-        mine, other = blocks[0] + got[:height], blocks[2] + got[height:]
-        return mine + flip_y(other.astype(BF16)).astype(F32)
+        return blocks[0] + got[:height], (blocks[2] + got[height:]).astype(BF16)
+
+    def plane_scatter(blocks):
+        mine, other = core_sum(blocks)
+        return mine + flip_y(other).astype(F32)
 
     def on_device(grad, left_basis, right_basis, first, second, left_factor, right_factor):
         b, width = grad.shape
@@ -122,7 +125,6 @@
         for s in range(X - 1, 0, -1):
             direction += [along_x[s](piece) for piece in direction[:per]]
         half = dot(jnp.concatenate(direction, axis=1), right, 1, 0).astype(BF16)
-        late, half = tie(grads[A - 2], half)
         halves = [half[:, lo:hi] for lo, hi in cuts]
 
         have = jnp.concatenate(grads)
@@ -138,7 +140,7 @@
         cols = jnp.concatenate(cols)
 
         term = dot(cols, have, 0, 0).reshape(4, span // 4, width)
-        right_sum = plane_scatter([at(term, (row % 4) ^ k) for k in range(4)])
+        right_sum, right_other = core_sum([at(term, (row % 4) ^ k) for k in range(4)])
 
         grad_rows = jnp.concatenate([grad, grad_c, grad_y, grad_yc])
         stacked = jnp.stack(grads)
@@ -148,16 +150,22 @@
         for s in range(1, X):
             piece = lax.dynamic_slice_in_dim(term, (x + s) % X * per * b, per * b, 1)
             left_sum += along_x[s](piece.astype(BF16)).astype(F32)
-        own, core, over, cross = jnp.split(left_sum.astype(BF16), 4)
-        got = flip_c(jnp.concatenate([core, cross]))
-        over_pair = flip_y(jnp.concatenate([over, got[b:]], axis=1))
-        joined = jnp.concatenate([own, got[:b], over_pair], axis=1)
         update = [dot(left_at[0], half, 0, 0) for half in halves]
         for r in range(1, A):
             halves = [up(half) for half in halves]
+            if r == A - 2:
+                halves[1], right_other = tie(halves[1], right_other)
+            if r == A - 2:
+                halves[1], left_sum = tie(halves[1], left_sum)
+                own, core, over, cross = jnp.split(left_sum.astype(BF16), 4)
+                got = flip_c(jnp.concatenate([core, cross]))
+            if r == A - 1:
+                over_pair = flip_y(jnp.concatenate([over, got[b:]], axis=1))
+                right_sum += flip_y(right_other).astype(F32)
             update = [total + dot(left_at[r], half, 0, 0) for total, half in zip(update, halves)]
         update = jnp.concatenate([plane_scatter(jnp.split(u, 4)) for u in update], axis=1)
 
+        joined = jnp.concatenate([own, got[:b], over_pair], axis=1)
         k, p, i = jnp.arange(4)[:, None, None], jnp.arange(per)[:, None], jnp.arange(b)
         goes = (p * wide + (k ^ (row % 4)) * b + i).reshape(-1)
         order = (goes[:, None] == jnp.arange(width)[None, :]).astype(BF16)

time: 226 us -> 223 us (0.987)
  waiting for transfers between devices: 143 us -> 138 us
    ppermute x54, waiting for transfers between devices: 143 us -> 138 us  [sender(): return lambda value: lax.ppermute(value, ('row', 'col'), pairs)]
  transfers between devices with their start and end apart: 54 -> 54, of which waited for: 31 -> 30; matrix products, arithmetic and copies ran while one was open for 19% -> 19% of each run, Pallas kernels for 0% -> 0%
where the time goes in v4:
time: 223 us
  waiting for transfers between devices  138 us (62%)
  starting transfers between devices  36.9 us (17%)
  matrix products  23.4 us (10%)
  local copies, waits for them, and re-layouts  14.8 us (7%)
  other arithmetic  8.04 us (4%)
    ppermute x54, waiting for transfers between devices, sender(): return lambda value: lax.ppermute(value, ('row', 'col'), pairs)  138 us
    ppermute x54, starting transfers between devices, sender(): return lambda value: lax.ppermute(value, ('row', 'col'), pairs)  36.9 us
    dot_general x23, matrix products, dot(): lax.dot_general(left, right, (((left_dim,), (right_dim,)), ((), ())), pre...  23.4 us
    unnamed x22, local copies, waits for them, and re-layouts  7.45 us
    dynamic_update_slice x16, local copies, waits for them, and re-layouts, on_device(): right = lax.dynamic_update_slice(right, piece[None, None, None], place)  5.01 us
  transfers between devices with their start and end apart: 54, of which 30 were waited for; matrix products, arithmetic and copies ran while one was open for 19% of the time, Pallas kernels for 0%

profile of v4, /device:TPU:0, one launch (start us, length us, event | category | flops | bytes accessed | tf_op | source)
XLA Modules:
  0.0 222.8 jit_solution(14961237085489573288)
XLA Ops:
  11.7 8.2 %collective-permute-done.7 = bf16[192,1536]{1,0:T(8,128)(2,1)S(1)} collective-permute-done((bf16[192,1536]{1,0:T(8,128)(2,1)}, bf16[192,1536]{1,0:T(8,128)(2,1)S(1)}, u32[]{:S(2)}, u32[]{:S(2)}) %collective-permute-start.7) | collective-permute-done | bytes 589856 | tf_op jit(solution)/shard_map/ppermute | solution.py:30
  22.4 6.2 %collective-permute-done.5 = bf16[192,1536]{1,0:T(8,128)(2,1)S(1)} collective-permute-done((bf16[192,1536]{1,0:T(8,128)(2,1)S(1)}, bf16[192,1536]{1,0:T(8,128)(2,1)S(1)}, u32[]{:S(2)}, u32[]{:S(2)}) %collective-permute-start.5) | collective-permute-done | bytes 589856 | tf_op jit(solution)/shard_map/ppermute | solution.py:30
  46.0 15.5 %collective-permute-done.9 = bf16[192,768]{1,0:T(8,128)(2,1)S(1)} collective-permute-done((bf16[192,768]{1,0:T(8,128)(2,1)S(1)}, bf16[192,768]{1,0:T(8,128)(2,1)S(1)}, u32[]{:S(2)}, u32[]{:S(2)}) %collective-permute-start.9) | collective-permute-done | bytes 294944 | tf_op jit(solution)/shard_map/ppermute | solution.py:30
  62.0 3.9 %collective-permute-done.13 = bf16[192,768]{1,0:T(8,128)(2,1)S(1)} collective-permute-done((bf16[192,768]{1,0:T(8,128)(2,1)S(1)}, bf16[192,768]{1,0:T(8,128)(2,1)S(1)}, u32[]{:S(2)}, u32[]{:S(2)}) %collective-permute-start.13) | collective-permute-done | bytes 294944 | tf_op jit(solution)/shard_map/ppermute | solution.py:30
  68.8 9.3 %collective-permute-done.14 = bf16[192,768]{1,0:T(8,128)(2,1)S(1)} collective-permute-done((bf16[192,768]{1,0:T(8,128)(2,1)S(1)}, bf16[192,768]{1,0:T(8,128)(2,1)S(1)}, u32[]{:S(2)}, u32[]{:S(2)}) %collective-permute-start.14) | collective-permute-done | bytes 294944 | tf_op jit(solution)/shard_map/ppermute | solution.py:30
  86.5 8.4 %collective-permute-done.23 = bf16[192,1536]{1,0:T(8,128)(2,1)S(1)} collective-permute-done((bf16[192,1536]{1,0:T(8,128)(2,1)}, bf16[192,1536]{1,0:T(8,128)(2,1)S(1)}, u32[]{:S(2)}, u32[]{:S(2)}) %collective-permute-start.23) | collective-permute-done | bytes 589856 | tf_op jit(solution)/shard_map/ppermute | solution.py:30
  97.0 4.7 %collective-permute-done.12 = bf16[192,768]{1,0:T(8,128)(2,1)S(1)} collective-permute-done((bf16[192,768]{1,0:T(8,128)(2,1)S(1)}, bf16[192,768]{1,0:T(8,128)(2,1)S(1)}, u32[]{:S(2)}, u32[]{:S(2)}) %collective-permute-start.12) | collective-permute-done | bytes 294944 | tf_op jit(solution)/shard_map/ppermute | solution.py:30
  103.9 3.2 %collective-permute-done.26 = bf16[192,1536]{1,0:T(8,128)(2,1)S(1)} collective-permute-done((bf16[192,1536]{1,0:T(8,128)(2,1)S(1)}, bf16[192,1536]{1,0:T(8,128)(2,1)S(1)}, u32[]{:S(2)}, u32[]{:S(2)}) %collective-permute-start.26) | collective-permute-done | bytes 589856 | tf_op jit(solution)/shard_map/ppermute | solution.py:30
  109.2 3.2 %fusion.161 = (bf16[192,3072]{1,0:T(8,128)(2,1)S(1)}, f32[192,3072]{1,0:T(8,128)S(1)}) fusion(bf16[192,1536]{1,0:T(8,128)(2,1)S(1)} %pad_maximum_fusion.4, bf16[3072,1536]{1,0:T(8,128)(2,1)S(1)} %bitcast.123), kind=kOutput, calls=%fused_computation.252 | convolution fusion | flops 1812529152 | bytes 13565952 | tf_op jit(solution)/shard_map/dot_general | solution.py:11
  114.6 3.6 %collective-permute-done.40 = bf16[192,1536]{1,0:T(8,128)(2,1)S(1)} collective-permute-done((bf16[192,1536]{1,0:T(8,128)(2,1)S(1)}, bf16[192,1536]{1,0:T(8,128)(2,1)S(1)}, u32[]{:S(2)}, u32[]{:S(2)}) %collective-permute-start.40) | collective-permute-done | bytes 589856 | tf_op jit(solution)/shard_map/ppermute | solution.py:30
  122.4 6.3 %collective-permute-done.29 = bf16[192,768]{1,0:T(8,128)(2,1)S(1)} collective-permute-done((bf16[192,768]{1,0:T(8,128)(2,1)S(1)}, bf16[192,768]{1,0:T(8,128)(2,1)S(1)}, u32[]{:S(2)}, u32[]{:S(2)}) %collective-permute-start.29) | collective-permute-done | bytes 294944 | tf_op jit(solution)/shard_map/ppermute | solution.py:30
  136.7 4.6 %collective-permute-done.31 = bf16[192,768]{1,0:T(8,128)(2,1)S(1)} collective-permute-done((bf16[192,768]{1,0:T(8,128)(2,1)S(1)}, bf16[192,768]{1,0:T(8,128)(2,1)S(1)}, u32[]{:S(2)}, u32[]{:S(2)}) %collective-permute-start.31) | collective-permute-done | bytes 294944 | tf_op jit(solution)/shard_map/ppermute | solution.py:30
  141.3 6.3 %collective-permute-done.30 = bf16[192,768]{1,0:T(8,128)(2,1)S(1)} collective-permute-done((bf16[192,768]{1,0:T(8,128)(2,1)S(1)}, bf16[192,768]{1,0:T(8,128)(2,1)S(1)}, u32[]{:S(2)}, u32[]{:S(2)}) %collective-permute-start.30) | collective-permute-done | bytes 294944 | tf_op jit(solution)/shard_map/ppermute | solution.py:30
  150.4 2.8 %collective-permute-done.43 = bf16[192,768]{1,0:T(8,128)(2,1)S(1)} collective-permute-done((bf16[192,768]{1,0:T(8,128)(2,1)S(1)}, bf16[192,768]{1,0:T(8,128)(2,1)S(1)}, u32[]{:S(2)}, u32[]{:S(2)}) %collective-permute-start.43) | collective-permute-done | bytes 294944 | tf_op jit(solution)/shard_map/ppermute | solution.py:30
  153.3 8.2 %collective-permute-done.32 = bf16[192,768]{1,0:T(8,128)(2,1)S(1)} collective-permute-done((bf16[192,768]{1,0:T(8,128)(2,1)S(1)}, bf16[192,768]{1,0:T(8,128)(2,1)S(1)}, u32[]{:S(2)}, u32[]{:S(2)}) %collective-permute-start.32) | collective-permute-done | bytes 294944 | tf_op jit(solution)/shard_map/ppermute | solution.py:30
  165.0 3.1 %fusion.12 = f32[768,768]{1,0:T(8,128)S(1)} fusion(bf16[192,1536]{1,0:T(8,128)(2,1)S(1)} %collective-permute-done.6, bf16[192,1536]{1,0:T(8,128)(2,1)S(1)} %copy-done.6, bf16[192,1536]{1,0:T(8,128)(2,1)} %collective-permute-done.4, bf16[192,1536]{1,0:T(8,128)(2,1)S(1)} %copy-done, bf16[192,1536]{1,0:T(8,128)(2,1)S(1)} %get-tuple-element.57, ...), kind=kOutput, calls=%fused_computation.14 | convolution fusion | flops 1830813696 | bytes 7077888 | tf_op jit(solution)/shard_map/dot_general | solution.py:11
  168.8 2.8 %collective-permute-done.33 = bf16[192,768]{1,0:T(8,128)(2,1)S(1)} collective-permute-done((bf16[192,768]{1,0:T(8,128)(2,1)S(1)}, bf16[192,768]{1,0:T(8,128)(2,1)S(1)}, u32[]{:S(2)}, u32[]{:S(2)}) %collective-permute-start.33) | collective-permute-done | bytes 294944 | tf_op jit(solution)/shard_map/ppermute | solution.py:30
  174.3 5.8 %collective-permute-done.34 = bf16[192,768]{1,0:T(8,128)(2,1)S(1)} collective-permute-done((bf16[192,768]{1,0:T(8,128)(2,1)S(1)}, bf16[192,768]{1,0:T(8,128)(2,1)S(1)}, u32[]{:S(2)}, u32[]{:S(2)}) %collective-permute-start.34) | collective-permute-done | bytes 294944 | tf_op jit(solution)/shard_map/ppermute | solution.py:30
  185.0 7.1 %collective-permute-done.36 = bf16[192,768]{1,0:T(8,128)(2,1)S(1)} collective-permute-done((bf16[192,768]{1,0:T(8,128)(2,1)S(1)}, bf16[192,768]{1,0:T(8,128)(2,1)S(1)}, u32[]{:S(2)}, u32[]{:S(2)}) %collective-permute-start.36) | collective-permute-done | bytes 294944 | tf_op jit(solution)/shard_map/ppermute | solution.py:30
  195.0 7.9 %collective-permute-done.48 = bf16[192,768]{1,0:T(8,128)(2,1)S(1)} collective-permute-done((bf16[192,768]{1,0:T(8,128)(2,1)S(1)}, bf16[192,768]{1,0:T(8,128)(2,1)S(1)}, u32[]{:S(2)}, u32[]{:S(2)}) %collective-permute-start.48) | collective-permute-done | bytes 294944 | tf_op jit(solution)/shard_map/ppermute | solution.py:30
  205.1 4.3 %collective-permute-done.53 = bf16[192,1536]{1,0:T(8,128)(2,1)S(1)} collective-permute-done((bf16[192,1536]{1,0:T(8,128)(2,1)S(1)}, bf16[192,1536]{1,0:T(8,128)(2,1)S(1)}, u32[]{:S(2)}, u32[]{:S(2)}) %collective-permute-start.53) | collective-permute-done | bytes 589856 | tf_op jit(solution)/shard_map/ppermute | solution.py:30
  212.3 3.4 %collective-permute-done.52 = bf16[192,768]{1,0:T(8,128)(2,1)S(1)} collective-permute-done((bf16[192,768]{1,0:T(8,128)(2,1)S(1)}, bf16[192,768]{1,0:T(8,128)(2,1)S(1)}, u32[]{:S(2)}, u32[]{:S(2)}) %collective-permute-start.52) | collective-permute-done | bytes 294944 | tf_op jit(solution)/shard_map/ppermute | solution.py:30
  215.7 3.0 %fusion.3 = f32[1536,192]{0,1:T(8,128)} fusion(s32[1536]{0:T(1024)S(1)} %add.514, f32[1536,192]{0,1:T(8,128)S(1)} %copy-done.8, bf16[192,768]{1,0:T(8,128)(2,1)S(1)} %collective-permute-done.52, bf16[192,384]{1,0:T(8,128)(2,1)S(1)} %get-tuple-element.74, bf16[192,384]{1,0:T(8,128)(2,1)S(1)} %get-tuple-element.68), kind=kOutput, calls=%fused_computation.4 | convolution fusion | flops 910983168 | bytes 2955264 | tf_op jit(solution)/shard_map/dot_general | solution.py:11
  218.7 2.8 %collective-permute-done.50 = bf16[192,768]{1,0:T(8,128)(2,1)S(1)} collective-permute-done((bf16[192,768]{1,0:T(8,128)(2,1)S(1)}, bf16[192,768]{1,0:T(8,128)(2,1)S(1)}, u32[]{:S(2)}, u32[]{:S(2)}) %collective-permute-start.50) | collective-permute-done | bytes 294944 | tf_op jit(solution)/shard_map/ppermute | solution.py:30
  (198 shorter events, 86.2 us)
Async XLA Ops:
  1.1 18.8 %collective-permute-start.7 = (bf16[192,1536]{1,0:T(8,128)(2,1)}, bf16[192,1536]{1,0:T(8,128)(2,1)S(1)}, u32[]{:S(2)}, u32[]{:S(2)}) collective-permute-start(bf16[192,1536]{1,0:T(8,128)(2,1)} %bitcast.152), channel_id=1, source_target_pairs={{0,8},{1,9},{2,10},{3,11},{4,12},{5,13},{6,14},{7,15},{8,16},{9,17... | collective-permute-start | bytes 1769480 | tf_op jit(solution)/shard_map/ppermute | solution.py:30
  8.7 19.9 %collective-permute-start.5 = (bf16[192,1536]{1,0:T(8,128)(2,1)S(1)}, bf16[192,1536]{1,0:T(8,128)(2,1)S(1)}, u32[]{:S(2)}, u32[]{:S(2)}) collective-permute-start(bf16[192,1536]{1,0:T(8,128)(2,1)S(1)} %copy-done), channel_id=1, source_target_pairs={{0,4},{1,5},{2,6},{3,7},{4,0},{5,1},{6,2},{7,3},{8,12},{9,13},{10,... | collective-permute-start | bytes 1769480 | tf_op jit(solution)/shard_map/ppermute | solution.py:30
  9.3 22.2 %collective-permute-start.4 = (bf16[192,1536]{1,0:T(8,128)(2,1)S(1)}, bf16[192,1536]{1,0:T(8,128)(2,1)}, u32[]{:S(2)}, u32[]{:S(2)}) collective-permute-start(bf16[192,1536]{1,0:T(8,128)(2,1)S(1)} %copy-done), channel_id=1, source_target_pairs={{0,2},{1,3},{2,0},{3,1},{4,6},{5,7},{6,4},{7,5},{8,10},{9,11},{10,... | collective-permute-start | bytes 1769480 | tf_op jit(solution)/shard_map/ppermute | solution.py:30
  10.2 18.5 %collective-permute-start.2 = (bf16[384,384]{0,1:T(8,128)(2,1)S(1)}, bf16[384,384]{0,1:T(8,128)(2,1)S(1)}, u32[]{:S(2)}, u32[]{:S(2)}) collective-permute-start(bf16[384,384]{0,1:T(8,128)(2,1)S(1)} %fusion.36), channel_id=1, source_target_pairs={{0,1},{1,0},{2,3},{3,2},{4,5},{5,4},{6,7},{7,6},{8,9},{9,8},{10,11... | collective-permute-start | bytes 884744 | tf_op jit(solution)/shard_map/ppermute | solution.py:30
  20.0 17.0 %collective-permute-start.8 = (bf16[192,1536]{1,0:T(8,128)(2,1)S(1)}, bf16[192,1536]{1,0:T(8,128)(2,1)}, u32[]{:S(2)}, u32[]{:S(2)}) collective-permute-start(bf16[192,1536]{1,0:T(8,128)(2,1)S(1)} %collective-permute-done.7), channel_id=1, source_target_pairs={{0,8},{1,9},{2,10},{3,11},{4,12},{5,13},{6,14},{7,15},{8,16},{9,17... | collective-permute-start | bytes 1769480 | tf_op jit(solution)/shard_map/ppermute | solution.py:30
  28.6 15.9 %collective-permute-start.17 = (bf16[192,1536]{1,0:T(8,128)(2,1)S(1)}, bf16[192,1536]{1,0:T(8,128)(2,1)}, u32[]{:S(2)}, u32[]{:S(2)}) collective-permute-start(bf16[192,1536]{1,0:T(8,128)(2,1)S(1)} %bitcast.154), channel_id=1, source_target_pairs={{0,4},{1,5},{2,6},{3,7},{4,0},{5,1},{6,2},{7,3},{8,12},{9,13},{10,... | collective-permute-start | bytes 1769480 | tf_op jit(solution)/shard_map/ppermute | solution.py:30
  30.2 52.3 %collective-permute-start.19 = (bf16[192,1536]{1,0:T(8,128)(2,1)S(1)}, bf16[192,1536]{1,0:T(8,128)(2,1)}, u32[]{:S(2)}, u32[]{:S(2)}) collective-permute-start(bf16[192,1536]{1,0:T(8,128)(2,1)S(1)} %collective-permute-done.7), channel_id=1, source_target_pairs={{0,2},{1,3},{2,0},{3,1},{4,6},{5,7},{6,4},{7,5},{8,10},{9,11},{10,... | collective-permute-start | bytes 1769480 | tf_op jit(solution)/shard_map/ppermute | solution.py:30
  37.0 25.0 %collective-permute-start.10 = (bf16[192,1536]{1,0:T(8,128)(2,1)}, bf16[192,1536]{1,0:T(8,128)(2,1)S(1)}, u32[]{:S(2)}, u32[]{:S(2)}) collective-permute-start(bf16[192,1536]{1,0:T(8,128)(2,1)} %collective-permute-done.8), channel_id=1, source_target_pairs={{0,8},{1,9},{2,10},{3,11},{4,12},{5,13},{6,14},{7,15},{8,16},{9,17... | collective-permute-start | bytes 1769480 | tf_op jit(solution)/shard_map/ppermute | solution.py:30
  40.0 21.6 %collective-permute-start.9 = (bf16[192,768]{1,0:T(8,128)(2,1)S(1)}, bf16[192,768]{1,0:T(8,128)(2,1)S(1)}, u32[]{:S(2)}, u32[]{:S(2)}) collective-permute-start(bf16[192,768]{1,0:T(8,128)(2,1)S(1)} %convolution_convert_fusion.2), channel_id=1, source_target_pairs={{0,8},{1,9},{2,10},{3,11},{4,12},{5,13},{6,14},{7,15},{8,16},{9,17... | collective-permute-start | bytes 884744 | tf_op jit(solution)/shard_map/ppermute | solution.py:30
  41.6 24.2 %collective-permute-start.13 = (bf16[192,768]{1,0:T(8,128)(2,1)S(1)}, bf16[192,768]{1,0:T(8,128)(2,1)S(1)}, u32[]{:S(2)}, u32[]{:S(2)}) collective-permute-start(bf16[192,768]{1,0:T(8,128)(2,1)S(1)} %convolution_convert_fusion.1), channel_id=1, source_target_pairs={{0,8},{1,9},{2,10},{3,11},{4,12},{5,13},{6,14},{7,15},{8,16},{9,17... | collective-permute-start | bytes 884744 | tf_op jit(solution)/shard_map/ppermute | solution.py:30
  44.5 34.0 %collective-permute-start.20 = (bf16[192,1536]{1,0:T(8,128)(2,1)S(1)}, bf16[192,1536]{1,0:T(8,128)(2,1)S(1)}, u32[]{:S(2)}, u32[]{:S(2)}) collective-permute-start(bf16[192,1536]{1,0:T(8,128)(2,1)S(1)} %collective-permute-done.7), channel_id=1, source_target_pairs={{0,4},{1,5},{2,6},{3,7},{4,0},{5,1},{6,2},{7,3},{8,12},{9,13},{10,... | collective-permute-start | bytes 1769480 | tf_op jit(solution)/shard_map/ppermute | solution.py:30
  61.5 20.3 %collective-permute-start.18 = (bf16[192,1536]{1,0:T(8,128)(2,1)}, bf16[192,1536]{1,0:T(8,128)(2,1)S(1)}, u32[]{:S(2)}, u32[]{:S(2)}) collective-permute-start(bf16[192,1536]{1,0:T(8,128)(2,1)} %collective-permute-done.17), channel_id=1, source_target_pairs={{0,2},{1,3},{2,0},{3,1},{4,6},{5,7},{6,4},{7,5},{8,10},{9,11},{10,... | collective-permute-start | bytes 1769480 | tf_op jit(solution)/shard_map/ppermute | solution.py:30
  78.5 16.4 %collective-permute-start.23 = (bf16[192,1536]{1,0:T(8,128)(2,1)}, bf16[192,1536]{1,0:T(8,128)(2,1)S(1)}, u32[]{:S(2)}, u32[]{:S(2)}) collective-permute-start(bf16[192,1536]{1,0:T(8,128)(2,1)} %collective-permute-done.8), channel_id=1, source_target_pairs={{0,4},{1,5},{2,6},{3,7},{4,0},{5,1},{6,2},{7,3},{8,12},{9,13},{10,... | collective-permute-start | bytes 1769480 | tf_op jit(solution)/shard_map/ppermute | solution.py:30
  81.8 25.4 %collective-permute-start.25 = (bf16[192,1536]{1,0:T(8,128)(2,1)S(1)}, bf16[192,1536]{1,0:T(8,128)(2,1)S(1)}, u32[]{:S(2)}, u32[]{:S(2)}) collective-permute-start(bf16[192,1536]{1,0:T(8,128)(2,1)S(1)} %collective-permute-done.10), channel_id=1, source_target_pairs={{0,2},{1,3},{2,0},{3,1},{4,6},{5,7},{6,4},{7,5},{8,10},{9,11},{10,... | collective-permute-start | bytes 1769480 | tf_op jit(solution)/shard_map/ppermute | solution.py:30
  82.5 24.6 %collective-permute-start.26 = (bf16[192,1536]{1,0:T(8,128)(2,1)S(1)}, bf16[192,1536]{1,0:T(8,128)(2,1)S(1)}, u32[]{:S(2)}, u32[]{:S(2)}) collective-permute-start(bf16[192,1536]{1,0:T(8,128)(2,1)S(1)} %collective-permute-done.10), channel_id=1, source_target_pairs={{0,4},{1,5},{2,6},{3,7},{4,0},{5,1},{6,2},{7,3},{8,12},{9,13},{10,... | collective-permute-start | bytes 1769480 | tf_op jit(solution)/shard_map/ppermute | solution.py:30
  86.1 15.6 %collective-permute-start.12 = (bf16[192,768]{1,0:T(8,128)(2,1)S(1)}, bf16[192,768]{1,0:T(8,128)(2,1)S(1)}, u32[]{:S(2)}, u32[]{:S(2)}) collective-permute-start(bf16[192,768]{1,0:T(8,128)(2,1)S(1)} %fusion.30), channel_id=1, source_target_pairs={{0,8},{1,9},{2,10},{3,11},{4,12},{5,13},{6,14},{7,15},{8,16},{9,17... | collective-permute-start | bytes 884744 | tf_op jit(solution)/shard_map/ppermute | solution.py:30
  102.1 16.1 %collective-permute-start.40 = (bf16[192,1536]{1,0:T(8,128)(2,1)S(1)}, bf16[192,1536]{1,0:T(8,128)(2,1)S(1)}, u32[]{:S(2)}, u32[]{:S(2)}) collective-permute-start(bf16[192,1536]{1,0:T(8,128)(2,1)S(1)} %copy-done), channel_id=1, source_target_pairs={{0,8},{1,9},{2,10},{3,11},{4,12},{5,13},{6,14},{7,15},{8,16},{9,17... | collective-permute-start | bytes 1769480 | tf_op jit(solution)/shard_map/ppermute | solution.py:30
  118.2 16.8 %collective-permute-start.41 = (bf16[192,768]{1,0:T(8,128)(2,1)S(1)}, bf16[192,768]{1,0:T(8,128)(2,1)S(1)}, u32[]{:S(2)}, u32[]{:S(2)}) collective-permute-start(bf16[192,768]{1,0:T(8,128)(2,1)S(1)} %constant_dynamic-slice_fusion.2), channel_id=1, source_target_pairs={{0,1},{1,0},{2,3},{3,2},{4,5},{5,4},{6,7},{7,6},{8,9},{9,8},{10,11... | collective-permute-start | bytes 884744 | tf_op jit(solution)/shard_map/ppermute | solution.py:30
  131.1 16.5 %collective-permute-start.30 = (bf16[192,768]{1,0:T(8,128)(2,1)S(1)}, bf16[192,768]{1,0:T(8,128)(2,1)S(1)}, u32[]{:S(2)}, u32[]{:S(2)}) collective-permute-start(bf16[192,768]{1,0:T(8,128)(2,1)S(1)} %get-tuple-element.45), channel_id=1, source_target_pairs={{0,1},{1,0},{2,3},{3,2},{4,5},{5,4},{6,7},{7,6},{8,9},{9,8},{10,11... | collective-permute-start | bytes 884744 | tf_op jit(solution)/shard_map/ppermute | solution.py:30
  135.2 18.0 %collective-permute-start.43 = (bf16[192,768]{1,0:T(8,128)(2,1)S(1)}, bf16[192,768]{1,0:T(8,128)(2,1)S(1)}, u32[]{:S(2)}, u32[]{:S(2)}) collective-permute-start(bf16[192,768]{1,0:T(8,128)(2,1)S(1)} %constant_dynamic-slice_fusion.1), channel_id=1, source_target_pairs={{0,1},{1,0},{2,3},{3,2},{4,5},{5,4},{6,7},{7,6},{8,9},{9,8},{10,11... | collective-permute-start | bytes 884744 | tf_op jit(solution)/shard_map/ppermute | solution.py:30
  136.7 25.3 %collective-permute-start.44 = (bf16[192,1536]{1,0:T(8,128)(2,1)S(1)}, bf16[192,1536]{1,0:T(8,128)(2,1)S(1)}, u32[]{:S(2)}, u32[]{:S(2)}) collective-permute-start(bf16[192,1536]{1,0:T(8,128)(2,1)S(1)} %collective-permute-done.42), channel_id=1, source_target_pairs={{0,8},{1,9},{2,10},{3,11},{4,12},{5,13},{6,14},{7,15},{8,16},{9,17... | collective-permute-start | bytes 1769480 | tf_op jit(solution)/shard_map/ppermute | solution.py:30
  150.3 31.9 %collective-permute-start.37 = (bf16[192,768]{1,0:T(8,128)(2,1)S(1)}, bf16[192,768]{1,0:T(8,128)(2,1)S(1)}, u32[]{:S(2)}, u32[]{:S(2)}) collective-permute-start(bf16[192,768]{1,0:T(8,128)(2,1)S(1)} %get-tuple-element.73), channel_id=1, source_target_pairs={{0,8},{1,9},{2,10},{3,11},{4,12},{5,13},{6,14},{7,15},{8,16},{9,17... | collective-permute-start | bytes 884744 | tf_op jit(solution)/shard_map/ppermute | solution.py:30
  168.2 16.7 %collective-permute-start.47 = (bf16[768,384]{1,0:T(8,128)(2,1)S(1)}, bf16[768,384]{1,0:T(8,128)(2,1)S(1)}, u32[]{:S(2)}, u32[]{:S(2)}) collective-permute-start(bf16[768,384]{1,0:T(8,128)(2,1)S(1)} %dynamic-slice_convert_fusion), channel_id=1, source_target_pairs={{0,1},{1,0},{2,3},{3,2},{4,5},{5,4},{6,7},{7,6},{8,9},{9,8},{10,11... | collective-permute-start | bytes 1769480 | tf_op jit(solution)/shard_map/ppermute | solution.py:30
  193.2 16.2 %collective-permute-start.53 = (bf16[192,1536]{1,0:T(8,128)(2,1)S(1)}, bf16[192,1536]{1,0:T(8,128)(2,1)S(1)}, u32[]{:S(2)}, u32[]{:S(2)}) collective-permute-start(bf16[192,1536]{1,0:T(8,128)(2,1)S(1)} %fusion.41), channel_id=1, source_target_pairs={{0,4},{1,5},{2,6},{3,7},{4,0},{5,1},{6,2},{7,3},{8,12},{9,13},{10,... | collective-permute-start | bytes 1769480 | tf_op jit(solution)/shard_map/ppermute | solution.py:30
  (39 other events, 371.2 us)

commit v5 on v4

--- a/solution.py
+++ b/solution.py
@@ -80,7 +80,7 @@
         for r in range(2, A + 1):
             sums = [total.astype(BF16) for total in sums]
             if r < A:
-                sums[0], rights[r] = tie(sums[0], rights[r])
+                sums[1], rights[r] = tie(sums[1], rights[r])
             sums = [up(total) for total in sums]
             sums = [
                 total.astype(F32) + dot(left_at[r % A], grad_plane[:, lo:hi], 1, 0)

time: 223 us -> 219 us (0.982)
  waiting for transfers between devices: 138 us -> 134 us
    ppermute x54, waiting for transfers between devices: 138 us -> 134 us  [sender(): return lambda value: lax.ppermute(value, ('row', 'col'), pairs)]
  transfers between devices with their start and end apart: 54 -> 54, of which waited for: 30 -> 30; matrix products, arithmetic and copies ran while one was open for 19% -> 20% of each run, Pallas kernels for 0% -> 0%
where the time goes in v5:
time: 219 us; the launch traced here: 218 us
  waiting for transfers between devices  134 us (61%)
  starting transfers between devices  36.2 us (17%)
  matrix products  23.4 us (11%)
  local copies, waits for them, and re-layouts  14.8 us (7%)
  other arithmetic  8.04 us (4%)
    ppermute x54, waiting for transfers between devices, sender(): return lambda value: lax.ppermute(value, ('row', 'col'), pairs)  134 us
    ppermute x54, starting transfers between devices, sender(): return lambda value: lax.ppermute(value, ('row', 'col'), pairs)  36.2 us
    dot_general x23, matrix products, dot(): lax.dot_general(left, right, (((left_dim,), (right_dim,)), ((), ())), pre...  23.4 us
    unnamed x22, local copies, waits for them, and re-layouts  7.45 us
    dynamic_update_slice x16, local copies, waits for them, and re-layouts, on_device(): right = lax.dynamic_update_slice(right, piece[None, None, None], place)  5.02 us
  transfers between devices with their start and end apart: 54, of which 30 were waited for; matrix products, arithmetic and copies ran while one was open for 20% of the time, Pallas kernels for 0%

profile of v5, /device:TPU:0, one launch (start us, length us, event | category | flops | bytes accessed | tf_op | source)
XLA Modules:
  0.0 218.4 jit_solution(17707390133627514679)
XLA Ops:
  11.7 8.2 %collective-permute-done.10 = bf16[192,1536]{1,0:T(8,128)(2,1)S(1)} collective-permute-done((bf16[192,1536]{1,0:T(8,128)(2,1)}, bf16[192,1536]{1,0:T(8,128)(2,1)S(1)}, u32[]{:S(2)}, u32[]{:S(2)}) %collective-permute-start.10) | collective-permute-done | bytes 589856 | tf_op jit(solution)/shard_map/ppermute | solution.py:30
  22.4 6.2 %collective-permute-done.5 = bf16[192,1536]{1,0:T(8,128)(2,1)S(1)} collective-permute-done((bf16[192,1536]{1,0:T(8,128)(2,1)S(1)}, bf16[192,1536]{1,0:T(8,128)(2,1)S(1)}, u32[]{:S(2)}, u32[]{:S(2)}) %collective-permute-start.5) | collective-permute-done | bytes 589856 | tf_op jit(solution)/shard_map/ppermute | solution.py:30
  46.0 15.5 %collective-permute-done.12 = bf16[192,768]{1,0:T(8,128)(2,1)S(1)} collective-permute-done((bf16[192,768]{1,0:T(8,128)(2,1)S(1)}, bf16[192,768]{1,0:T(8,128)(2,1)S(1)}, u32[]{:S(2)}, u32[]{:S(2)}) %collective-permute-start.12) | collective-permute-done | bytes 294944 | tf_op jit(solution)/shard_map/ppermute | solution.py:30
  62.0 3.8 %collective-permute-done.7 = bf16[192,768]{1,0:T(8,128)(2,1)S(1)} collective-permute-done((bf16[192,768]{1,0:T(8,128)(2,1)S(1)}, bf16[192,768]{1,0:T(8,128)(2,1)S(1)}, u32[]{:S(2)}, u32[]{:S(2)}) %collective-permute-start.7) | collective-permute-done | bytes 294944 | tf_op jit(solution)/shard_map/ppermute | solution.py:30
  67.4 6.2 %collective-permute-done.14 = bf16[192,768]{1,0:T(8,128)(2,1)S(1)} collective-permute-done((bf16[192,768]{1,0:T(8,128)(2,1)S(1)}, bf16[192,768]{1,0:T(8,128)(2,1)S(1)}, u32[]{:S(2)}, u32[]{:S(2)}) %collective-permute-start.14) | collective-permute-done | bytes 294944 | tf_op jit(solution)/shard_map/ppermute | solution.py:30
  75.5 4.1 %collective-permute-done.8 = bf16[192,768]{1,0:T(8,128)(2,1)S(1)} collective-permute-done((bf16[192,768]{1,0:T(8,128)(2,1)S(1)}, bf16[192,768]{1,0:T(8,128)(2,1)S(1)}, u32[]{:S(2)}, u32[]{:S(2)}) %collective-permute-start.8) | collective-permute-done | bytes 294944 | tf_op jit(solution)/shard_map/ppermute | solution.py:30
  84.6 5.8 %collective-permute-done.23 = bf16[192,1536]{1,0:T(8,128)(2,1)S(1)} collective-permute-done((bf16[192,1536]{1,0:T(8,128)(2,1)}, bf16[192,1536]{1,0:T(8,128)(2,1)S(1)}, u32[]{:S(2)}, u32[]{:S(2)}) %collective-permute-start.23) | collective-permute-done | bytes 589856 | tf_op jit(solution)/shard_map/ppermute | solution.py:30
  90.6 4.5 %collective-permute-done.15 = bf16[192,768]{1,0:T(8,128)(2,1)S(1)} collective-permute-done((bf16[192,768]{1,0:T(8,128)(2,1)S(1)}, bf16[192,768]{1,0:T(8,128)(2,1)S(1)}, u32[]{:S(2)}, u32[]{:S(2)}) %collective-permute-start.15) | collective-permute-done | bytes 294944 | tf_op jit(solution)/shard_map/ppermute | solution.py:30
  95.5 4.7 %collective-permute-done.9 = bf16[192,768]{1,0:T(8,128)(2,1)S(1)} collective-permute-done((bf16[192,768]{1,0:T(8,128)(2,1)S(1)}, bf16[192,768]{1,0:T(8,128)(2,1)S(1)}, u32[]{:S(2)}, u32[]{:S(2)}) %collective-permute-start.9) | collective-permute-done | bytes 294944 | tf_op jit(solution)/shard_map/ppermute | solution.py:30
  104.8 3.2 %fusion.161 = (bf16[192,3072]{1,0:T(8,128)(2,1)S(1)}, f32[192,3072]{1,0:T(8,128)S(1)}) fusion(bf16[192,1536]{1,0:T(8,128)(2,1)S(1)} %pad_maximum_fusion.4, bf16[3072,1536]{1,0:T(8,128)(2,1)S(1)} %bitcast.123), kind=kOutput, calls=%fused_computation.252 | convolution fusion | flops 1812529152 | bytes 13565952 | tf_op jit(solution)/shard_map/dot_general | solution.py:11
  110.2 6.5 %collective-permute-done.40 = bf16[192,1536]{1,0:T(8,128)(2,1)S(1)} collective-permute-done((bf16[192,1536]{1,0:T(8,128)(2,1)S(1)}, bf16[192,1536]{1,0:T(8,128)(2,1)S(1)}, u32[]{:S(2)}, u32[]{:S(2)}) %collective-permute-start.40) | collective-permute-done | bytes 589856 | tf_op jit(solution)/shard_map/ppermute | solution.py:30
  118.3 6.0 %collective-permute-done.29 = bf16[192,768]{1,0:T(8,128)(2,1)S(1)} collective-permute-done((bf16[192,768]{1,0:T(8,128)(2,1)S(1)}, bf16[192,768]{1,0:T(8,128)(2,1)S(1)}, u32[]{:S(2)}, u32[]{:S(2)}) %collective-permute-start.29) | collective-permute-done | bytes 294944 | tf_op jit(solution)/shard_map/ppermute | solution.py:30
  133.6 3.3 %collective-permute-done.31 = bf16[192,768]{1,0:T(8,128)(2,1)S(1)} collective-permute-done((bf16[192,768]{1,0:T(8,128)(2,1)S(1)}, bf16[192,768]{1,0:T(8,128)(2,1)S(1)}, u32[]{:S(2)}, u32[]{:S(2)}) %collective-permute-start.31) | collective-permute-done | bytes 294944 | tf_op jit(solution)/shard_map/ppermute | solution.py:30
  136.9 6.3 %collective-permute-done.30 = bf16[192,768]{1,0:T(8,128)(2,1)S(1)} collective-permute-done((bf16[192,768]{1,0:T(8,128)(2,1)S(1)}, bf16[192,768]{1,0:T(8,128)(2,1)S(1)}, u32[]{:S(2)}, u32[]{:S(2)}) %collective-permute-start.30) | collective-permute-done | bytes 294944 | tf_op jit(solution)/shard_map/ppermute | solution.py:30
  148.8 8.2 %collective-permute-done.32 = bf16[192,768]{1,0:T(8,128)(2,1)S(1)} collective-permute-done((bf16[192,768]{1,0:T(8,128)(2,1)S(1)}, bf16[192,768]{1,0:T(8,128)(2,1)S(1)}, u32[]{:S(2)}, u32[]{:S(2)}) %collective-permute-start.32) | collective-permute-done | bytes 294944 | tf_op jit(solution)/shard_map/ppermute | solution.py:30
  160.4 3.1 %fusion.12 = f32[768,768]{1,0:T(8,128)S(1)} fusion(bf16[192,1536]{1,0:T(8,128)(2,1)S(1)} %collective-permute-done.6, bf16[192,1536]{1,0:T(8,128)(2,1)S(1)} %copy-done.6, bf16[192,1536]{1,0:T(8,128)(2,1)} %collective-permute-done.4, bf16[192,1536]{1,0:T(8,128)(2,1)S(1)} %copy-done, bf16[192,1536]{1,0:T(8,128)(2,1)S(1)} %get-tuple-element.57, ...), kind=kOutput, calls=%fused_computation.14 | convolution fusion | flops 1830813696 | bytes 7077888 | tf_op jit(solution)/shard_map/dot_general | solution.py:11
  164.4 2.8 %collective-permute-done.33 = bf16[192,768]{1,0:T(8,128)(2,1)S(1)} collective-permute-done((bf16[192,768]{1,0:T(8,128)(2,1)S(1)}, bf16[192,768]{1,0:T(8,128)(2,1)S(1)}, u32[]{:S(2)}, u32[]{:S(2)}) %collective-permute-start.33) | collective-permute-done | bytes 294944 | tf_op jit(solution)/shard_map/ppermute | solution.py:30
  169.9 5.8 %collective-permute-done.34 = bf16[192,768]{1,0:T(8,128)(2,1)S(1)} collective-permute-done((bf16[192,768]{1,0:T(8,128)(2,1)S(1)}, bf16[192,768]{1,0:T(8,128)(2,1)S(1)}, u32[]{:S(2)}, u32[]{:S(2)}) %collective-permute-start.34) | collective-permute-done | bytes 294944 | tf_op jit(solution)/shard_map/ppermute | solution.py:30
  180.8 7.0 %collective-permute-done.36 = bf16[192,768]{1,0:T(8,128)(2,1)S(1)} collective-permute-done((bf16[192,768]{1,0:T(8,128)(2,1)S(1)}, bf16[192,768]{1,0:T(8,128)(2,1)S(1)}, u32[]{:S(2)}, u32[]{:S(2)}) %collective-permute-start.36) | collective-permute-done | bytes 294944 | tf_op jit(solution)/shard_map/ppermute | solution.py:30
  190.8 7.7 %collective-permute-done.48 = bf16[192,768]{1,0:T(8,128)(2,1)S(1)} collective-permute-done((bf16[192,768]{1,0:T(8,128)(2,1)S(1)}, bf16[192,768]{1,0:T(8,128)(2,1)S(1)}, u32[]{:S(2)}, u32[]{:S(2)}) %collective-permute-start.48) | collective-permute-done | bytes 294944 | tf_op jit(solution)/shard_map/ppermute | solution.py:30
  200.9 4.1 %collective-permute-done.53 = bf16[192,1536]{1,0:T(8,128)(2,1)S(1)} collective-permute-done((bf16[192,1536]{1,0:T(8,128)(2,1)S(1)}, bf16[192,1536]{1,0:T(8,128)(2,1)S(1)}, u32[]{:S(2)}, u32[]{:S(2)}) %collective-permute-start.53) | collective-permute-done | bytes 589856 | tf_op jit(solution)/shard_map/ppermute | solution.py:30
  208.0 3.3 %collective-permute-done.52 = bf16[192,768]{1,0:T(8,128)(2,1)S(1)} collective-permute-done((bf16[192,768]{1,0:T(8,128)(2,1)S(1)}, bf16[192,768]{1,0:T(8,128)(2,1)S(1)}, u32[]{:S(2)}, u32[]{:S(2)}) %collective-permute-start.52) | collective-permute-done | bytes 294944 | tf_op jit(solution)/shard_map/ppermute | solution.py:30
  211.3 3.0 %fusion.3 = f32[1536,192]{0,1:T(8,128)} fusion(s32[1536]{0:T(1024)S(1)} %add.514, f32[1536,192]{0,1:T(8,128)S(1)} %copy-done.8, bf16[192,768]{1,0:T(8,128)(2,1)S(1)} %collective-permute-done.52, bf16[192,384]{1,0:T(8,128)(2,1)S(1)} %get-tuple-element.74, bf16[192,384]{1,0:T(8,128)(2,1)S(1)} %get-tuple-element.68), kind=kOutput, calls=%fused_computation.4 | convolution fusion | flops 910983168 | bytes 2955264 | tf_op jit(solution)/shard_map/dot_general | solution.py:11
  214.3 2.8 %collective-permute-done.50 = bf16[192,768]{1,0:T(8,128)(2,1)S(1)} collective-permute-done((bf16[192,768]{1,0:T(8,128)(2,1)S(1)}, bf16[192,768]{1,0:T(8,128)(2,1)S(1)}, u32[]{:S(2)}, u32[]{:S(2)}) %collective-permute-start.50) | collective-permute-done | bytes 294944 | tf_op jit(solution)/shard_map/ppermute | solution.py:30
  (198 shorter events, 84.3 us)
Async XLA Ops:
  1.1 18.8 %collective-permute-start.10 = (bf16[192,1536]{1,0:T(8,128)(2,1)}, bf16[192,1536]{1,0:T(8,128)(2,1)S(1)}, u32[]{:S(2)}, u32[]{:S(2)}) collective-permute-start(bf16[192,1536]{1,0:T(8,128)(2,1)} %bitcast.152), channel_id=1, source_target_pairs={{0,8},{1,9},{2,10},{3,11},{4,12},{5,13},{6,14},{7,15},{8,16},{9,17... | collective-permute-start | bytes 1769480 | tf_op jit(solution)/shard_map/ppermute | solution.py:30
  8.7 19.9 %collective-permute-start.5 = (bf16[192,1536]{1,0:T(8,128)(2,1)S(1)}, bf16[192,1536]{1,0:T(8,128)(2,1)S(1)}, u32[]{:S(2)}, u32[]{:S(2)}) collective-permute-start(bf16[192,1536]{1,0:T(8,128)(2,1)S(1)} %copy-done), channel_id=1, source_target_pairs={{0,4},{1,5},{2,6},{3,7},{4,0},{5,1},{6,2},{7,3},{8,12},{9,13},{10,... | collective-permute-start | bytes 1769480 | tf_op jit(solution)/shard_map/ppermute | solution.py:30
  9.3 22.2 %collective-permute-start.4 = (bf16[192,1536]{1,0:T(8,128)(2,1)S(1)}, bf16[192,1536]{1,0:T(8,128)(2,1)}, u32[]{:S(2)}, u32[]{:S(2)}) collective-permute-start(bf16[192,1536]{1,0:T(8,128)(2,1)S(1)} %copy-done), channel_id=1, source_target_pairs={{0,2},{1,3},{2,0},{3,1},{4,6},{5,7},{6,4},{7,5},{8,10},{9,11},{10,... | collective-permute-start | bytes 1769480 | tf_op jit(solution)/shard_map/ppermute | solution.py:30
  10.2 18.5 %collective-permute-start.2 = (bf16[384,384]{0,1:T(8,128)(2,1)S(1)}, bf16[384,384]{0,1:T(8,128)(2,1)S(1)}, u32[]{:S(2)}, u32[]{:S(2)}) collective-permute-start(bf16[384,384]{0,1:T(8,128)(2,1)S(1)} %fusion.36), channel_id=1, source_target_pairs={{0,1},{1,0},{2,3},{3,2},{4,5},{5,4},{6,7},{7,6},{8,9},{9,8},{10,11... | collective-permute-start | bytes 884744 | tf_op jit(solution)/shard_map/ppermute | solution.py:30
  20.0 17.0 %collective-permute-start.11 = (bf16[192,1536]{1,0:T(8,128)(2,1)S(1)}, bf16[192,1536]{1,0:T(8,128)(2,1)}, u32[]{:S(2)}, u32[]{:S(2)}) collective-permute-start(bf16[192,1536]{1,0:T(8,128)(2,1)S(1)} %collective-permute-done.10), channel_id=1, source_target_pairs={{0,8},{1,9},{2,10},{3,11},{4,12},{5,13},{6,14},{7,15},{8,16},{9,17... | collective-permute-start | bytes 1769480 | tf_op jit(solution)/shard_map/ppermute | solution.py:30
  28.6 15.9 %collective-permute-start.17 = (bf16[192,1536]{1,0:T(8,128)(2,1)S(1)}, bf16[192,1536]{1,0:T(8,128)(2,1)}, u32[]{:S(2)}, u32[]{:S(2)}) collective-permute-start(bf16[192,1536]{1,0:T(8,128)(2,1)S(1)} %bitcast.154), channel_id=1, source_target_pairs={{0,4},{1,5},{2,6},{3,7},{4,0},{5,1},{6,2},{7,3},{8,12},{9,13},{10,... | collective-permute-start | bytes 1769480 | tf_op jit(solution)/shard_map/ppermute | solution.py:30
  30.2 50.4 %collective-permute-start.19 = (bf16[192,1536]{1,0:T(8,128)(2,1)S(1)}, bf16[192,1536]{1,0:T(8,128)(2,1)}, u32[]{:S(2)}, u32[]{:S(2)}) collective-permute-start(bf16[192,1536]{1,0:T(8,128)(2,1)S(1)} %collective-permute-done.10), channel_id=1, source_target_pairs={{0,2},{1,3},{2,0},{3,1},{4,6},{5,7},{6,4},{7,5},{8,10},{9,11},{10,... | collective-permute-start | bytes 1769480 | tf_op jit(solution)/shard_map/ppermute | solution.py:30
  37.0 25.0 %collective-permute-start.13 = (bf16[192,1536]{1,0:T(8,128)(2,1)}, bf16[192,1536]{1,0:T(8,128)(2,1)S(1)}, u32[]{:S(2)}, u32[]{:S(2)}) collective-permute-start(bf16[192,1536]{1,0:T(8,128)(2,1)} %collective-permute-done.11), channel_id=1, source_target_pairs={{0,8},{1,9},{2,10},{3,11},{4,12},{5,13},{6,14},{7,15},{8,16},{9,17... | collective-permute-start | bytes 1769480 | tf_op jit(solution)/shard_map/ppermute | solution.py:30
  40.0 21.6 %collective-permute-start.12 = (bf16[192,768]{1,0:T(8,128)(2,1)S(1)}, bf16[192,768]{1,0:T(8,128)(2,1)S(1)}, u32[]{:S(2)}, u32[]{:S(2)}) collective-permute-start(bf16[192,768]{1,0:T(8,128)(2,1)S(1)} %convolution_convert_fusion.1), channel_id=1, source_target_pairs={{0,8},{1,9},{2,10},{3,11},{4,12},{5,13},{6,14},{7,15},{8,16},{9,17... | collective-permute-start | bytes 884744 | tf_op jit(solution)/shard_map/ppermute | solution.py:30
  41.6 24.2 %collective-permute-start.7 = (bf16[192,768]{1,0:T(8,128)(2,1)S(1)}, bf16[192,768]{1,0:T(8,128)(2,1)S(1)}, u32[]{:S(2)}, u32[]{:S(2)}) collective-permute-start(bf16[192,768]{1,0:T(8,128)(2,1)S(1)} %convolution_convert_fusion.2), channel_id=1, source_target_pairs={{0,8},{1,9},{2,10},{3,11},{4,12},{5,13},{6,14},{7,15},{8,16},{9,17... | collective-permute-start | bytes 884744 | tf_op jit(solution)/shard_map/ppermute | solution.py:30
  44.5 29.6 %collective-permute-start.20 = (bf16[192,1536]{1,0:T(8,128)(2,1)S(1)}, bf16[192,1536]{1,0:T(8,128)(2,1)S(1)}, u32[]{:S(2)}, u32[]{:S(2)}) collective-permute-start(bf16[192,1536]{1,0:T(8,128)(2,1)S(1)} %collective-permute-done.10), channel_id=1, source_target_pairs={{0,4},{1,5},{2,6},{3,7},{4,0},{5,1},{6,2},{7,3},{8,12},{9,13},{10,... | collective-permute-start | bytes 1769480 | tf_op jit(solution)/shard_map/ppermute | solution.py:30
  61.5 18.4 %collective-permute-start.18 = (bf16[192,1536]{1,0:T(8,128)(2,1)}, bf16[192,1536]{1,0:T(8,128)(2,1)S(1)}, u32[]{:S(2)}, u32[]{:S(2)}) collective-permute-start(bf16[192,1536]{1,0:T(8,128)(2,1)} %collective-permute-done.17), channel_id=1, source_target_pairs={{0,2},{1,3},{2,0},{3,1},{4,6},{5,7},{6,4},{7,5},{8,10},{9,11},{10,... | collective-permute-start | bytes 1769480 | tf_op jit(solution)/shard_map/ppermute | solution.py:30
  74.1 16.4 %collective-permute-start.23 = (bf16[192,1536]{1,0:T(8,128)(2,1)}, bf16[192,1536]{1,0:T(8,128)(2,1)S(1)}, u32[]{:S(2)}, u32[]{:S(2)}) collective-permute-start(bf16[192,1536]{1,0:T(8,128)(2,1)} %collective-permute-done.11), channel_id=1, source_target_pairs={{0,4},{1,5},{2,6},{3,7},{4,0},{5,1},{6,2},{7,3},{8,12},{9,13},{10,... | collective-permute-start | bytes 1769480 | tf_op jit(solution)/shard_map/ppermute | solution.py:30
  80.0 22.8 %collective-permute-start.25 = (bf16[192,1536]{1,0:T(8,128)(2,1)S(1)}, bf16[192,1536]{1,0:T(8,128)(2,1)S(1)}, u32[]{:S(2)}, u32[]{:S(2)}) collective-permute-start(bf16[192,1536]{1,0:T(8,128)(2,1)S(1)} %collective-permute-done.13), channel_id=1, source_target_pairs={{0,2},{1,3},{2,0},{3,1},{4,6},{5,7},{6,4},{7,5},{8,10},{9,11},{10,... | collective-permute-start | bytes 1769480 | tf_op jit(solution)/shard_map/ppermute | solution.py:30
  80.7 22.0 %collective-permute-start.26 = (bf16[192,1536]{1,0:T(8,128)(2,1)S(1)}, bf16[192,1536]{1,0:T(8,128)(2,1)S(1)}, u32[]{:S(2)}, u32[]{:S(2)}) collective-permute-start(bf16[192,1536]{1,0:T(8,128)(2,1)S(1)} %collective-permute-done.13), channel_id=1, source_target_pairs={{0,4},{1,5},{2,6},{3,7},{4,0},{5,1},{6,2},{7,3},{8,12},{9,13},{10,... | collective-permute-start | bytes 1769480 | tf_op jit(solution)/shard_map/ppermute | solution.py:30
  84.5 15.6 %collective-permute-start.9 = (bf16[192,768]{1,0:T(8,128)(2,1)S(1)}, bf16[192,768]{1,0:T(8,128)(2,1)S(1)}, u32[]{:S(2)}, u32[]{:S(2)}) collective-permute-start(bf16[192,768]{1,0:T(8,128)(2,1)S(1)} %fusion.30), channel_id=1, source_target_pairs={{0,8},{1,9},{2,10},{3,11},{4,12},{5,13},{6,14},{7,15},{8,16},{9,17... | collective-permute-start | bytes 884744 | tf_op jit(solution)/shard_map/ppermute | solution.py:30
  100.6 16.1 %collective-permute-start.40 = (bf16[192,1536]{1,0:T(8,128)(2,1)S(1)}, bf16[192,1536]{1,0:T(8,128)(2,1)S(1)}, u32[]{:S(2)}, u32[]{:S(2)}) collective-permute-start(bf16[192,1536]{1,0:T(8,128)(2,1)S(1)} %copy-done), channel_id=1, source_target_pairs={{0,8},{1,9},{2,10},{3,11},{4,12},{5,13},{6,14},{7,15},{8,16},{9,17... | collective-permute-start | bytes 1769480 | tf_op jit(solution)/shard_map/ppermute | solution.py:30
  109.5 14.8 %collective-permute-start.29 = (bf16[192,768]{1,0:T(8,128)(2,1)S(1)}, bf16[192,768]{1,0:T(8,128)(2,1)S(1)}, u32[]{:S(2)}, u32[]{:S(2)}) collective-permute-start(bf16[192,768]{1,0:T(8,128)(2,1)S(1)} %get-tuple-element.65), channel_id=1, source_target_pairs={{0,1},{1,0},{2,3},{3,2},{4,5},{5,4},{6,7},{7,6},{8,9},{9,8},{10,11... | collective-permute-start | bytes 884744 | tf_op jit(solution)/shard_map/ppermute | solution.py:30
  126.6 16.6 %collective-permute-start.30 = (bf16[192,768]{1,0:T(8,128)(2,1)S(1)}, bf16[192,768]{1,0:T(8,128)(2,1)S(1)}, u32[]{:S(2)}, u32[]{:S(2)}) collective-permute-start(bf16[192,768]{1,0:T(8,128)(2,1)S(1)} %get-tuple-element.45), channel_id=1, source_target_pairs={{0,1},{1,0},{2,3},{3,2},{4,5},{5,4},{6,7},{7,6},{8,9},{9,8},{10,11... | collective-permute-start | bytes 884744 | tf_op jit(solution)/shard_map/ppermute | solution.py:30
  133.0 15.8 %collective-permute-start.43 = (bf16[192,768]{1,0:T(8,128)(2,1)S(1)}, bf16[192,768]{1,0:T(8,128)(2,1)S(1)}, u32[]{:S(2)}, u32[]{:S(2)}) collective-permute-start(bf16[192,768]{1,0:T(8,128)(2,1)S(1)} %constant_dynamic-slice_fusion.1), channel_id=1, source_target_pairs={{0,1},{1,0},{2,3},{3,2},{4,5},{5,4},{6,7},{7,6},{8,9},{9,8},{10,11... | collective-permute-start | bytes 884744 | tf_op jit(solution)/shard_map/ppermute | solution.py:30
  133.6 24.0 %collective-permute-start.44 = (bf16[192,1536]{1,0:T(8,128)(2,1)S(1)}, bf16[192,1536]{1,0:T(8,128)(2,1)S(1)}, u32[]{:S(2)}, u32[]{:S(2)}) collective-permute-start(bf16[192,1536]{1,0:T(8,128)(2,1)S(1)} %collective-permute-done.42), channel_id=1, source_target_pairs={{0,8},{1,9},{2,10},{3,11},{4,12},{5,13},{6,14},{7,15},{8,16},{9,17... | collective-permute-start | bytes 1769480 | tf_op jit(solution)/shard_map/ppermute | solution.py:30
  145.9 31.9 %collective-permute-start.37 = (bf16[192,768]{1,0:T(8,128)(2,1)S(1)}, bf16[192,768]{1,0:T(8,128)(2,1)S(1)}, u32[]{:S(2)}, u32[]{:S(2)}) collective-permute-start(bf16[192,768]{1,0:T(8,128)(2,1)S(1)} %get-tuple-element.73), channel_id=1, source_target_pairs={{0,8},{1,9},{2,10},{3,11},{4,12},{5,13},{6,14},{7,15},{8,16},{9,17... | collective-permute-start | bytes 884744 | tf_op jit(solution)/shard_map/ppermute | solution.py:30
  163.6 17.0 %collective-permute-start.47 = (bf16[768,384]{1,0:T(8,128)(2,1)S(1)}, bf16[768,384]{1,0:T(8,128)(2,1)S(1)}, u32[]{:S(2)}, u32[]{:S(2)}) collective-permute-start(bf16[768,384]{1,0:T(8,128)(2,1)S(1)} %dynamic-slice_convert_fusion), channel_id=1, source_target_pairs={{0,1},{1,0},{2,3},{3,2},{4,5},{5,4},{6,7},{7,6},{8,9},{9,8},{10,11... | collective-permute-start | bytes 1769480 | tf_op jit(solution)/shard_map/ppermute | solution.py:30
  188.8 16.2 %collective-permute-start.53 = (bf16[192,1536]{1,0:T(8,128)(2,1)S(1)}, bf16[192,1536]{1,0:T(8,128)(2,1)S(1)}, u32[]{:S(2)}, u32[]{:S(2)}) collective-permute-start(bf16[192,1536]{1,0:T(8,128)(2,1)S(1)} %fusion.41), channel_id=1, source_target_pairs={{0,4},{1,5},{2,6},{3,7},{4,0},{5,1},{6,2},{7,3},{8,12},{9,13},{10,... | collective-permute-start | bytes 1769480 | tf_op jit(solution)/shard_map/ppermute | solution.py:30
  (39 other events, 368.5 us)

commit v6 on v5

--- a/solution.py
+++ b/solution.py
@@ -154,13 +154,12 @@
         for r in range(1, A):
             halves = [up(half) for half in halves]
             if r == A - 2:
-                halves[1], right_other = tie(halves[1], right_other)
-            if r == A - 2:
                 halves[1], left_sum = tie(halves[1], left_sum)
                 own, core, over, cross = jnp.split(left_sum.astype(BF16), 4)
                 got = flip_c(jnp.concatenate([core, cross]))
             if r == A - 1:
                 over_pair = flip_y(jnp.concatenate([over, got[b:]], axis=1))
+                halves[1], right_other = tie(halves[1], right_other)
                 right_sum += flip_y(right_other).astype(F32)
             update = [total + dot(left_at[r], half, 0, 0) for total, half in zip(update, halves)]
         update = jnp.concatenate([plane_scatter(jnp.split(u, 4)) for u in update], axis=1)

time: 219 us -> 221 us (level)
  waiting for transfers between devices: 134 us -> 138 us
    ppermute x54, waiting for transfers between devices: 134 us -> 138 us  [sender(): return lambda value: lax.ppermute(value, ('row', 'col'), pairs)]
  transfers between devices with their start and end apart: 54 -> 54, of which waited for: 30 -> 29; matrix products, arithmetic and copies ran while one was open for 20% -> 20% of each run, Pallas kernels for 0% -> 0%
where the time goes in v6:
time: 221 us
  waiting for transfers between devices  138 us (62%)
  starting transfers between devices  35.6 us (16%)
  matrix products  23.3 us (11%)
  local copies, waits for them, and re-layouts  13.9 us (6%)
  other arithmetic  8.06 us (4%)
    ppermute x54, waiting for transfers between devices, sender(): return lambda value: lax.ppermute(value, ('row', 'col'), pairs)  138 us
    ppermute x54, starting transfers between devices, sender(): return lambda value: lax.ppermute(value, ('row', 'col'), pairs)  35.6 us
    dot_general x23, matrix products, dot(): lax.dot_general(left, right, (((left_dim,), (right_dim,)), ((), ())), pre...  23.3 us
    unnamed x22, local copies, waits for them, and re-layouts  6.57 us
    dynamic_update_slice x16, local copies, waits for them, and re-layouts, on_device(): right = lax.dynamic_update_slice(right, piece[None, None, None], place)  5.02 us
  transfers between devices with their start and end apart: 54, of which 29 were waited for; matrix products, arithmetic and copies ran while one was open for 20% of the time, Pallas kernels for 0%

profile of v6, /device:TPU:0, one launch (start us, length us, event | category | flops | bytes accessed | tf_op | source)
XLA Modules:
  0.0 220.9 jit_solution(11477080337047578488)
XLA Ops:
  1.1 2.6 %collective-permute-start.10 = (bf16[192,1536]{1,0:T(8,128)(2,1)}, bf16[192,1536]{1,0:T(8,128)(2,1)S(1)}, u32[]{:S(2)}, u32[]{:S(2)}) collective-permute-start(bf16[192,1536]{1,0:T(8,128)(2,1)} %bitcast.152), channel_id=1, source_target_pairs={{0,8},{1,9},{2,10},{3,11},{4,12},{5,13},{6,14},{7,15},{8,16},{9,17... | collective-permute-start | bytes 1769480 | tf_op jit(solution)/shard_map/ppermute | solution.py:30
  11.7 8.2 %collective-permute-done.10 = bf16[192,1536]{1,0:T(8,128)(2,1)S(1)} collective-permute-done((bf16[192,1536]{1,0:T(8,128)(2,1)}, bf16[192,1536]{1,0:T(8,128)(2,1)S(1)}, u32[]{:S(2)}, u32[]{:S(2)}) %collective-permute-start.10) | collective-permute-done | bytes 589856 | tf_op jit(solution)/shard_map/ppermute | solution.py:30
  22.4 6.2 %collective-permute-done.5 = bf16[192,1536]{1,0:T(8,128)(2,1)S(1)} collective-permute-done((bf16[192,1536]{1,0:T(8,128)(2,1)S(1)}, bf16[192,1536]{1,0:T(8,128)(2,1)S(1)}, u32[]{:S(2)}, u32[]{:S(2)}) %collective-permute-start.5) | collective-permute-done | bytes 589856 | tf_op jit(solution)/shard_map/ppermute | solution.py:30
  46.0 15.5 %collective-permute-done.12 = bf16[192,768]{1,0:T(8,128)(2,1)S(1)} collective-permute-done((bf16[192,768]{1,0:T(8,128)(2,1)S(1)}, bf16[192,768]{1,0:T(8,128)(2,1)S(1)}, u32[]{:S(2)}, u32[]{:S(2)}) %collective-permute-start.12) | collective-permute-done | bytes 294944 | tf_op jit(solution)/shard_map/ppermute | solution.py:30
  62.0 3.8 %collective-permute-done.7 = bf16[192,768]{1,0:T(8,128)(2,1)S(1)} collective-permute-done((bf16[192,768]{1,0:T(8,128)(2,1)S(1)}, bf16[192,768]{1,0:T(8,128)(2,1)S(1)}, u32[]{:S(2)}, u32[]{:S(2)}) %collective-permute-start.7) | collective-permute-done | bytes 294944 | tf_op jit(solution)/shard_map/ppermute | solution.py:30
  67.4 6.2 %collective-permute-done.14 = bf16[192,768]{1,0:T(8,128)(2,1)S(1)} collective-permute-done((bf16[192,768]{1,0:T(8,128)(2,1)S(1)}, bf16[192,768]{1,0:T(8,128)(2,1)S(1)}, u32[]{:S(2)}, u32[]{:S(2)}) %collective-permute-start.14) | collective-permute-done | bytes 294944 | tf_op jit(solution)/shard_map/ppermute | solution.py:30
  75.5 4.1 %collective-permute-done.8 = bf16[192,768]{1,0:T(8,128)(2,1)S(1)} collective-permute-done((bf16[192,768]{1,0:T(8,128)(2,1)S(1)}, bf16[192,768]{1,0:T(8,128)(2,1)S(1)}, u32[]{:S(2)}, u32[]{:S(2)}) %collective-permute-start.8) | collective-permute-done | bytes 294944 | tf_op jit(solution)/shard_map/ppermute | solution.py:30
  84.6 5.8 %collective-permute-done.23 = bf16[192,1536]{1,0:T(8,128)(2,1)S(1)} collective-permute-done((bf16[192,1536]{1,0:T(8,128)(2,1)}, bf16[192,1536]{1,0:T(8,128)(2,1)S(1)}, u32[]{:S(2)}, u32[]{:S(2)}) %collective-permute-start.23) | collective-permute-done | bytes 589856 | tf_op jit(solution)/shard_map/ppermute | solution.py:30
  90.6 4.5 %collective-permute-done.15 = bf16[192,768]{1,0:T(8,128)(2,1)S(1)} collective-permute-done((bf16[192,768]{1,0:T(8,128)(2,1)S(1)}, bf16[192,768]{1,0:T(8,128)(2,1)S(1)}, u32[]{:S(2)}, u32[]{:S(2)}) %collective-permute-start.15) | collective-permute-done | bytes 294944 | tf_op jit(solution)/shard_map/ppermute | solution.py:30
  95.5 4.7 %collective-permute-done.9 = bf16[192,768]{1,0:T(8,128)(2,1)S(1)} collective-permute-done((bf16[192,768]{1,0:T(8,128)(2,1)S(1)}, bf16[192,768]{1,0:T(8,128)(2,1)S(1)}, u32[]{:S(2)}, u32[]{:S(2)}) %collective-permute-start.9) | collective-permute-done | bytes 294944 | tf_op jit(solution)/shard_map/ppermute | solution.py:30
  104.8 3.2 %fusion.161 = (bf16[192,3072]{1,0:T(8,128)(2,1)S(1)}, f32[192,3072]{1,0:T(8,128)S(1)}) fusion(bf16[192,1536]{1,0:T(8,128)(2,1)S(1)} %pad_maximum_fusion.4, bf16[3072,1536]{1,0:T(8,128)(2,1)S(1)} %bitcast.123), kind=kOutput, calls=%fused_computation.252 | convolution fusion | flops 1812529152 | bytes 13565952 | tf_op jit(solution)/shard_map/dot_general | solution.py:11
  110.2 6.5 %collective-permute-done.39 = bf16[192,1536]{1,0:T(8,128)(2,1)S(1)} collective-permute-done((bf16[192,1536]{1,0:T(8,128)(2,1)S(1)}, bf16[192,1536]{1,0:T(8,128)(2,1)S(1)}, u32[]{:S(2)}, u32[]{:S(2)}) %collective-permute-start.39) | collective-permute-done | bytes 589856 | tf_op jit(solution)/shard_map/ppermute | solution.py:30
  118.3 6.0 %collective-permute-done.29 = bf16[192,768]{1,0:T(8,128)(2,1)S(1)} collective-permute-done((bf16[192,768]{1,0:T(8,128)(2,1)S(1)}, bf16[192,768]{1,0:T(8,128)(2,1)S(1)}, u32[]{:S(2)}, u32[]{:S(2)}) %collective-permute-start.29) | collective-permute-done | bytes 294944 | tf_op jit(solution)/shard_map/ppermute | solution.py:30
  133.6 3.3 %collective-permute-done.31 = bf16[192,768]{1,0:T(8,128)(2,1)S(1)} collective-permute-done((bf16[192,768]{1,0:T(8,128)(2,1)S(1)}, bf16[192,768]{1,0:T(8,128)(2,1)S(1)}, u32[]{:S(2)}, u32[]{:S(2)}) %collective-permute-start.31) | collective-permute-done | bytes 294944 | tf_op jit(solution)/shard_map/ppermute | solution.py:30
  136.9 6.3 %collective-permute-done.30 = bf16[192,768]{1,0:T(8,128)(2,1)S(1)} collective-permute-done((bf16[192,768]{1,0:T(8,128)(2,1)S(1)}, bf16[192,768]{1,0:T(8,128)(2,1)S(1)}, u32[]{:S(2)}, u32[]{:S(2)}) %collective-permute-start.30) | collective-permute-done | bytes 294944 | tf_op jit(solution)/shard_map/ppermute | solution.py:30
  148.8 8.8 %collective-permute-done.37 = bf16[192,768]{1,0:T(8,128)(2,1)S(1)} collective-permute-done((bf16[192,768]{1,0:T(8,128)(2,1)S(1)}, bf16[192,768]{1,0:T(8,128)(2,1)S(1)}, u32[]{:S(2)}, u32[]{:S(2)}) %collective-permute-start.37) | collective-permute-done | bytes 294944 | tf_op jit(solution)/shard_map/ppermute | solution.py:30
  157.6 6.3 %collective-permute-done.32 = bf16[192,768]{1,0:T(8,128)(2,1)S(1)} collective-permute-done((bf16[192,768]{1,0:T(8,128)(2,1)S(1)}, bf16[192,768]{1,0:T(8,128)(2,1)S(1)}, u32[]{:S(2)}, u32[]{:S(2)}) %collective-permute-start.32) | collective-permute-done | bytes 294944 | tf_op jit(solution)/shard_map/ppermute | solution.py:30
  166.4 3.1 %fusion.4 = f32[768,768]{1,0:T(8,128)S(1)} fusion(bf16[192,1536]{1,0:T(8,128)(2,1)S(1)} %collective-permute-done.6, bf16[192,1536]{1,0:T(8,128)(2,1)S(1)} %copy-done.6, bf16[192,1536]{1,0:T(8,128)(2,1)} %collective-permute-done.4, bf16[192,1536]{1,0:T(8,128)(2,1)S(1)} %copy-done, bf16[192,1536]{1,0:T(8,128)(2,1)S(1)} %get-tuple-element.57, ...), kind=kOutput, calls=%fused_computation.6 | convolution fusion | flops 1830813696 | bytes 7077888 | tf_op jit(solution)/shard_map/dot_general | solution.py:11
  170.4 3.6 %collective-permute-done.33 = bf16[192,768]{1,0:T(8,128)(2,1)S(1)} collective-permute-done((bf16[192,768]{1,0:T(8,128)(2,1)S(1)}, bf16[192,768]{1,0:T(8,128)(2,1)S(1)}, u32[]{:S(2)}, u32[]{:S(2)}) %collective-permute-start.33) | collective-permute-done | bytes 294944 | tf_op jit(solution)/shard_map/ppermute | solution.py:30
  177.5 5.1 %collective-permute-done.34 = bf16[192,768]{1,0:T(8,128)(2,1)S(1)} collective-permute-done((bf16[192,768]{1,0:T(8,128)(2,1)S(1)}, bf16[192,768]{1,0:T(8,128)(2,1)S(1)}, u32[]{:S(2)}, u32[]{:S(2)}) %collective-permute-start.34) | collective-permute-done | bytes 294944 | tf_op jit(solution)/shard_map/ppermute | solution.py:30
  188.1 7.4 %collective-permute-done.43 = bf16[192,768]{1,0:T(8,128)(2,1)S(1)} collective-permute-done((bf16[192,768]{1,0:T(8,128)(2,1)S(1)}, bf16[192,768]{1,0:T(8,128)(2,1)S(1)}, u32[]{:S(2)}, u32[]{:S(2)}) %collective-permute-start.43) | collective-permute-done | bytes 294944 | tf_op jit(solution)/shard_map/ppermute | solution.py:30
  198.3 3.0 %fusion.3 = f32[1536,192]{0,1:T(8,128)} fusion(s32[1536]{0:T(1024)S(1)} %add.514, f32[1536,192]{0,1:T(8,128)S(1)} %copy-done.8, bf16[192,768]{1,0:T(8,128)(2,1)S(1)} %collective-permute-done.52, bf16[192,384]{1,0:T(8,128)(2,1)S(1)} %get-tuple-element.74, bf16[192,384]{1,0:T(8,128)(2,1)S(1)} %get-tuple-element.68), kind=kOutput, calls=%fused_computation.4 | convolution fusion | flops 910983168 | bytes 2955264 | tf_op jit(solution)/shard_map/dot_general | solution.py:11
  203.1 10.9 %collective-permute-done.53 = bf16[192,1536]{1,0:T(8,128)(2,1)S(1)} collective-permute-done((bf16[192,1536]{1,0:T(8,128)(2,1)S(1)}, bf16[192,1536]{1,0:T(8,128)(2,1)S(1)}, u32[]{:S(2)}, u32[]{:S(2)}) %collective-permute-start.53) | collective-permute-done | bytes 589856 | tf_op jit(solution)/shard_map/ppermute | solution.py:30
  215.4 4.2 %collective-permute-done.50 = bf16[192,768]{1,0:T(8,128)(2,1)S(1)} collective-permute-done((bf16[192,768]{1,0:T(8,128)(2,1)S(1)}, bf16[192,768]{1,0:T(8,128)(2,1)S(1)}, u32[]{:S(2)}, u32[]{:S(2)}) %collective-permute-start.50) | collective-permute-done | bytes 294944 | tf_op jit(solution)/shard_map/ppermute | solution.py:30
  (198 shorter events, 79.6 us)
Async XLA Ops:
  1.1 18.8 %collective-permute-start.10 = (bf16[192,1536]{1,0:T(8,128)(2,1)}, bf16[192,1536]{1,0:T(8,128)(2,1)S(1)}, u32[]{:S(2)}, u32[]{:S(2)}) collective-permute-start(bf16[192,1536]{1,0:T(8,128)(2,1)} %bitcast.152), channel_id=1, source_target_pairs={{0,8},{1,9},{2,10},{3,11},{4,12},{5,13},{6,14},{7,15},{8,16},{9,17... | collective-permute-start | bytes 1769480 | tf_op jit(solution)/shard_map/ppermute | solution.py:30
  8.7 19.9 %collective-permute-start.5 = (bf16[192,1536]{1,0:T(8,128)(2,1)S(1)}, bf16[192,1536]{1,0:T(8,128)(2,1)S(1)}, u32[]{:S(2)}, u32[]{:S(2)}) collective-permute-start(bf16[192,1536]{1,0:T(8,128)(2,1)S(1)} %copy-done), channel_id=1, source_target_pairs={{0,4},{1,5},{2,6},{3,7},{4,0},{5,1},{6,2},{7,3},{8,12},{9,13},{10,... | collective-permute-start | bytes 1769480 | tf_op jit(solution)/shard_map/ppermute | solution.py:30
  9.3 22.2 %collective-permute-start.4 = (bf16[192,1536]{1,0:T(8,128)(2,1)S(1)}, bf16[192,1536]{1,0:T(8,128)(2,1)}, u32[]{:S(2)}, u32[]{:S(2)}) collective-permute-start(bf16[192,1536]{1,0:T(8,128)(2,1)S(1)} %copy-done), channel_id=1, source_target_pairs={{0,2},{1,3},{2,0},{3,1},{4,6},{5,7},{6,4},{7,5},{8,10},{9,11},{10,... | collective-permute-start | bytes 1769480 | tf_op jit(solution)/shard_map/ppermute | solution.py:30
  10.2 18.5 %collective-permute-start.2 = (bf16[384,384]{0,1:T(8,128)(2,1)S(1)}, bf16[384,384]{0,1:T(8,128)(2,1)S(1)}, u32[]{:S(2)}, u32[]{:S(2)}) collective-permute-start(bf16[384,384]{0,1:T(8,128)(2,1)S(1)} %fusion.36), channel_id=1, source_target_pairs={{0,1},{1,0},{2,3},{3,2},{4,5},{5,4},{6,7},{7,6},{8,9},{9,8},{10,11... | collective-permute-start | bytes 884744 | tf_op jit(solution)/shard_map/ppermute | solution.py:30
  20.0 17.0 %collective-permute-start.11 = (bf16[192,1536]{1,0:T(8,128)(2,1)S(1)}, bf16[192,1536]{1,0:T(8,128)(2,1)}, u32[]{:S(2)}, u32[]{:S(2)}) collective-permute-start(bf16[192,1536]{1,0:T(8,128)(2,1)S(1)} %collective-permute-done.10), channel_id=1, source_target_pairs={{0,8},{1,9},{2,10},{3,11},{4,12},{5,13},{6,14},{7,15},{8,16},{9,17... | collective-permute-start | bytes 1769480 | tf_op jit(solution)/shard_map/ppermute | solution.py:30
  28.6 15.9 %collective-permute-start.17 = (bf16[192,1536]{1,0:T(8,128)(2,1)S(1)}, bf16[192,1536]{1,0:T(8,128)(2,1)}, u32[]{:S(2)}, u32[]{:S(2)}) collective-permute-start(bf16[192,1536]{1,0:T(8,128)(2,1)S(1)} %bitcast.154), channel_id=1, source_target_pairs={{0,4},{1,5},{2,6},{3,7},{4,0},{5,1},{6,2},{7,3},{8,12},{9,13},{10,... | collective-permute-start | bytes 1769480 | tf_op jit(solution)/shard_map/ppermute | solution.py:30
  30.2 50.4 %collective-permute-start.19 = (bf16[192,1536]{1,0:T(8,128)(2,1)S(1)}, bf16[192,1536]{1,0:T(8,128)(2,1)}, u32[]{:S(2)}, u32[]{:S(2)}) collective-permute-start(bf16[192,1536]{1,0:T(8,128)(2,1)S(1)} %collective-permute-done.10), channel_id=1, source_target_pairs={{0,2},{1,3},{2,0},{3,1},{4,6},{5,7},{6,4},{7,5},{8,10},{9,11},{10,... | collective-permute-start | bytes 1769480 | tf_op jit(solution)/shard_map/ppermute | solution.py:30
  37.0 25.0 %collective-permute-start.13 = (bf16[192,1536]{1,0:T(8,128)(2,1)}, bf16[192,1536]{1,0:T(8,128)(2,1)S(1)}, u32[]{:S(2)}, u32[]{:S(2)}) collective-permute-start(bf16[192,1536]{1,0:T(8,128)(2,1)} %collective-permute-done.11), channel_id=1, source_target_pairs={{0,8},{1,9},{2,10},{3,11},{4,12},{5,13},{6,14},{7,15},{8,16},{9,17... | collective-permute-start | bytes 1769480 | tf_op jit(solution)/shard_map/ppermute | solution.py:30
  40.0 21.6 %collective-permute-start.12 = (bf16[192,768]{1,0:T(8,128)(2,1)S(1)}, bf16[192,768]{1,0:T(8,128)(2,1)S(1)}, u32[]{:S(2)}, u32[]{:S(2)}) collective-permute-start(bf16[192,768]{1,0:T(8,128)(2,1)S(1)} %convolution_convert_fusion.1), channel_id=1, source_target_pairs={{0,8},{1,9},{2,10},{3,11},{4,12},{5,13},{6,14},{7,15},{8,16},{9,17... | collective-permute-start | bytes 884744 | tf_op jit(solution)/shard_map/ppermute | solution.py:30
  41.6 24.2 %collective-permute-start.7 = (bf16[192,768]{1,0:T(8,128)(2,1)S(1)}, bf16[192,768]{1,0:T(8,128)(2,1)S(1)}, u32[]{:S(2)}, u32[]{:S(2)}) collective-permute-start(bf16[192,768]{1,0:T(8,128)(2,1)S(1)} %convolution_convert_fusion.2), channel_id=1, source_target_pairs={{0,8},{1,9},{2,10},{3,11},{4,12},{5,13},{6,14},{7,15},{8,16},{9,17... | collective-permute-start | bytes 884744 | tf_op jit(solution)/shard_map/ppermute | solution.py:30
  44.5 29.6 %collective-permute-start.20 = (bf16[192,1536]{1,0:T(8,128)(2,1)S(1)}, bf16[192,1536]{1,0:T(8,128)(2,1)S(1)}, u32[]{:S(2)}, u32[]{:S(2)}) collective-permute-start(bf16[192,1536]{1,0:T(8,128)(2,1)S(1)} %collective-permute-done.10), channel_id=1, source_target_pairs={{0,4},{1,5},{2,6},{3,7},{4,0},{5,1},{6,2},{7,3},{8,12},{9,13},{10,... | collective-permute-start | bytes 1769480 | tf_op jit(solution)/shard_map/ppermute | solution.py:30
  61.5 18.4 %collective-permute-start.18 = (bf16[192,1536]{1,0:T(8,128)(2,1)}, bf16[192,1536]{1,0:T(8,128)(2,1)S(1)}, u32[]{:S(2)}, u32[]{:S(2)}) collective-permute-start(bf16[192,1536]{1,0:T(8,128)(2,1)} %collective-permute-done.17), channel_id=1, source_target_pairs={{0,2},{1,3},{2,0},{3,1},{4,6},{5,7},{6,4},{7,5},{8,10},{9,11},{10,... | collective-permute-start | bytes 1769480 | tf_op jit(solution)/shard_map/ppermute | solution.py:30
  74.1 16.4 %collective-permute-start.23 = (bf16[192,1536]{1,0:T(8,128)(2,1)}, bf16[192,1536]{1,0:T(8,128)(2,1)S(1)}, u32[]{:S(2)}, u32[]{:S(2)}) collective-permute-start(bf16[192,1536]{1,0:T(8,128)(2,1)} %collective-permute-done.11), channel_id=1, source_target_pairs={{0,4},{1,5},{2,6},{3,7},{4,0},{5,1},{6,2},{7,3},{8,12},{9,13},{10,... | collective-permute-start | bytes 1769480 | tf_op jit(solution)/shard_map/ppermute | solution.py:30
  80.0 22.8 %collective-permute-start.25 = (bf16[192,1536]{1,0:T(8,128)(2,1)S(1)}, bf16[192,1536]{1,0:T(8,128)(2,1)S(1)}, u32[]{:S(2)}, u32[]{:S(2)}) collective-permute-start(bf16[192,1536]{1,0:T(8,128)(2,1)S(1)} %collective-permute-done.13), channel_id=1, source_target_pairs={{0,2},{1,3},{2,0},{3,1},{4,6},{5,7},{6,4},{7,5},{8,10},{9,11},{10,... | collective-permute-start | bytes 1769480 | tf_op jit(solution)/shard_map/ppermute | solution.py:30
  80.7 22.0 %collective-permute-start.26 = (bf16[192,1536]{1,0:T(8,128)(2,1)S(1)}, bf16[192,1536]{1,0:T(8,128)(2,1)S(1)}, u32[]{:S(2)}, u32[]{:S(2)}) collective-permute-start(bf16[192,1536]{1,0:T(8,128)(2,1)S(1)} %collective-permute-done.13), channel_id=1, source_target_pairs={{0,4},{1,5},{2,6},{3,7},{4,0},{5,1},{6,2},{7,3},{8,12},{9,13},{10,... | collective-permute-start | bytes 1769480 | tf_op jit(solution)/shard_map/ppermute | solution.py:30
  84.5 15.6 %collective-permute-start.9 = (bf16[192,768]{1,0:T(8,128)(2,1)S(1)}, bf16[192,768]{1,0:T(8,128)(2,1)S(1)}, u32[]{:S(2)}, u32[]{:S(2)}) collective-permute-start(bf16[192,768]{1,0:T(8,128)(2,1)S(1)} %fusion.30), channel_id=1, source_target_pairs={{0,8},{1,9},{2,10},{3,11},{4,12},{5,13},{6,14},{7,15},{8,16},{9,17... | collective-permute-start | bytes 884744 | tf_op jit(solution)/shard_map/ppermute | solution.py:30
  100.6 16.1 %collective-permute-start.39 = (bf16[192,1536]{1,0:T(8,128)(2,1)S(1)}, bf16[192,1536]{1,0:T(8,128)(2,1)S(1)}, u32[]{:S(2)}, u32[]{:S(2)}) collective-permute-start(bf16[192,1536]{1,0:T(8,128)(2,1)S(1)} %copy-done), channel_id=1, source_target_pairs={{0,8},{1,9},{2,10},{3,11},{4,12},{5,13},{6,14},{7,15},{8,16},{9,17... | collective-permute-start | bytes 1769480 | tf_op jit(solution)/shard_map/ppermute | solution.py:30
  126.6 16.6 %collective-permute-start.30 = (bf16[192,768]{1,0:T(8,128)(2,1)S(1)}, bf16[192,768]{1,0:T(8,128)(2,1)S(1)}, u32[]{:S(2)}, u32[]{:S(2)}) collective-permute-start(bf16[192,768]{1,0:T(8,128)(2,1)S(1)} %get-tuple-element.45), channel_id=1, source_target_pairs={{0,1},{1,0},{2,3},{3,2},{4,5},{5,4},{6,7},{7,6},{8,9},{9,8},{10,11... | collective-permute-start | bytes 884744 | tf_op jit(solution)/shard_map/ppermute | solution.py:30
  133.0 15.8 %collective-permute-start.46 = (bf16[192,768]{1,0:T(8,128)(2,1)S(1)}, bf16[192,768]{1,0:T(8,128)(2,1)S(1)}, u32[]{:S(2)}, u32[]{:S(2)}) collective-permute-start(bf16[192,768]{1,0:T(8,128)(2,1)S(1)} %constant_dynamic-slice_fusion.1), channel_id=1, source_target_pairs={{0,1},{1,0},{2,3},{3,2},{4,5},{5,4},{6,7},{7,6},{8,9},{9,8},{10,11... | collective-permute-start | bytes 884744 | tf_op jit(solution)/shard_map/ppermute | solution.py:30
  133.6 30.9 %collective-permute-start.41 = (bf16[192,1536]{1,0:T(8,128)(2,1)S(1)}, bf16[192,1536]{1,0:T(8,128)(2,1)S(1)}, u32[]{:S(2)}, u32[]{:S(2)}) collective-permute-start(bf16[192,1536]{1,0:T(8,128)(2,1)S(1)} %collective-permute-done.40), channel_id=1, source_target_pairs={{0,8},{1,9},{2,10},{3,11},{4,12},{5,13},{6,14},{7,15},{8,16},{9,17... | collective-permute-start | bytes 1769480 | tf_op jit(solution)/shard_map/ppermute | solution.py:30
  145.9 18.1 %collective-permute-start.32 = (bf16[192,768]{1,0:T(8,128)(2,1)S(1)}, bf16[192,768]{1,0:T(8,128)(2,1)S(1)}, u32[]{:S(2)}, u32[]{:S(2)}) collective-permute-start(bf16[192,768]{1,0:T(8,128)(2,1)S(1)} %get-tuple-element.72), channel_id=1, source_target_pairs={{0,8},{1,9},{2,10},{3,11},{4,12},{5,13},{6,14},{7,15},{8,16},{9,17... | collective-permute-start | bytes 884744 | tf_op jit(solution)/shard_map/ppermute | solution.py:30
  157.6 25.8 %collective-permute-start.38 = (bf16[192,768]{1,0:T(8,128)(2,1)S(1)}, bf16[192,768]{1,0:T(8,128)(2,1)S(1)}, u32[]{:S(2)}, u32[]{:S(2)}) collective-permute-start(bf16[192,768]{1,0:T(8,128)(2,1)S(1)} %collective-permute-done.37), channel_id=1, source_target_pairs={{0,8},{1,9},{2,10},{3,11},{4,12},{5,13},{6,14},{7,15},{8,16},{9,17... | collective-permute-start | bytes 884744 | tf_op jit(solution)/shard_map/ppermute | solution.py:30
  196.8 17.2 %collective-permute-start.53 = (bf16[192,1536]{1,0:T(8,128)(2,1)S(1)}, bf16[192,1536]{1,0:T(8,128)(2,1)S(1)}, u32[]{:S(2)}, u32[]{:S(2)}) collective-permute-start(bf16[192,1536]{1,0:T(8,128)(2,1)S(1)} %fusion.41), channel_id=1, source_target_pairs={{0,4},{1,5},{2,6},{3,7},{4,0},{5,1},{6,2},{7,3},{8,12},{9,13},{10,... | collective-permute-start | bytes 1769480 | tf_op jit(solution)/shard_map/ppermute | solution.py:30
  201.6 18.0 %collective-permute-start.50 = (bf16[192,768]{1,0:T(8,128)(2,1)S(1)}, bf16[192,768]{1,0:T(8,128)(2,1)S(1)}, u32[]{:S(2)}, u32[]{:S(2)}) collective-permute-start(bf16[192,768]{1,0:T(8,128)(2,1)S(1)} %fusion.72), channel_id=1, source_target_pairs={{0,4},{1,5},{2,6},{3,7},{4,0},{5,1},{6,2},{7,3},{8,12},{9,13},{10,... | collective-permute-start | bytes 884744 | tf_op jit(solution)/shard_map/ppermute | solution.py:30
  (39 other events, 375.7 us)
